TPU v7x, 256 devices: a whole 4x4x8 slice. The times are simulated.
256 devices in a mesh: dp: 128 (over x, y, z), sub: 2 (over core).
Axes of the slice: x: 4, y: 4, z: 8, core: 2. Of those that a mesh axis runs over, the one named last changes fastest.
Arguments:
- frames: bfloat16 [262144, 440], P(('dp', 'sub')), may hold values from -6 to 6
- freqs: bfloat16 [440, 1024], P(None, ('dp', 'sub')), may hold values from -0.38138504 to 0.38138504
- phase: float32 [1024], replicated, may hold values from -3.140625 to 3.140625
- labels: int32 [262144], P(('dp', 'sub')), may hold values from 0 to 146
- predictions: float32 [262144, 147], P(('dp', 'sub')), may hold values from -4 to 4
- coeffs_old: float32 [1024, 147], P(('dp', 'sub')), may hold values from -0.4 to 0.4
Outputs:
- new_predictions: float32 [262144, 147], P(('dp', 'sub'))
- coeffs_new: float32 [1024, 147], replicated
All inputs are finite; a program needn't handle non-finite values.
Results may differ from a plain program's by a relative error of at most 0.0015.
The roundings to bfloat16 on the way count: a program that leaves them out, or rounds other values in their place, can miss the bound.
Values may be sent and summed in bfloat16 or wider, within the bound.
No kernel may reach another device: no remote copies, remote signals or barrier semaphores. Data moves between devices by JAX's collectives and lax.ppermute only.
A program may use at most 64 MiB of HBM per device.

v0:
```python
import jax
import jax.numpy as jnp
from jax import lax
from jax.sharding import PartitionSpec as P

root_two = 1.4142135623730951
ridge = 1.0


def local(frames, freqs, phase, labels, predictions, coeffs_old):
    classes = predictions.shape[1]
    devices_all = lax.axis_size("dp") * lax.axis_size("sub")
    total_rows = frames.shape[0] * devices_all
    old_full = lax.all_gather(coeffs_old, ("dp", "sub"), axis=0, tiled=True)
    angles = (
        jnp.dot(
            frames,
            lax.all_gather(freqs, ("dp", "sub"), axis=1, tiled=True),
            preferred_element_type=jnp.float32,
        )
        + phase[None, :]
    )
    features = (root_two * jnp.cos(angles)).astype(jnp.bfloat16)
    onehot = (labels[:, None] == jnp.arange(classes, dtype=jnp.int32)[None, :]).astype(jnp.float32)
    residual = (onehot - predictions).astype(jnp.bfloat16)
    block_width = features.shape[1]
    contract = (((0,), (0,)), ((), ()))
    gram_part = lax.dot_general(features, features, contract, preferred_element_type=jnp.float32)
    cross_part = lax.dot_general(features, residual, contract, preferred_element_type=jnp.float32)
    gram, cross = lax.psum((gram_part, cross_part), ("dp", "sub"))
    system = gram / total_rows + ridge * jnp.eye(block_width, dtype=jnp.float32)
    right_side = (
        cross
        + jnp.dot(
            gram, old_full, precision=lax.Precision.HIGHEST, preferred_element_type=jnp.float32
        )
    ) / total_rows
    factor = jnp.linalg.cholesky(system)
    halfway = lax.linalg.triangular_solve(factor, right_side, left_side=True, lower=True)
    coeffs_new = lax.linalg.triangular_solve(
        factor, halfway, left_side=True, lower=True, transpose_a=True
    )
    change = (coeffs_new - old_full).astype(jnp.bfloat16)
    new_predictions = predictions + jnp.dot(features, change, preferred_element_type=jnp.float32)
    return (new_predictions, coeffs_new)


def solution(mesh):
    placed = (
        P(("dp", "sub"), None),
        P(None, ("dp", "sub")),
        P(),
        P(("dp", "sub")),
        P(("dp", "sub"), None),
        P(("dp", "sub"), None),
    )
    return jax.shard_map(
        local, mesh=mesh, in_specs=placed, out_specs=(P(("dp", "sub"), None), P()), check_vma=False
    )
```

profile of v0, /device:TPU:1, one launch (start us, length us, event | category | flops | bytes accessed | tf_op | source)
XLA Modules:
  0.0 731.8 jit_solution(4493545048139382601)
XLA Ops:
  7.2 67.8 %all-gather = bf16[256,4,440]{2,1,0:T(4,128)(2,1)S(1)} all-gather(bf16[1,4,440]{2,1,0:T(4,128)(2,1)} %bitcast.139), channel_id=1, replica_groups=mesh['dp'=128,'sub'=2] {'dp','sub'}, dimensions={0}, use_global_device_ids=true | all-gather | bytes 904640 | tf_op jit(solution)/shard_map/all_gather | solution.py:18
  76.4 15.8 %multiply_convert_fusion = bf16[1024,1024]{1,0:T(8,128)(2,1)S(1)} fusion(bf16[1024,440]{0,1:T(8,128)(2,1)S(1)} %copy-done, bf16[1024,440]{1,0:T(8,128)(2,1)} %reshape.113, f32[1024]{0:T(1024)} %param.8), kind=kOutput, calls=%fused_computation.8 | convolution fusion | flops 925892608 | bytes 3903488 | tf_op jit(solution)/shard_map/dot_general | solution.py:16
  98.0 65.1 %all-gather.1 = f32[256,4,147]{2,1,0:T(4,128)} all-gather(f32[1,4,147]{2,1,0:T(4,128)S(1)} %bitcast.140), channel_id=1, replica_groups=mesh['dp'=128,'sub'=2] {'dp','sub'}, dimensions={0}, use_global_device_ids=true | all-gather | bytes 604464 | tf_op jit(solution)/shard_map/all_gather | solution.py:14
  168.2 197.2 %all-reduce.4.cloned.1.call-done = (f32[1024,147]{0,1:T(8,128)}, f32[1024,1024]{0,1:T(8,128)}) async-done(((f32[1024,147]{0,1:T(8,128)}, f32[1024,1024]{0,1:T(8,128)}), (f32[1024,147]{0,1:T(8,128)}, f32[1024,1024]{0,1:T(8,128)})) %all-reduce.4.cloned.1.call-update) | async-done | bytes 4796432 | tf_op jit(solution)/shard_map/psum | solution.py:30
  365.4 5.2 convert_add_fusion
  374.3 5.5 copy.15
  386.2 11.7 %cholesky.223 = f32[128,128]{1,0:T(8,128)S(1)} custom-call(f32[128,128]{1,0:T(8,128)S(1)} %cholesky.580), custom_call_target="Cholesky" | custom-call | tf_op jit(solution)/shard_map/jit(cholesky)/cholesky | solution.py:38
  400.5 9.8 %custom-call.64 = f32[1,128,128]{1,2,0:T(8,128)S(1)} custom-call(f32[1,128,128]{2,1,0:T(8,128)S(1)} %get-tuple-element.60), custom_call_target="InvertDiagBlocksLowerTriangular" | custom-call | tf_op jit(solution)/shard_map/jit(cholesky)/cholesky | solution.py:38
  414.9 12.9 %cholesky.244 = f32[128,128]{1,0:T(8,128)S(1)} custom-call(f32[128,128]{1,0:T(8,128)} %cholesky.584), custom_call_target="Cholesky" | custom-call | tf_op jit(solution)/shard_map/jit(cholesky)/cholesky | solution.py:38
  428.5 10.6 %custom-call.65 = f32[1,128,128]{1,2,0:T(8,128)S(1)} custom-call(f32[1,128,128]{2,1,0:T(8,128)} %get-tuple-element.57), custom_call_target="InvertDiagBlocksLowerTriangular" | custom-call | tf_op jit(solution)/shard_map/jit(cholesky)/cholesky | solution.py:38
  442.5 11.7 %cholesky.468 = f32[128,128]{1,0:T(8,128)S(1)} custom-call(f32[128,128]{1,0:T(8,128)S(1)} %cholesky.589), custom_call_target="Cholesky" | custom-call | tf_op jit(solution)/shard_map/jit(cholesky)/cholesky | solution.py:38
  454.8 9.8 %custom-call.66 = f32[1,128,128]{1,2,0:T(8,128)S(1)} custom-call(f32[1,128,128]{2,1,0:T(8,128)S(1)} %get-tuple-element.54), custom_call_target="InvertDiagBlocksLowerTriangular" | custom-call | tf_op jit(solution)/shard_map/jit(cholesky)/cholesky | solution.py:38
  468.2 11.9 %cholesky.487 = f32[128,128]{1,0:T(8,128)S(1)} custom-call(f32[128,128]{1,0:T(8,128)S(1)} %cholesky.594), custom_call_target="Cholesky" | custom-call | tf_op jit(solution)/shard_map/jit(cholesky)/cholesky | solution.py:38
  480.7 9.8 %custom-call.67 = f32[1,128,128]{1,2,0:T(8,128)S(1)} custom-call(f32[1,128,128]{2,1,0:T(8,128)S(1)} %get-tuple-element.51), custom_call_target="InvertDiagBlocksLowerTriangular" | custom-call | tf_op jit(solution)/shard_map/jit(cholesky)/cholesky | solution.py:38
  493.9 11.7 %cholesky.506 = f32[128,128]{1,0:T(8,128)S(1)} custom-call(f32[128,128]{1,0:T(8,128)S(1)} %cholesky.599), custom_call_target="Cholesky" | custom-call | tf_op jit(solution)/shard_map/jit(cholesky)/cholesky | solution.py:38
  506.3 10.0 %custom-call.68 = f32[1,128,128]{1,2,0:T(8,128)S(1)} custom-call(f32[1,128,128]{2,1,0:T(8,128)S(1)} %get-tuple-element.48), custom_call_target="InvertDiagBlocksLowerTriangular" | custom-call | tf_op jit(solution)/shard_map/jit(cholesky)/cholesky | solution.py:38
  519.6 11.7 %cholesky.526 = f32[128,128]{1,0:T(8,128)S(1)} custom-call(f32[128,128]{1,0:T(8,128)S(1)} %cholesky.604), custom_call_target="Cholesky" | custom-call | tf_op jit(solution)/shard_map/jit(cholesky)/cholesky | solution.py:38
  531.9 9.8 %custom-call.69 = f32[1,128,128]{1,2,0:T(8,128)S(1)} custom-call(f32[1,128,128]{2,1,0:T(8,128)S(1)} %get-tuple-element.45), custom_call_target="InvertDiagBlocksLowerTriangular" | custom-call | tf_op jit(solution)/shard_map/jit(cholesky)/cholesky | solution.py:38
  544.7 12.1 %cholesky.546 = f32[128,128]{1,0:T(8,128)S(1)} custom-call(f32[128,128]{1,0:T(8,128)S(1)} %cholesky.609), custom_call_target="Cholesky" | custom-call | tf_op jit(solution)/shard_map/jit(cholesky)/cholesky | solution.py:38
  557.5 9.8 %custom-call.70 = f32[1,128,128]{1,2,0:T(8,128)S(1)} custom-call(f32[1,128,128]{2,1,0:T(8,128)S(1)} %get-tuple-element.42), custom_call_target="InvertDiagBlocksLowerTriangular" | custom-call | tf_op jit(solution)/shard_map/jit(cholesky)/cholesky | solution.py:38
  569.9 11.7 %cholesky.564 = f32[128,128]{1,0:T(8,128)S(1)} custom-call(f32[128,128]{1,0:T(8,128)S(1)} %convolution_subtract_fusion.20), custom_call_target="Cholesky" | custom-call | tf_op jit(solution)/shard_map/jit(cholesky)/cholesky | solution.py:38
  592.0 4.8 select_select_fusion
  596.8 27.6 %while.1 = (s32[]{:T(128)}, f32[1024,1024]{1,0:T(8,128)}, s32[8,2]{0,1:T(2,128)S(1)}, f32[8,128,128]{2,1,0:T(8,128)}, s32[]{:T(128)}) while((s32[]{:T(128)}, f32[1024,1024]{1,0:T(8,128)}, s32[8,2]{0,1:T(2,128)S(1)}, f32[8,128,128]{2,1,0:T(8,128)}, s32[]{:T(128)}) %tuple.60), condition=%wide.while_cond, body=%wide.while_body.sunk | while | flops 2 | bytes 132205 | solution.py:40
  624.4 79.6 %custom-call.71 = f32[8,128,128]{1,2,0:T(8,128)S(1)} custom-call(f32[8,128,128]{2,1,0:T(8,128)} %get-tuple-element.9), custom_call_target="InvertDiagBlocksLowerTriangular" | custom-call | tf_op jit(solution)/shard_map/triangular_solve | solution.py:40
  (150 shorter events, 105.7 us)
Async XLA Ops:
  7.2 69.3 %copy-start = (bf16[1024,440]{0,1:T(8,128)(2,1)S(1)}, bf16[1024,440]{0,1:T(8,128)(2,1)}, u32[]{:S(2)}) copy-start(bf16[1024,440]{0,1:T(8,128)(2,1)} %param.6) | copy-start | bytes 2703364
  7.2 358.2 %all-reduce.4.cloned.1.call-start = ((), (), s32[]{:S(2)}) async-start(), calls=%async_computation | async-start | bytes 9633792 | tf_op jit(solution)/shard_map/psum | solution.py:30
  92.3 4.4 copy-start.6
  92.3 4.4 copy-start.11
  96.7 1.4 copy-start.10
  365.4 5.2 copy-start.1
  365.4 5.2 copy-start.4
  365.4 5.2 copy-start.9
  384.3 1.9 copy-start.3
  704.0 7.8 %copy-start.2 = (f32[1024,1024]{1,0:T(8,128)S(1)}, f32[1024,1024]{1,0:T(8,128)}, u32[]{:S(2)}) copy-start(f32[1024,1024]{1,0:T(8,128)} %get-tuple-element.129) | copy-start | bytes 12582916
  719.3 3.8 copy-start.5
  719.3 3.8 copy-start.7
  723.1 1.7 copy-start.8
Sparse Core Ops, SparseCore 0:
  98.1 267.1 all-reduce.3
where the time goes:
time: 741 us; the launch traced here: 732 us
  other arithmetic  268 us (36%)
  waiting for transfers between devices  197 us (27%)
  blocking collectives  133 us (18%)
  matrix products  68.4 us (9%)
  local copies, waits for them, and re-layouts  44.9 us (6%)
  between operations  19.9 us (3%)
    psum x1, waiting for transfers between devices, local(): gram, cross = lax.psum((gram_part, cross_part), ('dp', 'sub'))  197 us
    another operation x30, other arithmetic, local(): factor = jnp.linalg.cholesky(system)  174 us
    another operation x3, other arithmetic, local(): lax.linalg.triangular_solve(factor, halfway, left_side=True, lower=True,...  84.4 us
    all_gather x1, blocking collectives, local(): lax.all_gather(freqs, ('dp', 'sub'), axis=1, tiled=True)  67.8 us
    all_gather x1, blocking collectives, local(): old_full = lax.all_gather(coeffs_old, ('dp', 'sub'), axis=0, tiled=True)  65.1 us
    another operation x24, local copies, waits for them, and re-layouts  27.6 us
    another operation x14, matrix products, local(): factor = jnp.linalg.cholesky(system)  23.1 us
    dot_general x1, matrix products, local(): jnp.dot(frames, lax.all_gather(freqs, ('dp', 'sub'), axis=1, tiled=True),...  15.8 us
  transfers between devices with their start and end apart: 1, of which 1 were waited for; matrix products, arithmetic and copies ran while one was open for 1% of the time, Pallas kernels for 0%

commit v1 on v0

v1 whole, which is shorter than its diff:
```python
import functools

import jax
import jax.numpy as jnp
import numpy as np
from jax import lax
from jax.experimental import pallas as pl
from jax.experimental.pallas import tpu as pltpu
from jax.sharding import Mesh, PartitionSpec as P

f32 = jnp.float32
bf16 = jnp.bfloat16
root_two = 1.4142135623730951
ridge = 1.0
tile = 128
step = 256
NN = (((1,), (0,)), ((), ()))
NT = (((1,), (1,)), ((), ()))


def cosine_coefficients(degree):
    nodes = 0.125 * np.cos(np.pi * (np.arange(400) + 0.5) / 400) + 0.125
    wanted = root_two * np.cos(2 * np.pi * np.sqrt(nodes))
    fitted = np.polynomial.chebyshev.Chebyshev.fit(nodes, wanted, degree, domain=[0, 0.25])
    return [float(c) for c in fitted.convert(kind=np.polynomial.Polynomial).coef]


cosine = cosine_coefficients(6)


def features_of(angles):
    turns = angles * (0.5 / np.pi)
    part = turns - jnp.round(turns)
    square = part * part
    value = cosine[-1] * square + cosine[-2]
    for coefficient in cosine[-3::-1]:
        value = value * square + coefficient
    return value.astype(bf16)


def dot(a, b, dims=NN):
    return lax.dot_general(a, b, dims, preferred_element_type=f32)


def split(x):
    high = x.astype(bf16)
    return high, (x - high.astype(f32)).astype(bf16)


def product(a, b):
    return dot(a[0], b[0]) + (dot(a[0], b[1]) + dot(a[1], b[0]))


def pairs(blocks):
    return [(a, b) for a in range(blocks) for b in range(a + 1)]


def layout(width, classes):
    blocks = width // tile
    lower = len(pairs(blocks)) * tile
    each = (-(-(lower + blocks * classes) // 2048) * 2048 - lower) // blocks
    return blocks, lower, each, lower + blocks * each


def moment_kernel(frames, freqs, phase, labels, predictions, turned, packed, padded):
    width, (rows, classes) = freqs.shape[0], predictions.shape
    blocks, lower, each, _ = layout(width, classes)
    padded[...] = jnp.zeros_like(padded)
    padded[:, :classes] = predictions[...]
    onehot = labels[...] == lax.broadcasted_iota(jnp.int32, (padded.shape[1], rows), 0)
    residual = (onehot.astype(f32) - padded[...].T)[:each].astype(bf16)
    row = 0
    for i in range(width // step):
        mine = slice(i * step, (i + 1) * step)
        angles = dot(freqs[mine, : frames.shape[1]], frames[...], NT) + phase[mine, :]
        block = features_of(angles)
        turned[mine, :] = block
        gram = dot(block, turned[: (i + 1) * step, :], NT)
        cross = dot(residual, block, NT)
        for j in range(step // tile):
            a = i * (step // tile) + j
            for b in range(a + 1):
                packed[row : row + tile, :] = gram[j * tile : (j + 1) * tile, b * tile : (b + 1) * tile]
                row += tile
            packed[lower + a * each : lower + (a + 1) * each, :] = cross[:, j * tile : (j + 1) * tile]


def moments(frames, freqs, phase, labels, predictions):
    width, (rows, classes) = freqs.shape[0], predictions.shape
    _, _, _, total = layout(width, classes)
    here = pl.BlockSpec(memory_space=pltpu.VMEM)
    return pl.pallas_call(
        moment_kernel,
        out_shape=(
            jax.ShapeDtypeStruct((width, rows), bf16),
            jax.ShapeDtypeStruct((total, tile), f32),
        ),
        in_specs=[here] * 5,
        out_specs=(here, here),
        scratch_shapes=[pltpu.VMEM((rows, 2 * tile), f32)],
        compiler_params=pltpu.CompilerParams(vmem_limit_bytes=48 * 1024 * 1024),
        name="moments",
    )(frames, freqs, phase, labels, predictions)


def inverse(a, eye):
    bound = 2.0 * a.shape[0]
    scale = 2.0 / (2.0 * ridge + bound)
    spread = bound / (2.0 * ridge + bound)
    rest = eye - scale * a
    for k in range(7):
        gain = 2.0 / (2.0 - spread * spread)
        parts = split(rest)
        x = (gain * scale) * (eye + rest) if k == 0 else gain * (x + product(split(x), parts))
        spread = spread * spread / (2.0 - spread * spread)
        if k < 6:
            rest = gain * product(parts, parts) - spread * eye
    missing = eye - product(split(a), split(x))
    return x + product(split(x), split(missing))


def solve_kernel(
    total_rows, packed, old, turned, predictions, coeffs, updated,
    system, work, inv_h, inv_l, low_h, low_l, up_h, up_l, right, found,
):
    width = system.shape[0]
    classes = coeffs.shape[1]
    blocks, lower, each, _ = layout(width, classes)
    count = width // step
    scale = 1.0 / total_rows
    padded = right.shape[0]
    eye = (
        lax.broadcasted_iota(jnp.int32, (step, step), 0)
        == lax.broadcasted_iota(jnp.int32, (step, step), 1)
    ).astype(f32)
    for t, (a, b) in enumerate(pairs(blocks)):
        part = packed[t * tile : (t + 1) * tile, :] * scale
        if a == b:
            part = part + ridge * eye[:tile, :tile]
        system[a * tile : (a + 1) * tile, b * tile : (b + 1) * tile] = part
        if a != b:
            system[b * tile : (b + 1) * tile, a * tile : (a + 1) * tile] = part.T
    for m in range(blocks):
        lanes = slice(m * tile, (m + 1) * tile)
        start = lower + m * each
        right[:, lanes] = packed[start : start + padded, :] * scale - old[:, lanes]

    def at(k):
        return slice(k * step, (k + 1) * step)

    for k in range(count):
        source = system if k == 0 else work
        x = split(inverse(source[at(k), at(k)], eye))
        inv_h[at(k), :], inv_l[at(k), :] = x
        if k == count - 1:
            break
        after = slice((k + 1) * step, width)
        column = split(product(split(source[after, at(k)]), x))
        low_h[after, at(k)], low_l[after, at(k)] = column
        row = split(source[at(k), after])
        up_h[at(k), after], up_l[at(k), after] = row
        work[after, after] = source[after, after] - product(column, row)

    def apply(parts):
        parts = list(parts)
        for k in range(count):
            now = parts[k] = product(split(parts[k]), (inv_h[at(k), :], inv_l[at(k), :]))
            if k < count - 1:
                after = slice((k + 1) * step, width)
                less = product(split(now), (up_h[at(k), after], up_l[at(k), after]))
                for i in range(k + 1, count):
                    parts[i] = parts[i] - less[:, (i - k - 1) * step : (i - k) * step]
        for k in reversed(range(1, count)):
            before = slice(0, k * step)
            less = product(split(parts[k]), (low_h[at(k), before], low_l[at(k), before]))
            for i in range(k):
                parts[i] = parts[i] - less[:, i * step : (i + 1) * step]
        return parts

    for k, part in enumerate(apply([right[:, at(k)] for k in range(count)])):
        found[:, at(k)] = part
    for _ in range(2):
        short = right[...] - lax.dot_general(
            found[...], system[...], NN, precision=lax.Precision.HIGHEST, preferred_element_type=f32
        )
        for k, part in enumerate(apply([short[:, at(k)] for k in range(count)])):
            found[:, at(k)] += part
    change = found[...]
    empty = jnp.zeros((2 * tile - padded, width), f32)
    coeffs[...] = jnp.concatenate([old[...] + change, empty], axis=0).T[:, :classes]
    added = dot(change.astype(bf16), turned[...])
    empty = jnp.zeros((2 * tile - padded, turned.shape[1]), f32)
    updated[...] = predictions[...] + jnp.concatenate([added, empty], axis=0).T[:, :classes]


def solve(packed, old, turned, predictions, total_rows):
    width, (rows, classes) = turned.shape[0], predictions.shape
    here = pl.BlockSpec(memory_space=pltpu.VMEM)
    padded = old.shape[0]
    return pl.pallas_call(
        functools.partial(solve_kernel, float(total_rows)),
        out_shape=(
            jax.ShapeDtypeStruct((width, classes), f32),
            jax.ShapeDtypeStruct((rows, classes), f32),
        ),
        in_specs=[here] * 4,
        out_specs=(here, here),
        scratch_shapes=[
            pltpu.VMEM((width, width), f32),
            pltpu.VMEM((width, width), f32),
            pltpu.VMEM((width, step), bf16),
            pltpu.VMEM((width, step), bf16),
            pltpu.VMEM((width, width), bf16),
            pltpu.VMEM((width, width), bf16),
            pltpu.VMEM((width, width), bf16),
            pltpu.VMEM((width, width), bf16),
            pltpu.VMEM((padded, width), f32),
            pltpu.VMEM((padded, width), f32),
        ],
        compiler_params=pltpu.CompilerParams(vmem_limit_bytes=56 * 1024 * 1024),
        name="solve",
    )(packed, old, turned, predictions)


def exchange(x, axis):
    return lax.all_to_all(x, axis, 0, 0, tiled=True)


def spread_out(x, axes):
    for axis in reversed(axes):
        x = exchange(jnp.broadcast_to(x[None], (lax.axis_size(axis), *x.shape)), axis)
    return x


def add_up(x):
    rows, lanes = x.shape
    for axis in ("core", "x", "y", "z"):
        n = lax.axis_size(axis)
        x = exchange(x.reshape(n, -1, lanes), axis).sum(0)
    return spread_out(x, ("core", "x", "y", "z")).reshape(rows, lanes)


def local(frames, freqs, phase, labels, predictions, coeffs_old):
    rows, classes = predictions.shape
    depth, own = freqs.shape
    width = phase.shape[0]
    devices = width // own
    first = lax.reduce_precision(coeffs_old, 8, 7)
    second = lax.reduce_precision(coeffs_old - first, 8, 7)
    third = coeffs_old - first - second
    first, second, third = (part.astype(bf16) for part in (first, second, third))
    filled = depth + 3 * classes
    sent = jnp.concatenate(
        [freqs.T, first, second, third, jnp.zeros((own, -filled % tile), bf16)], axis=1
    )
    everything = spread_out(sent, ("core", "x", "y", "z"))
    everything = jnp.moveaxis(everything, 0, 3).reshape(width, sent.shape[1])
    parts = [everything[:, depth + i * classes : depth + (i + 1) * classes].astype(f32) for i in range(3)]
    old = (parts[0] + parts[1]) + parts[2]
    old = jnp.pad(old.T, ((0, -classes % 32), (0, 0)))
    turned, packed = moments(
        frames, everything, phase[:, None], labels[None, :], predictions
    )
    packed = add_up(packed)
    coeffs_new, new_predictions = solve(packed, old, turned, predictions, rows * devices)
    return new_predictions, coeffs_new


def solution(mesh):
    chips = mesh.devices.reshape(4, 4, 8, 2)
    inner = Mesh(chips, ("x", "y", "z", "core"))
    every = ("x", "y", "z", "core")
    placed = (P(every, None), P(None, every), P(), P(every), P(every, None), P(every, None))
    return jax.shard_map(
        local, mesh=inner, in_specs=placed, out_specs=(P(every, None), P()), check_vma=False
    )
```

time: 741 us -> 214 us (0.29); the launches traced: 732 us -> 213 us
  other arithmetic: 268 us -> 4.68 us
  waiting for transfers between devices: 197 us -> 16 us
  matrix products: 68.4 us -> 0 us
  Pallas kernels: 0 us -> 40.1 us
  local copies, waits for them, and re-layouts: 44.9 us -> 22.7 us
  between operations: 19.9 us -> 0.78 us
  blocking collectives: 133 us -> 121 us
  starting transfers between devices: 0.04 us -> 7.71 us
    another operation x33 -> x0, other arithmetic: 259 us -> none  [the longest x30 174 us: local(): factor = jnp.linalg.cholesky(system)]
    psum x1 -> x0, waiting for transfers between devices: 197 us -> none  [local(): gram, cross = lax.psum((gram_part, cross_part), ('dp', 'sub'))]
    all_gather x2 -> x0, blocking collectives: 133 us -> none  [the longest x1 67.8 us: local(): lax.all_gather(freqs, ('dp', 'sub'), axis=1, tiled=True)]
    all_to_all x0 -> x10, blocking collectives: none -> 121 us  [exchange(): return lax.all_to_all(x, axis, 0, 0, tiled=True)]
    another operation x44 -> x0, matrix products: 41.5 us -> none  [the longest x14 23.1 us: local(): factor = jnp.linalg.cholesky(system)]
    pallas_call x0 -> x2, Pallas kernels: none -> 40.1 us  [the longest x1 33.5 us: solve(): pl.pallas_call(functools.partial(solve_kernel, float(total_rows)), out_sh...]
    another operation x37 -> x0, local copies, waits for them, and re-layouts: 30.8 us -> none
    dot_general x5 -> x0, matrix products: 26.9 us -> none  [the longest x1 15.8 us: local(): jnp.dot(frames, lax.all_gather(freqs, ('dp', 'sub'), axis=1, tiled=True),...]
  transfers between devices with their start and end apart: 1 -> 2, of which waited for: 1 -> 2; matrix products, arithmetic and copies ran while one was open for 1% -> 4% of each run, Pallas kernels for 0% -> 0%
where the time goes in v1:
time: 214 us; the launch traced here: 213 us
  blocking collectives  121 us (57%)
  Pallas kernels  40.1 us (19%)
  local copies, waits for them, and re-layouts  22.7 us (11%)
  waiting for transfers between devices  16 us (7%)
  starting transfers between devices  7.71 us (4%)
  other arithmetic  4.68 us (2%)
    all_to_all x10, blocking collectives, exchange(): return lax.all_to_all(x, axis, 0, 0, tiled=True)  121 us
    pallas_call x1, Pallas kernels, solve(): pl.pallas_call(functools.partial(solve_kernel, float(total_rows)), out_sh...  33.5 us
    all_to_all x2, waiting for transfers between devices, exchange(): return lax.all_to_all(x, axis, 0, 0, tiled=True)  16 us
    unnamed x21, local copies, waits for them, and re-layouts  10.3 us
    all_to_all x2, starting transfers between devices, exchange(): return lax.all_to_all(x, axis, 0, 0, tiled=True)  7.71 us
    pallas_call x1, Pallas kernels, moments(): pl.pallas_call(moment_kernel, out_shape=(jax.ShapeDtypeStruct((width, row...  6.58 us
  transfers between devices with their start and end apart: 2, of which 2 were waited for; matrix products, arithmetic and copies ran while one was open for 4% of the time, Pallas kernels for 0%

profile of v1, /device:TPU:1, one launch (start us, length us, event | category | flops | bytes accessed | tf_op | source)
XLA Modules:
  0.0 212.7 jit_solution(17962261381067320499)
XLA Ops:
  2.1 16.1 %all_to_all.60 = bf16[8,4,896]{2,1,0:T(4,128)(2,1)S(1)} all-to-all(bf16[8,4,896]{2,1,0:T(4,128)(2,1)S(1)} %broadcast_in_dim.23), channel_id=1, replica_groups=mesh['x'=4,'y'=4,'z'=8,'core'=2] {'z'}, dimensions={0} | all-to-all | bytes 114688 | tf_op jit(solution)/shard_map/all_to_all | solution.py:226
  18.3 9.3 %all_to_all.61 = bf16[4,8,4,896]{3,2,1,0:T(4,128)(2,1)S(1)} all-to-all(bf16[4,8,4,896]{3,2,1,0:T(4,128)(2,1)S(1)} %broadcast_in_dim.24), channel_id=1, replica_groups=mesh['x'=4,'y'=4,'z'=8,'core'=2] {'y'}, dimensions={0} | all-to-all | bytes 458752 | tf_op jit(solution)/shard_map/all_to_all | solution.py:226
  28.8 4.1 %all-to-all-start.2 = ((bf16[4,4,8,4,896]{4,3,2,1,0:T(4,128)(2,1)}), bf16[4,4,8,4,896]{4,3,2,1,0:T(4,128)(2,1)S(1)}, u32[]{:S(2)}, u32[]{:S(2)}) async-start(bf16[4,4,8,4,896]{4,3,2,1,0:T(4,128)(2,1)} %broadcast_in_dim.25), calls=%async_computation.2 | async-start | bytes 1835008 | tf_op jit(solution)/shard_map/all_to_all | solution.py:226
  33.2 1.4 copy.37.predictions
  34.6 1.4 copy.35.frames
  35.9 6.7 %all-to-all-done.2 = bf16[4,4,8,4,896]{4,3,2,1,0:T(4,128)(2,1)S(1)} async-done(((bf16[4,4,8,4,896]{4,3,2,1,0:T(4,128)(2,1)}), bf16[4,4,8,4,896]{4,3,2,1,0:T(4,128)(2,1)S(1)}, u32[]{:S(2)}, u32[]{:S(2)}) %all-to-all-start.2) | async-done | bytes 917536 | tf_op jit(solution)/shard_map/all_to_all | solution.py:226
  43.2 9.8 %all_to_all.62 = bf16[2,4,4,8,4,896]{5,4,3,2,1,0:T(4,128)(2,1)S(1)} all-to-all(bf16[2,4,4,8,4,896]{5,4,3,2,1,0:T(4,128)(2,1)S(1)} %broadcast_in_dim.26), channel_id=1, replica_groups=mesh['x'=4,'y'=4,'z'=8,'core'=2] {'core'}, dimensions={0} | all-to-all | bytes 3670016 | tf_op jit(solution)/shard_map/all_to_all | solution.py:226
  53.0 2.2 %copy.34 = bf16[4,4,8,2,4,896]{5,4,3,2,1,0:T(4,128)(2,1)} copy(bf16[4,4,8,2,4,896]{5,4,2,1,0,3:T(4,128)(2,1)S(1)} %bitcast.13) | data formatting | bytes 3670016 | tf_op jit(solution)/shard_map/transpose | solution.py:257
  55.2 2.9 %reshape.30.freqs = bf16[1024,896]{1,0:T(8,128)(2,1)S(1)} reshape(bf16[4,4,8,2,4,896]{5,4,3,2,1,0:T(4,128)(2,1)} %copy.34) | data formatting | bytes 3670016 | tf_op jit(solution)/shard_map/reshape | solution.py:257
  59.4 6.6 %moments.1 = (bf16[1024,1024]{1,0:T(8,128)(2,1)}, f32[6144,128]{1,0:T(8,128)}) custom-call(bf16[1024,440]{1,0:T(8,128)(2,1)S(1)} %copy-done.1, bf16[1024,896]{1,0:T(8,128)(2,1)S(1)} %reshape.30.freqs, f32[1024,1]{1,0:T(8,128)S(1)} %copy.36.phase, s32[1,1024]{1,0:T(1,128)S(1)} %bitcast.11, f32[1024,147]{1,0:T(8,128)S(1)} %copy.37.predictions), custom_call_target="tpu_custom_call" | custom-call | tf_op jit(solution)/shard_map/moments/pallas_call | solution.py:92
  66.0 10.4 %all_to_all.63 = f32[2,3072,128]{2,1,0:T(8,128)} all-to-all(f32[2,3072,128]{2,1,0:T(8,128)} %bitcast.15), channel_id=1, replica_groups=mesh['x'=4,'y'=4,'z'=8,'core'=2] {'core'}, dimensions={0} | all-to-all | bytes 6291456 | tf_op jit(solution)/shard_map/all_to_all | solution.py:226
  76.3 2.3 %reduce_sum.36 = f32[3072,128]{1,0:T(8,128)S(1)} reduce(f32[2,3072,128]{2,1,0:T(8,128)} %all_to_all.63, f32[]{:T(128)} %constant.1.clone.1), dimensions={0}, to_apply=%region_0.1 | reduce | flops 393216 | bytes 4718596 | tf_op jit(solution)/shard_map/reduce_sum | solution.py:239
  78.6 23.7 %all_to_all.64 = f32[4,768,128]{2,1,0:T(8,128)} all-to-all(f32[4,768,128]{2,1,0:T(8,128)S(1)} %bitcast.14), channel_id=1, replica_groups=mesh['x'=4,'y'=4,'z'=8,'core'=2] {'x'}, dimensions={0} | all-to-all | bytes 3145728 | tf_op jit(solution)/shard_map/all_to_all | solution.py:226
  102.3 1.5 reduce_sum.37
  103.8 9.3 %all_to_all.65 = f32[4,192,128]{2,1,0:T(8,128)S(1)} all-to-all(f32[4,192,128]{2,1,0:T(8,128)S(1)} %bitcast.16), channel_id=1, replica_groups=mesh['x'=4,'y'=4,'z'=8,'core'=2] {'y'}, dimensions={0} | all-to-all | bytes 786432 | tf_op jit(solution)/shard_map/all_to_all | solution.py:226
  113.1 10.1 %all_to_all.66 = f32[8,24,128]{2,1,0:T(8,128)S(1)} all-to-all(f32[8,24,128]{2,1,0:T(8,128)S(1)} %bitcast.17), channel_id=1, replica_groups=mesh['x'=4,'y'=4,'z'=8,'core'=2] {'z'}, dimensions={0} | all-to-all | bytes 196608 | tf_op jit(solution)/shard_map/all_to_all | solution.py:226
  123.2 10.0 %all_to_all.67 = f32[8,24,128]{2,1,0:T(8,128)S(1)} all-to-all(f32[8,24,128]{2,1,0:T(8,128)S(1)} %broadcast_in_dim.29), channel_id=1, replica_groups=mesh['x'=4,'y'=4,'z'=8,'core'=2] {'z'}, dimensions={0} | all-to-all | bytes 196608 | tf_op jit(solution)/shard_map/all_to_all | solution.py:226
  133.2 8.6 %all_to_all.68 = f32[4,8,24,128]{3,2,1,0:T(8,128)S(1)} all-to-all(f32[4,8,24,128]{3,2,1,0:T(8,128)S(1)} %broadcast_in_dim.30), channel_id=1, replica_groups=mesh['x'=4,'y'=4,'z'=8,'core'=2] {'y'}, dimensions={0} | all-to-all | bytes 786432 | tf_op jit(solution)/shard_map/all_to_all | solution.py:226
  143.1 3.6 %all-to-all-start.10 = ((f32[4,4,8,24,128]{4,3,2,1,0:T(8,128)}), f32[4,4,8,24,128]{4,3,2,1,0:T(8,128)S(1)}, u32[]{:S(2)}, u32[]{:S(2)}) async-start(f32[4,4,8,24,128]{4,3,2,1,0:T(8,128)} %broadcast_in_dim.31), calls=%async_computation.10 | async-start | bytes 3145728 | tf_op jit(solution)/shard_map/all_to_all | solution.py:226
  146.7 1.8 fusion.1
  152.3 9.3 %all-to-all-done.10 = f32[4,4,8,24,128]{4,3,2,1,0:T(8,128)S(1)} async-done(((f32[4,4,8,24,128]{4,3,2,1,0:T(8,128)}), f32[4,4,8,24,128]{4,3,2,1,0:T(8,128)S(1)}, u32[]{:S(2)}, u32[]{:S(2)}) %all-to-all-start.10) | async-done | bytes 1572896 | tf_op jit(solution)/shard_map/all_to_all | solution.py:226
  162.0 13.6 %all_to_all.69 = f32[2,4,4,8,24,128]{5,4,3,2,1,0:T(8,128)} all-to-all(f32[2,4,4,8,24,128]{5,4,3,2,1,0:T(8,128)S(1)} %broadcast_in_dim.32), channel_id=1, replica_groups=mesh['x'=4,'y'=4,'z'=8,'core'=2] {'core'}, dimensions={0} | all-to-all | bytes 6291456 | tf_op jit(solution)/shard_map/all_to_all | solution.py:226
  175.6 33.5 %solve.1 = (f32[1024,147]{1,0:T(8,128)}, f32[1024,147]{1,0:T(8,128)}) custom-call(f32[6144,128]{1,0:T(8,128)} %bitcast.12, f32[160,1024]{1,0:T(8,128)} %pad.4.old, bf16[1024,1024]{1,0:T(8,128)(2,1)} %get-tuple-element.7.turned, f32[1024,147]{1,0:T(8,128)} %copy-done), custom_call_target="tpu_custom_call" | custom-call | tf_op jit(solution)/shard_map/solve/pallas_call | solution.py:200
  209.1 2.4 %copy.42 = f32[1024,147]{0,1:T(8,128)} copy(f32[1024,147]{1,0:T(8,128)} %get-tuple-element.16) | data formatting | bytes 1204224
  (34 shorter events, 11.4 us)
Async XLA Ops:
  18.2 14.7 %copy-start.6 = (f32[1024]{0:T(1024)S(1)}, f32[1024]{0:T(1024)}, u32[]{:S(2)}) copy-start(f32[1024]{0:T(1024)} %param.8) | copy-start | bytes 12292
  28.8 5.8 %copy-start.5 = (bf16[1024,440]{0,1:T(8,128)(2,1)S(1)}, bf16[1024,440]{0,1:T(8,128)(2,1)}, u32[]{:S(2)}) copy-start(bf16[1024,440]{0,1:T(8,128)(2,1)} %param.6) | copy-start | bytes 2703364
  28.8 13.9 %all-to-all-start.2 = ((bf16[4,4,8,4,896]{4,3,2,1,0:T(4,128)(2,1)}), bf16[4,4,8,4,896]{4,3,2,1,0:T(4,128)(2,1)S(1)}, u32[]{:S(2)}, u32[]{:S(2)}) async-start(bf16[4,4,8,4,896]{4,3,2,1,0:T(4,128)(2,1)} %broadcast_in_dim.25), calls=%async_computation.2 | async-start | bytes 1835008 | tf_op jit(solution)/shard_map/all_to_all | solution.py:226
  34.6 23.6 %copy-start = (f32[1024,147]{1,0:T(8,128)}, f32[1024,147]{1,0:T(8,128)S(1)}, u32[]{:S(2)}) copy-start(f32[1024,147]{1,0:T(8,128)S(1)} %copy.37.predictions) | copy-start | bytes 1806340
  55.2 3.0 %copy-start.2 = (s32[1024]{0:T(1024)S(1)}, s32[1024]{0:T(1024)}, u32[]{:S(2)}) copy-start(s32[1024]{0:T(1024)} %param.9) | copy-start | bytes 12292
  58.2 1.2 copy-start.1
  143.1 18.5 %all-to-all-start.10 = ((f32[4,4,8,24,128]{4,3,2,1,0:T(8,128)}), f32[4,4,8,24,128]{4,3,2,1,0:T(8,128)S(1)}, u32[]{:S(2)}, u32[]{:S(2)}) async-start(f32[4,4,8,24,128]{4,3,2,1,0:T(8,128)} %broadcast_in_dim.31), calls=%async_computation.10 | async-start | bytes 3145728 | tf_op jit(solution)/shard_map/all_to_all | solution.py:226
  148.5 2.5 %copy-start.3 = (bf16[1024,147]{1,0:T(8,128)(2,1)S(1)}, bf16[1024,147]{1,0:T(8,128)(2,1)}, u32[]{:S(2)}) copy-start(bf16[1024,147]{1,0:T(8,128)(2,1)} %get-tuple-element.20) | copy-start | bytes 903172
  209.1 2.5 %copy-start.4 = (f32[1024,147]{1,0:T(8,128)S(1)}, f32[1024,147]{1,0:T(8,128)}, u32[]{:S(2)}) copy-start(f32[1024,147]{1,0:T(8,128)} %get-tuple-element.17) | copy-start | bytes 1806340

commit v2 on v1

v2 whole, which is shorter than its diff:
```python
import functools

import jax
import jax.numpy as jnp
import numpy as np
from jax import lax
from jax.experimental import pallas as pl
from jax.experimental.pallas import tpu as pltpu
from jax.sharding import Mesh, PartitionSpec as P

f32 = jnp.float32
bf16 = jnp.bfloat16
root_two = 1.4142135623730951
ridge = 1.0
tile = 128
step = 256
own_width = 4
NN = (((1,), (0,)), ((), ()))
NT = (((1,), (1,)), ((), ()))


def cosine_coefficients(degree):
    nodes = 0.125 * np.cos(np.pi * (np.arange(400) + 0.5) / 400) + 0.125
    wanted = root_two * np.cos(2 * np.pi * np.sqrt(nodes))
    fitted = np.polynomial.chebyshev.Chebyshev.fit(nodes, wanted, degree, domain=[0, 0.25])
    return [float(c) for c in fitted.convert(kind=np.polynomial.Polynomial).coef]


cosine = cosine_coefficients(6)


def features_of(angles):
    turns = angles * (0.5 / np.pi)
    part = turns - jnp.round(turns)
    square = part * part
    value = cosine[-1] * square + cosine[-2]
    for coefficient in cosine[-3::-1]:
        value = value * square + coefficient
    return value.astype(bf16)


def dot(a, b, dims=NN):
    return lax.dot_general(a, b, dims, preferred_element_type=f32)


def split(x):
    high = x.astype(bf16)
    return high, (x - high.astype(f32)).astype(bf16)


def product(a, b):
    return dot(a[0], b[0]) + (dot(a[0], b[1]) + dot(a[1], b[0]))


def pairs(blocks):
    return [(a, b) for a in range(blocks) for b in range(a + 1)]


def layout(width, classes):
    blocks = width // tile
    lower = len(pairs(blocks)) * tile
    each = (-(-(lower + blocks * classes) // 2048) * 2048 - lower) // blocks
    return blocks, lower, each, lower + blocks * each


def moment_kernel(
    total_rows, place, mine, other, frames, phase, labels, predictions, own, turned, keep, send,
    packed, residual, sems,
):
    width, (classes, rows) = phase.shape[0], predictions.shape
    depth = frames.shape[0]
    blocks, lower, each, total = layout(width, classes)
    half = total // 2
    core, x = place[0], place[1]
    residual[...] = jnp.zeros_like(residual)
    onehot = labels[...] == lax.broadcasted_iota(jnp.int32, (classes, rows), 0)
    residual[:classes, :] = onehot.astype(f32) - predictions[...]
    wanted = residual[...].astype(bf16)
    row = 0
    for i in range(width // step):
        here = slice(i * step, (i + 1) * step)
        first = (i * step) % (width // 2)
        side = core == (i * step) // (width // 2)
        freqs = jnp.where(side, mine[first : first + step, :], other[first : first + step, :])
        angles = dot(freqs[:, :depth], frames[...]) + phase[here, :]
        block = features_of(angles)
        turned[here, :] = block
        gram = dot(block, turned[: (i + 1) * step, :], NT)
        cross = dot(wanted, block, NT)
        for j in range(step // tile):
            a = i * (step // tile) + j
            for b in range(a + 1):
                packed[row // half, row % half : row % half + tile, :] = gram[
                    j * tile : (j + 1) * tile, b * tile : (b + 1) * tile
                ]
                row += tile
            start = lower + a * each - half
            packed[1, start : start + each, :] = cross[:, j * tile : (j + 1) * tile]
    start = pl.multiple_of(lower - half + each * (core * (blocks // 2) + x), 8)
    packed[1, pl.ds(start, each), :] -= own[...] * total_rows
    copies = [
        pltpu.make_async_copy(packed.at[core], keep, sems.at[0]),
        pltpu.make_async_copy(packed.at[1 - core], send, sems.at[1]),
    ]
    for copy in copies:
        copy.start()
    for copy in copies:
        copy.wait()


def moments(place, mine, other, frames, phase, labels, predictions, own, total_rows):
    width, (classes, rows) = phase.shape[0], predictions.shape
    _, _, each, total = layout(width, classes)
    here = pl.BlockSpec(memory_space=pltpu.VMEM)
    half = jax.ShapeDtypeStruct((total // 2, tile), f32)
    return pl.pallas_call(
        functools.partial(moment_kernel, float(total_rows)),
        out_shape=(jax.ShapeDtypeStruct((width, rows), bf16), half, half),
        in_specs=[pl.BlockSpec(memory_space=pltpu.SMEM)] + [here] * 7,
        out_specs=(here, pl.BlockSpec(memory_space=pl.ANY), pl.BlockSpec(memory_space=pl.ANY)),
        scratch_shapes=[
            pltpu.VMEM((2, total // 2, tile), f32),
            pltpu.VMEM((each, rows), f32),
            pltpu.SemaphoreType.DMA((2,)),
        ],
        compiler_params=pltpu.CompilerParams(vmem_limit_bytes=40 * 1024 * 1024),
        name="moments",
    )(place, mine, other, frames, phase, labels, predictions, own)


def inverse(a, eye):
    bound = 2.0 * a.shape[0]
    scale = 2.0 / (2.0 * ridge + bound)
    spread = bound / (2.0 * ridge + bound)
    rest = eye - scale * a
    for k in range(7):
        gain = 2.0 / (2.0 - spread * spread)
        parts = split(rest)
        x = (gain * scale) * (eye + rest) if k == 0 else gain * (x + product(split(x), parts))
        spread = spread * spread / (2.0 - spread * spread)
        if k < 6:
            rest = gain * product(parts, parts) - spread * eye
    missing = eye - product(split(a), split(x))
    return x + product(split(x), split(missing))


def solve_kernel(
    total_rows, place, mine, other, old, turned, predictions, coeffs, updated,
    system, work, inv_h, inv_l, low_h, low_l, up_h, up_l, right, found,
):
    width = system.shape[0]
    classes = predictions.shape[0]
    blocks, lower, each, total = layout(width, classes)
    count = width // step
    scale = 1.0 / total_rows
    padded = right.shape[0]
    core = place[0]

    def sums(start, rows):
        part, start = divmod(start, total // 2)
        there = slice(start, start + rows)
        return jnp.where(core == part, mine[there, :], other[there, :])

    eye = (
        lax.broadcasted_iota(jnp.int32, (step, step), 0)
        == lax.broadcasted_iota(jnp.int32, (step, step), 1)
    ).astype(f32)
    for t, (a, b) in enumerate(pairs(blocks)):
        part = sums(t * tile, tile) * scale
        if a == b:
            part = part + ridge * eye[:tile, :tile]
        system[a * tile : (a + 1) * tile, b * tile : (b + 1) * tile] = part
        if a != b:
            system[b * tile : (b + 1) * tile, a * tile : (a + 1) * tile] = part.T
    for m in range(blocks):
        right[:, m * tile : (m + 1) * tile] = sums(lower + m * each, padded) * scale

    def at(k):
        return slice(k * step, (k + 1) * step)

    for k in range(count):
        source = system if k == 0 else work
        x = split(inverse(source[at(k), at(k)], eye))
        inv_h[at(k), :], inv_l[at(k), :] = x
        if k == count - 1:
            break
        after = slice((k + 1) * step, width)
        column = split(product(split(source[after, at(k)]), x))
        low_h[after, at(k)], low_l[after, at(k)] = column
        row = split(source[at(k), after])
        up_h[at(k), after], up_l[at(k), after] = row
        work[after, after] = source[after, after] - product(column, row)

    def apply(parts):
        parts = list(parts)
        for k in range(count):
            now = parts[k] = product(split(parts[k]), (inv_h[at(k), :], inv_l[at(k), :]))
            if k < count - 1:
                after = slice((k + 1) * step, width)
                less = product(split(now), (up_h[at(k), after], up_l[at(k), after]))
                for i in range(k + 1, count):
                    parts[i] = parts[i] - less[:, (i - k - 1) * step : (i - k) * step]
        for k in reversed(range(1, count)):
            before = slice(0, k * step)
            less = product(split(parts[k]), (low_h[at(k), before], low_l[at(k), before]))
            for i in range(k):
                parts[i] = parts[i] - less[:, i * step : (i + 1) * step]
        return parts

    for k, part in enumerate(apply([right[:, at(k)] for k in range(count)])):
        found[:, at(k)] = part
    for _ in range(2):
        short = right[...] - lax.dot_general(
            found[...], system[...], NN, precision=lax.Precision.HIGHEST, preferred_element_type=f32
        )
        for k, part in enumerate(apply([short[:, at(k)] for k in range(count)])):
            found[:, at(k)] += part
    change = found[...]
    added = dot(change.astype(bf16), turned[...])
    updated[...] = predictions[...] + added[:classes]
    at_row = lax.broadcasted_iota(jnp.int32, (2 * tile, 2 * tile), 0)
    at_lane = lax.broadcasted_iota(jnp.int32, (2 * tile, 2 * tile), 1)
    goal = (at_row % tile) // own_width * (2 * own_width) + at_row // tile * own_width + at_row % own_width
    order = (goal == at_lane).astype(bf16)
    early = old[pl.ds(0, width, stride=2), :]
    late = old[pl.ds(1, width, stride=2), :]
    for u in range(width // (2 * tile)):
        one, two = slice(u * tile, (u + 1) * tile), slice(width // 2 + u * tile, width // 2 + (u + 1) * tile)
        lanes = slice(2 * u * tile, 2 * (u + 1) * tile)
        part = jnp.concatenate([found[:, one], found[:, two]], axis=1)
        high, low = split(part)
        last = (part - high.astype(f32) - low.astype(f32)).astype(bf16)
        moved = (dot(high, order) + dot(low, order)) + dot(last, order)
        coeffs[:tile, lanes] = moved[:tile] + early[lanes].T
        coeffs[tile:, lanes] = moved[tile:classes] + late[lanes].T[: classes - tile]


def solve(place, mine, other, old, turned, predictions, total_rows):
    width, (classes, rows) = turned.shape[0], predictions.shape
    here = pl.BlockSpec(memory_space=pltpu.VMEM)
    padded = -(-classes // 16) * 16
    return pl.pallas_call(
        functools.partial(solve_kernel, float(total_rows)),
        out_shape=(
            jax.ShapeDtypeStruct((classes, width), f32),
            jax.ShapeDtypeStruct((classes, rows), f32),
        ),
        in_specs=[pl.BlockSpec(memory_space=pltpu.SMEM)] + [here] * 5,
        out_specs=(here, here),
        scratch_shapes=[
            pltpu.VMEM((width, width), f32),
            pltpu.VMEM((width, width), f32),
            pltpu.VMEM((width, step), bf16),
            pltpu.VMEM((width, step), bf16),
            pltpu.VMEM((width, width), bf16),
            pltpu.VMEM((width, width), bf16),
            pltpu.VMEM((width, width), bf16),
            pltpu.VMEM((width, width), bf16),
            pltpu.VMEM((padded, width), f32),
            pltpu.VMEM((padded, width), f32),
        ],
        compiler_params=pltpu.CompilerParams(vmem_limit_bytes=48 * 1024 * 1024),
        name="solve",
    )(place, mine, other, old, turned, predictions)


def exchange(x, axes):
    return lax.all_to_all(x, axes, 0, 0, tiled=True)


def gather(x, axes):
    return exchange(jnp.broadcast_to(x[None], (lax.axis_size(axes), *x.shape)), axes)


def swap(x):
    return lax.ppermute(x, "core", [(0, 1), (1, 0)])


def local(frames, freqs, phase, labels, predictions, coeffs_old):
    rows, classes = predictions.shape
    depth, own = freqs.shape
    width = phase.shape[0]
    cores = lax.axis_size("core")
    devices = width // own
    x, y, z = (lax.axis_index(axis) for axis in ("x", "y", "z"))
    place = jnp.stack([lax.axis_index("core"), x]).astype(jnp.int32)
    sent = jnp.pad(freqs.T, ((0, 0), (0, -depth % tile)))
    mine = gather(sent, "z").reshape(-1, sent.shape[1])
    mine = gather(mine, ("x", "y")).reshape(width // cores, sent.shape[1])
    other = swap(mine)
    old = jnp.pad(coeffs_old, ((0, 0), (0, -classes % tile))).reshape(-1, tile)
    old = lax.all_gather(old, ("x", "y", "z", "core"), axis=0, tiled=True)
    phase = phase.reshape(devices // cores, cores, own).swapaxes(0, 1).reshape(width, 1)
    _, _, each, total = layout(width, classes)
    owned = jnp.zeros((each, tile), f32)
    owned = lax.dynamic_update_slice(
        owned, coeffs_old.T, (0, (y * lax.axis_size("z") + z) * own)
    )
    turned, keep, send = moments(
        place, mine, other, frames.T, phase, labels[None, :], predictions.T, owned, rows * devices
    )
    sums = (keep + swap(send)).reshape(lax.axis_size(("x", "y")), -1, tile)
    sums = exchange(sums, ("x", "y")).sum(0)
    sums = exchange(sums.reshape(lax.axis_size("z"), -1, tile), "z").sum(0)
    sums = gather(sums, "z").reshape(-1, tile)
    mine = gather(sums, ("x", "y")).reshape(-1, tile)
    other = swap(mine)
    coeffs_new, new_predictions = solve(
        place, mine, other, old, turned, predictions.T, rows * devices
    )
    return new_predictions.T, coeffs_new.T


def solution(mesh):
    chips = mesh.devices.reshape(4, 4, 8, 2)
    inner = Mesh(chips, ("x", "y", "z", "core"))
    every = ("x", "y", "z", "core")
    placed = (P(every, None), P(None, every), P(), P(every), P(every, None), P(every, None))
    return jax.shard_map(
        local, mesh=inner, in_specs=placed, out_specs=(P(every, None), P()), check_vma=False
    )
```

time: 214 us -> 253 us (1.18)
  waiting for transfers between devices: 16 us -> 105 us
  blocking collectives: 121 us -> 76.3 us
  local copies, waits for them, and re-layouts: 22.7 us -> 5.57 us
  between operations: 0.78 us -> 14.2 us
  starting transfers between devices: 7.71 us -> 13.3 us
  other arithmetic: 4.68 us -> 0.33 us
    all_gather x0 -> x1, waiting for transfers between devices: none -> 82.9 us  [local(): old = lax.all_gather(old, ('x', 'y', 'z', 'core'), axis=0, tiled=True)]
    all_to_all x10 -> x5, blocking collectives: 121 us -> 76.3 us  [exchange(): return lax.all_to_all(x, axes, 0, 0, tiled=True)]
    ppermute x0 -> x3, starting transfers between devices: none -> 9.05 us  [swap(): return lax.ppermute(x, 'core', [(0, 1), (1, 0)])]
    unnamed x21 -> x15, local copies, waits for them, and re-layouts: 10.3 us -> 1.35 us
    reduce_sum x4 -> x2, other arithmetic: 3.83 us -> 0.09 us  [the longest x1 0.08 us: local(): sums = exchange(sums, ('x', 'y')).sum(0)]
    all_to_all x2 -> x1, starting transfers between devices: 7.71 us -> 4.19 us  [exchange(): return lax.all_to_all(x, axes, 0, 0, tiled=True)]
    ppermute x0 -> x3, waiting for transfers between devices: none -> 3.28 us  [swap(): return lax.ppermute(x, 'core', [(0, 1), (1, 0)])]
    all_to_all x2 -> x1, waiting for transfers between devices: 16 us -> 18.3 us  [exchange(): return lax.all_to_all(x, axes, 0, 0, tiled=True)]
  transfers between devices with their start and end apart: 2 -> 5, of which waited for: 2 -> 3; matrix products, arithmetic and copies ran while one was open for 4% -> 1% of each run, Pallas kernels for 0% -> 0%
where the time goes in v2:
time: 253 us
  waiting for transfers between devices  105 us (42%)
  blocking collectives  76.3 us (30%)
  Pallas kernels  38.3 us (15%)
  between operations  14.2 us (6%)
  starting transfers between devices  13.3 us (5%)
  local copies, waits for them, and re-layouts  5.57 us (2%)
    all_gather x1, waiting for transfers between devices, local(): old = lax.all_gather(old, ('x', 'y', 'z', 'core'), axis=0, tiled=True)  82.9 us
    all_to_all x5, blocking collectives, exchange(): return lax.all_to_all(x, axes, 0, 0, tiled=True)  76.3 us
    pallas_call x1, Pallas kernels, solve(): pl.pallas_call(functools.partial(solve_kernel, float(total_rows)), out_sh...  32.6 us
    all_to_all x1, waiting for transfers between devices, exchange(): return lax.all_to_all(x, axes, 0, 0, tiled=True)  18.3 us
    ppermute x3, starting transfers between devices, swap(): return lax.ppermute(x, 'core', [(0, 1), (1, 0)])  9.05 us
    pallas_call x1, Pallas kernels, moments(): pl.pallas_call(functools.partial(moment_kernel, float(total_rows)), out_s...  5.7 us
  transfers between devices with their start and end apart: 5, of which 3 were waited for; matrix products, arithmetic and copies ran while one was open for 1% of the time, Pallas kernels for 0%

profile of v2, /device:TPU:1, one launch (start us, length us, event | category | flops | bytes accessed | tf_op | source)
XLA Modules:
  0.0 252.6 jit_solution(979561602922595480)
XLA Ops:
  7.2 0.7 pad.8
  7.9 15.7 %all_to_all.30 = bf16[8,4,512]{2,1,0:T(4,128)(2,1)S(1)} all-to-all(bf16[8,4,512]{2,1,0:T(4,128)(2,1)S(1)} %broadcast_in_dim.32), channel_id=1, replica_groups=mesh['x'=4,'y'=4,'z'=8,'core'=2] {'z'}, dimensions={0} | all-to-all | bytes 65536 | tf_op jit(solution)/shard_map/all_to_all | solution.py:268
  23.7 15.9 %all_to_all.31 = bf16[16,32,512]{2,1,0:T(8,128)(2,1)S(1)} all-to-all(bf16[16,32,512]{2,1,0:T(8,128)(2,1)S(1)} %broadcast_in_dim.34), channel_id=1, replica_groups=mesh['x'=4,'y'=4,'z'=8,'core'=2] {'x','y'}, dimensions={0} | all-to-all | bytes 1048576 | tf_op jit(solution)/shard_map/all_to_all | solution.py:268
  39.6 3.2 %collective-permute-start = (bf16[512,512]{1,0:T(8,128)(2,1)S(1)}, bf16[512,512]{1,0:T(8,128)(2,1)S(1)}, u32[]{:S(2)}, u32[]{:S(2)}) collective-permute-start(bf16[512,512]{1,0:T(8,128)(2,1)S(1)} %bitcast.19), channel_id=1, source_target_pairs={{0,1},{1,0},{2,3},{3,2},{4,5},{5,4},{6,7},{7,6},{8,9},{9,8},{10,11... | collective-permute-start | bytes 1572872 | tf_op jit(solution)/shard_map/ppermute | solution.py:276
  42.8 0.1 copy.13
  43.0 0.2 reshape.30
  43.2 0.2 reshape.36.phase
  43.4 1.1 dynamic_update_slice.3.own
  44.6 5.7 %moments.1 = (bf16[1024,1024]{1,0:T(8,128)(2,1)S(1)}, f32[3072,128]{1,0:T(8,128)S(1)}, f32[3072,128]{1,0:T(8,128)S(1)}) custom-call(s32[2]{0:T(128)S(1)} %pad_add_fusion.place, bf16[512,512]{1,0:T(8,128)(2,1)S(1)} %bitcast.20, bf16[512,512]{1,0:T(8,128)(2,1)S(1)} %collective-permute-done.other, bf16[440,1024]{1,0:T(8,128)(2,1)S(1)} %bitcast.21, ...), custom_call_target="tpu_custom_call" | custom-call | tf_op jit(solution)/shard_map/moments/pallas_call | solution.py:116
  50.3 0.2 collective-permute-start.1
  50.6 3.3 %collective-permute-done.1 = f32[3072,128]{1,0:T(8,128)S(1)} collective-permute-done((f32[3072,128]{1,0:T(8,128)S(1)}, f32[3072,128]{1,0:T(8,128)S(1)}, u32[]{:S(2)}, u32[]{:S(2)}) %collective-permute-start.1) | collective-permute-done | bytes 1572896 | tf_op jit(solution)/shard_map/ppermute | solution.py:276
  53.8 0.2 add.15
  54.0 24.8 %all_to_all.32 = f32[16,192,128]{2,1,0:T(8,128)S(1)} all-to-all(f32[16,192,128]{2,1,0:T(8,128)S(1)} %bitcast.23), channel_id=1, replica_groups=mesh['x'=4,'y'=4,'z'=8,'core'=2] {'x','y'}, dimensions={0} | all-to-all | bytes 3145728 | tf_op jit(solution)/shard_map/all_to_all | solution.py:268
  78.8 0.1 reduce_sum.18
  78.9 10.0 %all_to_all.33 = f32[8,24,128]{2,1,0:T(8,128)S(1)} all-to-all(f32[8,24,128]{2,1,0:T(8,128)S(1)} %bitcast.25), channel_id=1, replica_groups=mesh['x'=4,'y'=4,'z'=8,'core'=2] {'z'}, dimensions={0} | all-to-all | bytes 196608 | tf_op jit(solution)/shard_map/all_to_all | solution.py:268
  88.9 10.0 %all_to_all.34 = f32[8,24,128]{2,1,0:T(8,128)S(1)} all-to-all(f32[8,24,128]{2,1,0:T(8,128)S(1)} %broadcast_in_dim.37), channel_id=1, replica_groups=mesh['x'=4,'y'=4,'z'=8,'core'=2] {'z'}, dimensions={0} | all-to-all | bytes 196608 | tf_op jit(solution)/shard_map/all_to_all | solution.py:268
  98.8 1.3 broadcast_in_dim.39
  100.1 4.2 %all-to-all-start.5 = ((f32[16,192,128]{2,1,0:T(8,128)}), f32[16,192,128]{2,1,0:T(8,128)S(1)}, u32[]{:S(2)}, u32[]{:S(2)}) async-start(f32[16,192,128]{2,1,0:T(8,128)} %broadcast_in_dim.39), calls=%async_computation.5 | async-start | bytes 3145728 | tf_op jit(solution)/shard_map/all_to_all | solution.py:268
  104.4 0.6 reshape.35
  105.1 18.3 %all-to-all-done.5 = f32[16,192,128]{2,1,0:T(8,128)S(1)} async-done(((f32[16,192,128]{2,1,0:T(8,128)}), f32[16,192,128]{2,1,0:T(8,128)S(1)}, u32[]{:S(2)}, u32[]{:S(2)}) %all-to-all-start.5) | async-done | bytes 1572896 | tf_op jit(solution)/shard_map/all_to_all | solution.py:268
  123.4 5.6 %collective-permute-start.2 = (f32[3072,128]{1,0:T(8,128)S(1)}, f32[3072,128]{1,0:T(8,128)}, u32[]{:S(2)}, u32[]{:S(2)}) collective-permute-start(f32[3072,128]{1,0:T(8,128)S(1)} %bitcast.15), channel_id=1, source_target_pairs={{0,1},{1,0},{2,3},{3,2},{4,5},{5,4},{6,7},{7,6},{8,9},{9,8},{10,11... | collective-permute-start | bytes 4718600 | tf_op jit(solution)/shard_map/ppermute | solution.py:276
  129.0 82.9 %all-gather.2.cloned.1.call-done.old = f32[2048,128]{1,0:T(8,128)} async-done(((f32[8,128]{1,0:T(8,128)}), f32[2048,128]{1,0:T(8,128)}) %all-gather.2.cloned.1.call-update) | async-done | bytes 1048592 | tf_op jit(solution)/shard_map/all_gather | solution.py:292
  211.9 1.2 copy-done.2
  213.1 32.6 %solve.1 = (f32[147,1024]{1,0:T(8,128)}, f32[147,1024]{1,0:T(8,128)}) custom-call(s32[2]{0:T(128)S(1)} %pad_add_fusion.place, f32[3072,128]{1,0:T(8,128)S(1)} %bitcast.16, f32[3072,128]{1,0:T(8,128)} %collective-permute-done.2.other, f32[2048,128]{1,0:T(8,128)S(1)} %copy-done.2, bf16[1024,1024]{1,0:T(8,128)(2,1)} %copy-done.1, f32[147,1024]{1,0:T(8,128)S(1)} %bitcast.18), custom_call_target="tpu_custom_call" | custom-call | tf_op jit(solution)/shard_map/solve/pallas_call | solution.py:242
  (26 shorter events, 0.3 us)
Async XLA Ops:
  7.2 35.7 %copy-start.5 = (f32[4,147]{1,0:T(4,128)S(1)}, f32[4,147]{1,0:T(4,128)}, u32[]{:S(2)}) copy-start(f32[4,147]{1,0:T(4,128)} %param.11) | copy-start | bytes 7060
  7.2 35.8 %copy-start.6 = (f32[1024]{0:T(1024)S(1)}, f32[1024]{0:T(1024)}, u32[]{:S(2)}) copy-start(f32[1024]{0:T(1024)} %param.8) | copy-start | bytes 12292
  23.6 21.0 %copy-start = (f32[1024,147]{0,1:T(8,128)S(1)}, f32[1024,147]{0,1:T(8,128)}, u32[]{:S(2)}) copy-start(f32[1024,147]{0,1:T(8,128)} %param.10) | copy-start | bytes 1806340
  23.6 21.0 %copy-start.3 = (bf16[1024,440]{0,1:T(8,128)(2,1)S(1)}, bf16[1024,440]{0,1:T(8,128)(2,1)}, u32[]{:S(2)}) copy-start(bf16[1024,440]{0,1:T(8,128)(2,1)} %param.6) | copy-start | bytes 2703364
  23.6 21.0 %copy-start.4 = (s32[1024]{0:T(1024)S(1)}, s32[1024]{0:T(1024)}, u32[]{:S(2)}) copy-start(s32[1024]{0:T(1024)} %param.9) | copy-start | bytes 12292
  39.6 5.0 %collective-permute-start = (bf16[512,512]{1,0:T(8,128)(2,1)S(1)}, bf16[512,512]{1,0:T(8,128)(2,1)S(1)}, u32[]{:S(2)}, u32[]{:S(2)}) collective-permute-start(bf16[512,512]{1,0:T(8,128)(2,1)S(1)} %bitcast.19), channel_id=1, source_target_pairs={{0,1},{1,0},{2,3},{3,2},{4,5},{5,4},{6,7},{7,6},{8,9},{9,8},{10,11... | collective-permute-start | bytes 1572872 | tf_op jit(solution)/shard_map/ppermute | solution.py:276
  50.3 3.7 %copy-start.1 = (bf16[1024,1024]{1,0:T(8,128)(2,1)}, bf16[1024,1024]{1,0:T(8,128)(2,1)S(1)}, u32[]{:S(2)}) copy-start(bf16[1024,1024]{1,0:T(8,128)(2,1)S(1)} %get-tuple-element.9.turned) | copy-start | bytes 6291460
  50.3 3.5 %collective-permute-start.1 = (f32[3072,128]{1,0:T(8,128)S(1)}, f32[3072,128]{1,0:T(8,128)S(1)}, u32[]{:S(2)}, u32[]{:S(2)}) collective-permute-start(f32[3072,128]{1,0:T(8,128)S(1)} %get-tuple-element.8), channel_id=1, source_target_pairs={{0,1},{1,0},{2,3},{3,2},{4,5},{5,4},{6,7},{7,6},{8,9},{9,8},{10,11... | collective-permute-start | bytes 4718600 | tf_op jit(solution)/shard_map/ppermute | solution.py:276
  100.1 23.2 %all-to-all-start.5 = ((f32[16,192,128]{2,1,0:T(8,128)}), f32[16,192,128]{2,1,0:T(8,128)S(1)}, u32[]{:S(2)}, u32[]{:S(2)}) async-start(f32[16,192,128]{2,1,0:T(8,128)} %broadcast_in_dim.39), calls=%async_computation.5 | async-start | bytes 3145728 | tf_op jit(solution)/shard_map/all_to_all | solution.py:268
  104.3 107.5 %all-gather.2.cloned.1.call-start = ((), (), s32[]{:S(2)}) async-start(), calls=%async_computation.6 | async-start | bytes 1052672 | tf_op jit(solution)/shard_map/all_gather | solution.py:292
  123.4 88.5 %collective-permute-start.2 = (f32[3072,128]{1,0:T(8,128)S(1)}, f32[3072,128]{1,0:T(8,128)}, u32[]{:S(2)}, u32[]{:S(2)}) collective-permute-start(f32[3072,128]{1,0:T(8,128)S(1)} %bitcast.15), channel_id=1, source_target_pairs={{0,1},{1,0},{2,3},{3,2},{4,5},{5,4},{6,7},{7,6},{8,9},{9,8},{10,11... | collective-permute-start | bytes 4718600 | tf_op jit(solution)/shard_map/ppermute | solution.py:276
  211.9 1.2 copy-start.2
Sparse Core Ops, SparseCore 0:
  109.5 102.3 all-gather.1

commit v3 on v2

v3 whole, which is shorter than its diff:
```python
import functools

import jax
import jax.numpy as jnp
import numpy as np
from jax import lax
from jax.experimental import pallas as pl
from jax.experimental.pallas import tpu as pltpu
from jax.sharding import Mesh, PartitionSpec as P

f32 = jnp.float32
bf16 = jnp.bfloat16
root_two = 1.4142135623730951
ridge = 1.0
tile = 128
step = 256
own_width = 4
depth_of = 440
NN = (((1,), (0,)), ((), ()))
NT = (((1,), (1,)), ((), ()))


def cosine_coefficients(degree):
    nodes = 0.125 * np.cos(np.pi * (np.arange(400) + 0.5) / 400) + 0.125
    wanted = root_two * np.cos(2 * np.pi * np.sqrt(nodes))
    fitted = np.polynomial.chebyshev.Chebyshev.fit(nodes, wanted, degree, domain=[0, 0.25])
    return [float(c) for c in fitted.convert(kind=np.polynomial.Polynomial).coef]


cosine = cosine_coefficients(6)


def features_of(angles):
    turns = angles * (0.5 / np.pi)
    part = turns - jnp.round(turns)
    square = part * part
    value = cosine[-1] * square + cosine[-2]
    for coefficient in cosine[-3::-1]:
        value = value * square + coefficient
    return value.astype(bf16)


def dot(a, b, dims=NN):
    return lax.dot_general(a, b, dims, preferred_element_type=f32)


def split(x):
    high = x.astype(bf16)
    return high, (x - high.astype(f32)).astype(bf16)


def product(a, b):
    return dot(a[0], b[0]) + (dot(a[0], b[1]) + dot(a[1], b[0]))


def pairs(blocks):
    return [(a, b) for a in range(blocks) for b in range(a + 1)]


def layout(width, classes):
    blocks = width // tile
    lower = len(pairs(blocks)) * tile
    each = (-(-(lower + blocks * classes) // 2048) * 2048 - lower) // blocks
    return blocks, lower, each, lower + blocks * each


def moment_kernel(
    place, mine, other, frames, phase, labels, predictions, turned, keep, send,
    packed, residual, sems,
):
    width, (classes, rows) = phase.shape[0], predictions.shape
    depth = frames.shape[0]
    blocks, lower, each, total = layout(width, classes)
    half = total // 2
    core = place[0]
    residual[...] = jnp.zeros_like(residual)
    onehot = labels[...] == lax.broadcasted_iota(jnp.int32, (classes, rows), 0)
    residual[:classes, :] = onehot.astype(f32) - predictions[...]
    wanted = residual[...].astype(bf16)
    row = 0
    for i in range(width // step):
        here = slice(i * step, (i + 1) * step)
        first = (i * step) % (width // 2)
        side = core == (i * step) // (width // 2)
        there = slice(first, first + step)
        freqs = jnp.where(side, mine[there, :depth], other[there, :depth])
        angles = dot(freqs, frames[...]) + phase[here, :]
        block = features_of(angles)
        turned[here, :] = block
        gram = dot(block, turned[: (i + 1) * step, :], NT)
        cross = dot(wanted, block, NT)
        for j in range(step // tile):
            a = i * (step // tile) + j
            for b in range(a + 1):
                packed[row // half, row % half : row % half + tile, :] = gram[
                    j * tile : (j + 1) * tile, b * tile : (b + 1) * tile
                ]
                row += tile
            start = lower + a * each - half
            packed[1, start : start + each, :] = cross[:, j * tile : (j + 1) * tile]
    copies = [
        pltpu.make_async_copy(packed.at[core], keep, sems.at[0]),
        pltpu.make_async_copy(packed.at[1 - core], send, sems.at[1]),
    ]
    for copy in copies:
        copy.start()
    for copy in copies:
        copy.wait()


def moments(place, mine, other, frames, phase, labels, predictions):
    width, (classes, rows) = phase.shape[0], predictions.shape
    _, _, each, total = layout(width, classes)
    here = pl.BlockSpec(memory_space=pltpu.VMEM)
    half = jax.ShapeDtypeStruct((total // 2, tile), f32)
    return pl.pallas_call(
        moment_kernel,
        out_shape=(jax.ShapeDtypeStruct((width, rows), bf16), half, half),
        in_specs=[pl.BlockSpec(memory_space=pltpu.SMEM)] + [here] * 6,
        out_specs=(here, pl.BlockSpec(memory_space=pl.ANY), pl.BlockSpec(memory_space=pl.ANY)),
        scratch_shapes=[
            pltpu.VMEM((2, total // 2, tile), f32),
            pltpu.VMEM((each, rows), f32),
            pltpu.SemaphoreType.DMA((2,)),
        ],
        compiler_params=pltpu.CompilerParams(vmem_limit_bytes=40 * 1024 * 1024),
        name="moments",
    )(place, mine, other, frames, phase, labels, predictions)


def inverse(a, eye):
    bound = 2.0 * a.shape[0]
    scale = 2.0 / (2.0 * ridge + bound)
    spread = bound / (2.0 * ridge + bound)
    rest = eye - scale * a
    x = scale * eye
    for k in range(7):
        gain = 2.0 / (2.0 - spread * spread)
        parts = split(rest)
        spread = spread * spread / (2.0 - spread * spread)
        if k == 0:
            x = gain * (x + scale * rest)
            rest = gain * product(parts, parts) - spread * eye
        else:
            x = gain * (x + product(split(x), parts))
            if k < 6:
                rest = gain * product(parts, parts) - spread * eye
    missing = eye - product(split(a), split(x))
    return x + product(split(x), split(missing))


def solve_kernel(
    total_rows, place, mine, other, mine_old, other_old, turned, predictions, coeffs, updated,
    system, work, inv_h, inv_l, low_h, low_l, up_h, up_l, found, old,
):
    width = turned.shape[0]
    classes = predictions.shape[0]
    blocks, lower, each, total = layout(width, classes)
    count = width // step
    scale = 1.0 / total_rows
    padded = found.shape[0]
    core = place[0]

    def sums(start, rows):
        part, start = divmod(start, total // 2)
        there = slice(start, start + rows)
        return jnp.where(core == part, mine[there, :], other[there, :])

    def at(k):
        return slice(k * step, (k + 1) * step)

    eye = (
        lax.broadcasted_iota(jnp.int32, (step, step), 0)
        == lax.broadcasted_iota(jnp.int32, (step, step), 1)
    ).astype(f32)
    for t, (a, b) in enumerate(pairs(blocks)):
        part = sums(t * tile, tile) * scale
        if a == b:
            part = part + ridge * eye[:tile, :tile]
        system[a * tile : (a + 1) * tile, b * tile : (b + 1) * tile] = part
        if a != b:
            system[b * tile : (b + 1) * tile, a * tile : (a + 1) * tile] = part.T
    for m in range(blocks):
        lanes = slice(m * tile, (m + 1) * tile)
        there = slice(m * tile % (width // 2), m * tile % (width // 2) + tile)
        side = core == m * tile // (width // 2)
        main, rest = 0.0, 0.0
        ends = jnp.where(side, mine_old[there, 3 * tile : 4 * tile], other_old[there, 3 * tile : 4 * tile])
        ends = ends.astype(f32).T
        first = depth_of % tile
        for i in range(3):
            lane = slice((4 + i) * tile, (5 + i) * tile)
            main = main + jnp.where(side, mine_old[there, lane], other_old[there, lane]).astype(f32)
            rest = rest + ends[first + i * (classes - tile) : first + (i + 1) * (classes - tile)]
        old[:tile, lanes] = main.T
        old[tile:, lanes] = jnp.zeros((padded - tile, tile), f32)
        old[tile:classes, lanes] = rest
        system[width:, lanes] = sums(lower + m * each, padded) * scale - old[:, lanes]
    parts = []
    for k in range(count):
        source = system if k == 0 else work
        x = split(inverse(source[at(k), at(k)], eye))
        inv_h[at(k), :], inv_l[at(k), :] = x
        column = product(split(source[(k + 1) * step :, at(k)]), x)
        parts.append(column[-padded:])
        if k == count - 1:
            break
        after = slice((k + 1) * step, width)
        column = split(column)
        low_h[after, at(k)], low_l[after, at(k)] = column[0][:-padded], column[1][:-padded]
        row = split(source[at(k), after])
        up_h[at(k), after], up_l[at(k), after] = row
        work[(k + 1) * step :, after] = source[(k + 1) * step :, after] - product(column, row)

    def backward(parts):
        for k in reversed(range(1, count)):
            before = slice(0, k * step)
            less = product(split(parts[k]), (low_h[at(k), before], low_l[at(k), before]))
            for i in range(k):
                parts[i] = parts[i] - less[:, i * step : (i + 1) * step]
        return parts

    def apply(parts):
        for k in range(count):
            now = parts[k] = product(split(parts[k]), (inv_h[at(k), :], inv_l[at(k), :]))
            if k < count - 1:
                after = slice((k + 1) * step, width)
                less = product(split(now), (up_h[at(k), after], up_l[at(k), after]))
                for i in range(k + 1, count):
                    parts[i] = parts[i] - less[:, (i - k - 1) * step : (i - k) * step]
        return backward(parts)

    for k, part in enumerate(backward(parts)):
        found[:, at(k)] = part

    def refine(state):
        short = system[width:, :] - lax.dot_general(
            found[...], system[:width, :], NN, precision=lax.Precision.HIGHEST,
            preferred_element_type=f32,
        )
        moved, size = 0.0, 0.0
        for k, part in enumerate(apply([short[:, at(k)] for k in range(count)])):
            found[:, at(k)] += part
            moved = jnp.maximum(moved, jnp.max(jnp.abs(part)))
            size = jnp.maximum(size, jnp.max(jnp.abs(found[:, at(k)])))
        return state[0] + 1, moved > 3e-4 * size

    lax.while_loop(lambda state: state[1] & (state[0] < 5), refine, (0, True))
    change = found[...]
    added = dot(change.astype(bf16), turned[...])
    updated[...] = predictions[...] + added[:classes]
    at_row = lax.broadcasted_iota(jnp.int32, (2 * tile, 2 * tile), 0)
    at_lane = lax.broadcasted_iota(jnp.int32, (2 * tile, 2 * tile), 1)
    goal = (at_row % tile) // own_width * (2 * own_width) + at_row // tile * own_width + at_row % own_width
    order = (goal == at_lane).astype(bf16)
    for u in range(width // (2 * tile)):
        one, two = slice(u * tile, (u + 1) * tile), slice(width // 2 + u * tile, width // 2 + (u + 1) * tile)
        part = jnp.concatenate([found[:, one] + old[:, one], found[:, two] + old[:, two]], axis=1)
        high, low = split(part)
        last = (part - high.astype(f32) - low.astype(f32)).astype(bf16)
        moved = (dot(high, order) + dot(low, order)) + dot(last, order)
        coeffs[:, 2 * u * tile : 2 * (u + 1) * tile] = moved[:classes]


def solve(place, mine, other, mine_old, other_old, turned, predictions, total_rows):
    width, (classes, rows) = turned.shape[0], predictions.shape
    here = pl.BlockSpec(memory_space=pltpu.VMEM)
    padded = -(-classes // 16) * 16
    return pl.pallas_call(
        functools.partial(solve_kernel, float(total_rows)),
        out_shape=(
            jax.ShapeDtypeStruct((classes, width), f32),
            jax.ShapeDtypeStruct((classes, rows), f32),
        ),
        in_specs=[pl.BlockSpec(memory_space=pltpu.SMEM)] + [here] * 6,
        out_specs=(here, here),
        scratch_shapes=[
            pltpu.VMEM((width + padded, width), f32),
            pltpu.VMEM((width + padded, width), f32),
            pltpu.VMEM((width, step), bf16),
            pltpu.VMEM((width, step), bf16),
            pltpu.VMEM((width, width), bf16),
            pltpu.VMEM((width, width), bf16),
            pltpu.VMEM((width, width), bf16),
            pltpu.VMEM((width, width), bf16),
            pltpu.VMEM((padded, width), f32),
            pltpu.VMEM((padded, width), f32),
        ],
        compiler_params=pltpu.CompilerParams(vmem_limit_bytes=48 * 1024 * 1024),
        name="solve",
    )(place, mine, other, mine_old, other_old, turned, predictions)


def exchange(x, axes):
    return lax.all_to_all(x, axes, 0, 0, tiled=True)


def gather(x, axes):
    return exchange(jnp.broadcast_to(x[None], (lax.axis_size(axes), *x.shape)), axes)


def swap(x):
    return lax.ppermute(x, "core", [(0, 1), (1, 0)])


def local(frames, freqs, phase, labels, predictions, coeffs_old):
    rows, classes = predictions.shape
    depth, own = freqs.shape
    width = phase.shape[0]
    cores = lax.axis_size("core")
    devices = width // own
    place = lax.axis_index("core").astype(jnp.int32)[None]
    first = lax.reduce_precision(coeffs_old, 8, 7)
    second = lax.reduce_precision(coeffs_old - first, 8, 7)
    olds = [part.astype(bf16) for part in (first, second, coeffs_old - first - second)]
    ends = jnp.concatenate([freqs.T] + [part[:, tile:] for part in olds], axis=1)
    ends = jnp.pad(ends, ((0, 0), (0, -ends.shape[1] % tile)))
    sent = jnp.concatenate([ends] + [part[:, :tile] for part in olds], axis=1)
    mine_sent = gather(sent, "z").reshape(-1, sent.shape[1])
    mine_sent = gather(mine_sent, ("x", "y")).reshape(width // cores, sent.shape[1])
    other_sent = swap(mine_sent)
    phase = phase.reshape(devices // cores, cores, own).swapaxes(0, 1).reshape(width, 1)
    turned, keep, send = moments(
        place, mine_sent, other_sent, frames.T, phase, labels[None, :], predictions.T
    )
    sums = (keep + swap(send)).reshape(lax.axis_size(("x", "y")), -1, tile)
    sums = exchange(sums, ("x", "y")).sum(0)
    sums = exchange(sums.reshape(lax.axis_size("z"), -1, tile), "z").sum(0)
    sums = gather(sums, "z").reshape(-1, tile)
    mine = gather(sums, ("x", "y")).reshape(-1, tile)
    other = swap(mine)
    coeffs_new, new_predictions = solve(
        place, mine, other, mine_sent, other_sent, turned, predictions.T, rows * devices
    )
    return new_predictions.T, coeffs_new.T


def solution(mesh):
    chips = mesh.devices.reshape(4, 4, 8, 2)
    inner = Mesh(chips, ("x", "y", "z", "core"))
    every = ("x", "y", "z", "core")
    placed = (P(every, None), P(None, every), P(), P(every), P(every, None), P(every, None))
    return jax.shard_map(
        local, mesh=inner, in_specs=placed, out_specs=(P(every, None), P()), check_vma=False
    )
```

time: 253 us -> 161 us (0.64); the launches traced: 253 us -> 158 us
  waiting for transfers between devices: 105 us -> 7.74 us
  blocking collectives: 76.3 us -> 102 us
  between operations: 14.2 us -> 0.77 us
  Pallas kernels: 38.3 us -> 32.6 us
  local copies, waits for them, and re-layouts: 5.57 us -> 1.88 us
  starting transfers between devices: 13.3 us -> 10.1 us
  other arithmetic: 0.33 us -> 3.14 us
    all_gather x1 -> x0, waiting for transfers between devices: 82.9 us -> none  [local(): old = lax.all_gather(old, ('x', 'y', 'z', 'core'), axis=0, tiled=True)]
    all_to_all x5 -> x6, blocking collectives: 76.3 us -> 102 us  [exchange(): return lax.all_to_all(x, axes, 0, 0, tiled=True)]
    all_to_all x1 -> x0, waiting for transfers between devices: 18.3 us -> none  [exchange(): return lax.all_to_all(x, axes, 0, 0, tiled=True)]
    pallas_call x1, Pallas kernels: 32.6 us -> 27.5 us  [solve(): pl.pallas_call(functools.partial(solve_kernel, float(total_rows)), out_sh...]
    ppermute x3, waiting for transfers between devices: 3.28 us -> 7.74 us  [swap(): return lax.ppermute(x, 'core', [(0, 1), (1, 0)])]
    all_to_all x1 -> x0, starting transfers between devices: 4.19 us -> none  [exchange(): return lax.all_to_all(x, axes, 0, 0, tiled=True)]
  transfers between devices with their start and end apart: 5 -> 3, of which waited for: 3 -> 3; matrix products, arithmetic and copies ran while one was open for 1% -> 0% of each run, Pallas kernels for 0% -> 0%
where the time goes in v3:
time: 161 us; the launch traced here: 158 us
  blocking collectives  102 us (63%)
  Pallas kernels  32.6 us (20%)
  starting transfers between devices  10.1 us (6%)
  waiting for transfers between devices  7.74 us (5%)
  other arithmetic  3.14 us (2%)
  local copies, waits for them, and re-layouts  1.88 us (1%)
    all_to_all x6, blocking collectives, exchange(): return lax.all_to_all(x, axes, 0, 0, tiled=True)  102 us
    pallas_call x1, Pallas kernels, solve(): pl.pallas_call(functools.partial(solve_kernel, float(total_rows)), out_sh...  27.5 us
    ppermute x3, starting transfers between devices, swap(): return lax.ppermute(x, 'core', [(0, 1), (1, 0)])  10.1 us
    ppermute x3, waiting for transfers between devices, swap(): return lax.ppermute(x, 'core', [(0, 1), (1, 0)])  7.74 us
    pallas_call x1, Pallas kernels, moments(): pl.pallas_call(moment_kernel, out_shape=(jax.ShapeDtypeStruct((width, row...  5.1 us
  transfers between devices with their start and end apart: 3, of which 3 were waited for; matrix products, arithmetic and copies ran while one was open for 0% of the time, Pallas kernels for 0%

profile of v3, /device:TPU:1, one launch (start us, length us, event | category | flops | bytes accessed | tf_op | source)
XLA Modules:
  0.0 157.9 jit_solution(15157967501532843920)
XLA Ops:
  0.6 0.7 reduce-precision_convert_fusion.1
  1.4 0.8 fusion.7
  2.2 16.1 %all_to_all.30 = bf16[8,4,896]{2,1,0:T(4,128)(2,1)S(1)} all-to-all(bf16[8,4,896]{2,1,0:T(4,128)(2,1)S(1)} %broadcast_in_dim.33), channel_id=1, replica_groups=mesh['x'=4,'y'=4,'z'=8,'core'=2] {'z'}, dimensions={0} | all-to-all | bytes 114688 | tf_op jit(solution)/shard_map/all_to_all | solution.py:295
  18.3 0.1 broadcast_in_dim.35
  18.3 0.0 copy-start
  18.4 19.7 %all_to_all.31 = bf16[16,32,896]{2,1,0:T(8,128)(2,1)S(1)} all-to-all(bf16[16,32,896]{2,1,0:T(8,128)(2,1)S(1)} %broadcast_in_dim.35), channel_id=1, replica_groups=mesh['x'=4,'y'=4,'z'=8,'core'=2] {'x','y'}, dimensions={0} | all-to-all | bytes 1835008 | tf_op jit(solution)/shard_map/all_to_all | solution.py:295
  38.0 3.4 %collective-permute-start = (bf16[512,896]{1,0:T(8,128)(2,1)S(1)}, bf16[512,896]{1,0:T(8,128)(2,1)S(1)}, u32[]{:S(2)}, u32[]{:S(2)}) collective-permute-start(bf16[512,896]{1,0:T(8,128)(2,1)S(1)} %bitcast.13), channel_id=1, source_target_pairs={{0,1},{1,0},{2,3},{3,2},{4,5},{5,4},{6,7},{7,6},{8,9},{9,8},{10,11... | collective-permute-start | bytes 2752520 | tf_op jit(solution)/shard_map/ppermute | solution.py:303
  41.4 0.2 reshape.27
  41.7 0.2 reshape.32.phase
  41.9 1.7 %collective-permute-done.other.other_old = bf16[512,896]{1,0:T(8,128)(2,1)S(1)} collective-permute-done((bf16[512,896]{1,0:T(8,128)(2,1)S(1)}, bf16[512,896]{1,0:T(8,128)(2,1)S(1)}, u32[]{:S(2)}, u32[]{:S(2)}) %collective-permute-start) | collective-permute-done | bytes 917536 | tf_op jit(solution)/shard_map/ppermute | solution.py:303
  43.5 1.2 copy-done.2
  44.7 5.1 %moments.1 = (bf16[1024,1024]{1,0:T(8,128)(2,1)S(1)}, f32[3072,128]{1,0:T(8,128)S(1)}, f32[3072,128]{1,0:T(8,128)S(1)}) custom-call(s32[1]{0:T(128)} %bitcast.place, bf16[512,896]{1,0:T(8,128)(2,1)S(1)} %bitcast.14, bf16[512,896]{1,0:T(8,128)(2,1)S(1)} %collective-permute-done.other.other_old, bf16[440,1024]{1,0:T(8,128)(2,1)S(1)} %bitcast.20, ...), custom_call_target="tpu_custom_call" | custom-call | tf_op jit(solution)/shard_map/moments/pallas_call | solution.py:116
  49.8 0.5 collective-permute-start.1
  50.3 3.0 %collective-permute-done.1 = f32[3072,128]{1,0:T(8,128)S(1)} collective-permute-done((f32[3072,128]{1,0:T(8,128)S(1)}, f32[3072,128]{1,0:T(8,128)S(1)}, u32[]{:S(2)}, u32[]{:S(2)}) %collective-permute-start.1) | collective-permute-done | bytes 1572896 | tf_op jit(solution)/shard_map/ppermute | solution.py:303
  53.3 0.2 add.5
  53.5 25.0 %all_to_all.32 = f32[16,192,128]{2,1,0:T(8,128)} all-to-all(f32[16,192,128]{2,1,0:T(8,128)S(1)} %bitcast.22), channel_id=1, replica_groups=mesh['x'=4,'y'=4,'z'=8,'core'=2] {'x','y'}, dimensions={0} | all-to-all | bytes 3145728 | tf_op jit(solution)/shard_map/all_to_all | solution.py:295
  78.5 1.5 reduce_sum.18
  80.0 10.1 %all_to_all.33 = f32[8,24,128]{2,1,0:T(8,128)S(1)} all-to-all(f32[8,24,128]{2,1,0:T(8,128)S(1)} %bitcast.24), channel_id=1, replica_groups=mesh['x'=4,'y'=4,'z'=8,'core'=2] {'z'}, dimensions={0} | all-to-all | bytes 196608 | tf_op jit(solution)/shard_map/all_to_all | solution.py:295
  90.1 10.1 %all_to_all.34 = f32[8,24,128]{2,1,0:T(8,128)S(1)} all-to-all(f32[8,24,128]{2,1,0:T(8,128)S(1)} %broadcast_in_dim.37), channel_id=1, replica_groups=mesh['x'=4,'y'=4,'z'=8,'core'=2] {'z'}, dimensions={0} | all-to-all | bytes 196608 | tf_op jit(solution)/shard_map/all_to_all | solution.py:295
  100.1 0.1 broadcast_in_dim.39
  100.3 20.8 %all_to_all.35 = f32[16,192,128]{2,1,0:T(8,128)S(1)} all-to-all(f32[16,192,128]{2,1,0:T(8,128)S(1)} %broadcast_in_dim.39), channel_id=1, replica_groups=mesh['x'=4,'y'=4,'z'=8,'core'=2] {'x','y'}, dimensions={0} | all-to-all | bytes 3145728 | tf_op jit(solution)/shard_map/all_to_all | solution.py:295
  121.0 6.2 %collective-permute-start.2 = (f32[3072,128]{1,0:T(8,128)S(1)}, f32[3072,128]{1,0:T(8,128)S(1)}, u32[]{:S(2)}, u32[]{:S(2)}) collective-permute-start(f32[3072,128]{1,0:T(8,128)S(1)} %bitcast.16), channel_id=1, source_target_pairs={{0,1},{1,0},{2,3},{3,2},{4,5},{5,4},{6,7},{7,6},{8,9},{9,8},{10,11... | collective-permute-start | bytes 4718600 | tf_op jit(solution)/shard_map/ppermute | solution.py:303
  127.3 3.0 %collective-permute-done.2.other = f32[3072,128]{1,0:T(8,128)S(1)} collective-permute-done((f32[3072,128]{1,0:T(8,128)S(1)}, f32[3072,128]{1,0:T(8,128)S(1)}, u32[]{:S(2)}, u32[]{:S(2)}) %collective-permute-start.2) | collective-permute-done | bytes 1572896 | tf_op jit(solution)/shard_map/ppermute | solution.py:303
  130.3 27.5 %solve.1 = (f32[147,1024]{1,0:T(8,128)}, f32[147,1024]{1,0:T(8,128)}) custom-call(s32[1]{0:T(128)} %bitcast.place, f32[3072,128]{1,0:T(8,128)S(1)} %bitcast.17, f32[3072,128]{1,0:T(8,128)S(1)} %collective-permute-done.2.other, bf16[512,896]{1,0:T(8,128)(2,1)S(1)} %bitcast.15, bf16[512,896]{1,0:T(8,128)(2,1)S(1)} %collective-permute-done.other.other_old, ...), custom_call_target="tpu_custom_call" | custom-call | tf_op jit(solution)/shard_map/solve/pallas_call | solution.py:269
  (20 shorter events, 0.1 us)
Async XLA Ops:
  1.3 40.1 %copy-start.4 = (f32[1024]{0:T(1024)S(1)}, f32[1024]{0:T(1024)}, u32[]{:S(2)}) copy-start(f32[1024]{0:T(1024)} %param.8) | copy-start | bytes 12292
  18.3 25.2 %copy-start = (f32[1024,147]{0,1:T(8,128)S(1)}, f32[1024,147]{0,1:T(8,128)}, u32[]{:S(2)}) copy-start(f32[1024,147]{0,1:T(8,128)} %param.10) | copy-start | bytes 1806340
  18.3 25.2 %copy-start.3 = (s32[1024]{0:T(1024)S(1)}, s32[1024]{0:T(1024)}, u32[]{:S(2)}) copy-start(s32[1024]{0:T(1024)} %param.9) | copy-start | bytes 12292
  38.0 5.5 %collective-permute-start = (bf16[512,896]{1,0:T(8,128)(2,1)S(1)}, bf16[512,896]{1,0:T(8,128)(2,1)S(1)}, u32[]{:S(2)}, u32[]{:S(2)}) collective-permute-start(bf16[512,896]{1,0:T(8,128)(2,1)S(1)} %bitcast.13), channel_id=1, source_target_pairs={{0,1},{1,0},{2,3},{3,2},{4,5},{5,4},{6,7},{7,6},{8,9},{9,8},{10,11... | collective-permute-start | bytes 2752520 | tf_op jit(solution)/shard_map/ppermute | solution.py:303
  43.5 1.2 copy-start.2
  49.8 3.7 %copy-start.1 = (bf16[1024,1024]{1,0:T(8,128)(2,1)}, bf16[1024,1024]{1,0:T(8,128)(2,1)S(1)}, u32[]{:S(2)}) copy-start(bf16[1024,1024]{1,0:T(8,128)(2,1)S(1)} %get-tuple-element.9.turned) | copy-start | bytes 6291460
  49.8 3.5 %collective-permute-start.1 = (f32[3072,128]{1,0:T(8,128)S(1)}, f32[3072,128]{1,0:T(8,128)S(1)}, u32[]{:S(2)}, u32[]{:S(2)}) collective-permute-start(f32[3072,128]{1,0:T(8,128)S(1)} %get-tuple-element.8), channel_id=1, source_target_pairs={{0,1},{1,0},{2,3},{3,2},{4,5},{5,4},{6,7},{7,6},{8,9},{9,8},{10,11... | collective-permute-start | bytes 4718600 | tf_op jit(solution)/shard_map/ppermute | solution.py:303
  121.0 9.3 %collective-permute-start.2 = (f32[3072,128]{1,0:T(8,128)S(1)}, f32[3072,128]{1,0:T(8,128)S(1)}, u32[]{:S(2)}, u32[]{:S(2)}) collective-permute-start(f32[3072,128]{1,0:T(8,128)S(1)} %bitcast.16), channel_id=1, source_target_pairs={{0,1},{1,0},{2,3},{3,2},{4,5},{5,4},{6,7},{7,6},{8,9},{9,8},{10,11... | collective-permute-start | bytes 4718600 | tf_op jit(solution)/shard_map/ppermute | solution.py:303

commit v4 on v3

--- a/solution.py
+++ b/solution.py
@@ -53,15 +53,24 @@
     return dot(a[0], b[0]) + (dot(a[0], b[1]) + dot(a[1], b[0]))
 
 
+def exact_product(a, b):
+    return lax.dot_general(a, b, NN, precision=lax.Precision.HIGHEST, preferred_element_type=f32)
+
+
 def pairs(blocks):
-    return [(a, b) for a in range(blocks) for b in range(a + 1)]
+    return [(a, b) for a in range(blocks) for b in range(a)]
 
 
 def layout(width, classes):
     blocks = width // tile
-    lower = len(pairs(blocks)) * tile
-    each = (-(-(lower + blocks * classes) // 2048) * 2048 - lower) // blocks
-    return blocks, lower, each, lower + blocks * each
+    below = len(pairs(blocks)) * tile
+    lower = below + blocks // 2 * tile
+    each = -(-(classes + 1) // 16) * 16
+    return blocks, below, lower, each, lower + blocks * each
+
+
+def coordinates(side):
+    return tuple(lax.broadcasted_iota(jnp.int32, (side, side), axis) for axis in (0, 1))
 
 
 def moment_kernel(
@@ -70,9 +79,10 @@
 ):
     width, (classes, rows) = phase.shape[0], predictions.shape
     depth = frames.shape[0]
-    blocks, lower, each, total = layout(width, classes)
+    blocks, below, lower, each, total = layout(width, classes)
     half = total // 2
     core = place[0]
+    at_row, at_lane = coordinates(tile)
     residual[...] = jnp.zeros_like(residual)
     onehot = labels[...] == lax.broadcasted_iota(jnp.int32, (classes, rows), 0)
     residual[:classes, :] = onehot.astype(f32) - predictions[...]
@@ -91,13 +101,19 @@
         cross = dot(wanted, block, NT)
         for j in range(step // tile):
             a = i * (step // tile) + j
-            for b in range(a + 1):
+            for b in range(a):
                 packed[row // half, row % half : row % half + tile, :] = gram[
                     j * tile : (j + 1) * tile, b * tile : (b + 1) * tile
                 ]
                 row += tile
             start = lower + a * each - half
             packed[1, start : start + each, :] = cross[:, j * tile : (j + 1) * tile]
+        even = gram[:tile, 2 * i * tile : (2 * i + 1) * tile]
+        odd = gram[tile:, (2 * i + 1) * tile :]
+        start = below + i * tile
+        packed[start // half, start % half : start % half + tile, :] = jnp.where(at_row >= at_lane, even, odd)
+        start = lower + (2 * i + 1) * each + classes - half
+        packed[1, start : start + 1, :] = jnp.sum(jnp.where(at_row == at_lane, odd, 0.0), axis=0, keepdims=True)
     copies = [
         pltpu.make_async_copy(packed.at[core], keep, sems.at[0]),
         pltpu.make_async_copy(packed.at[1 - core], send, sems.at[1]),
@@ -110,7 +126,7 @@
 
 def moments(place, mine, other, frames, phase, labels, predictions):
     width, (classes, rows) = phase.shape[0], predictions.shape
-    _, _, each, total = layout(width, classes)
+    _, _, _, each, total = layout(width, classes)
     here = pl.BlockSpec(memory_space=pltpu.VMEM)
     half = jax.ShapeDtypeStruct((total // 2, tile), f32)
     return pl.pallas_call(
@@ -123,28 +139,36 @@
             pltpu.VMEM((each, rows), f32),
             pltpu.SemaphoreType.DMA((2,)),
         ],
-        compiler_params=pltpu.CompilerParams(vmem_limit_bytes=40 * 1024 * 1024),
+        compiler_params=pltpu.CompilerParams(vmem_limit_bytes=18 * 1024 * 1024),
         name="moments",
     )(place, mine, other, frames, phase, labels, predictions)
 
 
-def inverse(a, eye):
-    bound = 2.0 * a.shape[0]
+def inverse(a, eye, bound, steps, loop=False):
     scale = 2.0 / (2.0 * ridge + bound)
-    spread = bound / (2.0 * ridge + bound)
-    rest = eye - scale * a
-    x = scale * eye
-    for k in range(7):
+
+    def advance(k, state):
+        x, rest, spread = state
         gain = 2.0 / (2.0 - spread * spread)
+        spread = spread * spread / (2.0 - spread * spread)
         parts = split(rest)
+        x = gain * (x + product(split(x), parts))
+        if loop or k < steps - 1:
+            rest = gain * product(parts, parts) - spread * eye
+        return x, rest, spread
+
+    state = scale * eye, eye - scale * a, bound / (2.0 * ridge + bound)
+    if loop:
+        state = lax.fori_loop(0, steps, advance, state[:2] + (jnp.float32(state[2]),))
+    else:
+        x, rest, spread = state
+        gain = 2.0 / (2.0 - spread * spread)
         spread = spread * spread / (2.0 - spread * spread)
-        if k == 0:
-            x = gain * (x + scale * rest)
-            rest = gain * product(parts, parts) - spread * eye
-        else:
-            x = gain * (x + product(split(x), parts))
-            if k < 6:
-                rest = gain * product(parts, parts) - spread * eye
+        parts = split(rest)
+        state = gain * (x + scale * rest), gain * product(parts, parts) - spread * eye, spread
+        for k in range(1, steps):
+            state = advance(k, state)
+    x = state[0]
     missing = eye - product(split(a), split(x))
     return x + product(split(x), split(missing))
 
@@ -155,7 +179,7 @@
 ):
     width = turned.shape[0]
     classes = predictions.shape[0]
-    blocks, lower, each, total = layout(width, classes)
+    blocks, below, lower, each, total = layout(width, classes)
     count = width // step
     scale = 1.0 / total_rows
     padded = found.shape[0]
@@ -169,17 +193,21 @@
     def at(k):
         return slice(k * step, (k + 1) * step)
 
-    eye = (
-        lax.broadcasted_iota(jnp.int32, (step, step), 0)
-        == lax.broadcasted_iota(jnp.int32, (step, step), 1)
-    ).astype(f32)
+    eye = functools.reduce(jnp.equal, coordinates(step)).astype(f32)
+    at_row, at_lane = coordinates(tile)
     for t, (a, b) in enumerate(pairs(blocks)):
         part = sums(t * tile, tile) * scale
-        if a == b:
-            part = part + ridge * eye[:tile, :tile]
         system[a * tile : (a + 1) * tile, b * tile : (b + 1) * tile] = part
-        if a != b:
-            system[b * tile : (b + 1) * tile, a * tile : (a + 1) * tile] = part.T
+        system[b * tile : (b + 1) * tile, a * tile : (a + 1) * tile] = part.T
+    for i in range(blocks // 2):
+        part = sums(below + i * tile, tile)
+        other_way = part.T
+        diagonal = sums(lower + (2 * i + 1) * each + classes, 1)
+        even = jnp.where(at_row >= at_lane, part, other_way)
+        odd = jnp.where(at_row == at_lane, diagonal, jnp.where(at_row < at_lane, part, other_way))
+        for a, part in ((2 * i, even), (2 * i + 1, odd)):
+            there = slice(a * tile, (a + 1) * tile)
+            system[there, there] = part * scale + ridge * eye[:tile, :tile]
     for m in range(blocks):
         lanes = slice(m * tile, (m + 1) * tile)
         there = slice(m * tile % (width // 2), m * tile % (width // 2) + tile)
@@ -195,12 +223,23 @@
         old[:tile, lanes] = main.T
         old[tile:, lanes] = jnp.zeros((padded - tile, tile), f32)
         old[tile:classes, lanes] = rest
-        system[width:, lanes] = sums(lower + m * each, padded) * scale - old[:, lanes]
+        valid = lax.broadcasted_iota(jnp.int32, (padded, tile), 0) < classes
+        system[width:, lanes] = jnp.where(valid, sums(lower + m * each, padded) * scale - old[:, lanes], 0.0)
     parts = []
     for k in range(count):
         source = system if k == 0 else work
-        x = split(inverse(source[at(k), at(k)], eye))
-        inv_h[at(k), :], inv_l[at(k), :] = x
+        block = source[at(k), at(k)]
+
+        def invert(bound, steps, loop=False):
+            inv_h[at(k), :], inv_l[at(k), :] = split(inverse(block, eye, bound, steps, loop))
+
+        if k == 0:
+            invert(2.0 * step, 7)
+        else:
+            small = jnp.max(jnp.sum(jnp.abs(block - ridge * eye), axis=0)) <= 6.0
+            pl.when(small)(functools.partial(invert, 6.0, 3))
+            pl.when(jnp.logical_not(small))(functools.partial(invert, 2.0 * step, 7, True))
+        x = inv_h[at(k), :], inv_l[at(k), :]
         column = product(split(source[(k + 1) * step :, at(k)]), x)
         parts.append(column[-padded:])
         if k == count - 1:
@@ -234,18 +273,47 @@
         found[:, at(k)] = part
 
     def refine(state):
-        short = system[width:, :] - lax.dot_general(
-            found[...], system[:width, :], NN, precision=lax.Precision.HIGHEST,
-            preferred_element_type=f32,
-        )
+        short = system[width:, :] - exact_product(found[...], system[:width, :])
         moved, size = 0.0, 0.0
         for k, part in enumerate(apply([short[:, at(k)] for k in range(count)])):
             found[:, at(k)] += part
-            moved = jnp.maximum(moved, jnp.max(jnp.abs(part)))
-            size = jnp.maximum(size, jnp.max(jnp.abs(found[:, at(k)])))
-        return state[0] + 1, moved > 3e-4 * size
-
-    lax.while_loop(lambda state: state[1] & (state[0] < 5), refine, (0, True))
+            moved += jnp.sum(part * part)
+            size += jnp.sum(found[:, at(k)] * found[:, at(k)])
+        return state[0] + 1, jnp.logical_not((moved <= 1e-6 * size) & (size < 1e30))
+
+    _, rough = lax.while_loop(lambda state: state[1] & (state[0] < 3), refine, (0, True))
+
+    @pl.when(rough)
+    def _():
+        found[...] = jnp.zeros_like(found)
+        gained, short, ahead = (slice(i * padded, (i + 1) * padded) for i in range(3))
+        tiny = 1e-30
+
+        def norms(there):
+            return jnp.sum(work[there, :] * work[there, :], axis=1, keepdims=True)
+
+        def restart(_, carry):
+            work[short, :] = system[width:, :] - exact_product(found[...], system[:width, :])
+            work[ahead, :] = work[short, :]
+            work[gained, :] = jnp.zeros_like(found)
+            first = norms(short)
+
+            def advance(state):
+                turn, _, size = state
+                image = exact_product(work[ahead, :], system[:width, :])
+                far = size / jnp.maximum(jnp.sum(work[ahead, :] * image, axis=1, keepdims=True), tiny)
+                work[gained, :] += far * work[ahead, :]
+                work[short, :] -= far * image
+                after = norms(short)
+                work[ahead, :] = work[short, :] + after / jnp.maximum(size, tiny) * work[ahead, :]
+                return turn + 1, jnp.max(after - 1e-12 * first) > 0.0, after
+
+            lax.while_loop(lambda state: state[1] & (state[0] < 500), advance, (0, True, first))
+            found[...] += work[gained, :]
+            return carry
+
+        lax.fori_loop(0, 3, restart, 0)
+
     change = found[...]
     added = dot(change.astype(bf16), turned[...])
     updated[...] = predictions[...] + added[:classes]
@@ -286,7 +354,7 @@
             pltpu.VMEM((padded, width), f32),
             pltpu.VMEM((padded, width), f32),
         ],
-        compiler_params=pltpu.CompilerParams(vmem_limit_bytes=48 * 1024 * 1024),
+        compiler_params=pltpu.CompilerParams(vmem_limit_bytes=38 * 1024 * 1024),
         name="solve",
     )(place, mine, other, mine_old, other_old, turned, predictions)
 
@@ -323,10 +391,13 @@
     turned, keep, send = moments(
         place, mine_sent, other_sent, frames.T, phase, labels[None, :], predictions.T
     )
+    shares = lax.axis_size("z")
     sums = (keep + swap(send)).reshape(lax.axis_size(("x", "y")), -1, tile)
     sums = exchange(sums, ("x", "y")).sum(0)
-    sums = exchange(sums.reshape(lax.axis_size("z"), -1, tile), "z").sum(0)
-    sums = gather(sums, "z").reshape(-1, tile)
+    share = sums.shape[0]
+    sums = jnp.pad(sums, ((0, -share % (8 * shares)), (0, 0)))
+    sums = exchange(sums.reshape(shares, -1, tile), "z").sum(0)
+    sums = gather(sums, "z").reshape(-1, tile)[:share]
     mine = gather(sums, ("x", "y")).reshape(-1, tile)
     other = swap(mine)
     coeffs_new, new_predictions = solve(

time: 161 us -> 147 us (0.913); the launches traced: 158 us -> 147 us
  Pallas kernels: 32.6 us -> 26.5 us
  blocking collectives: 102 us -> 98.5 us
    pallas_call x1, Pallas kernels: 27.5 us -> 21.3 us  [solve(): pl.pallas_call(functools.partial(solve_kernel, float(total_rows)), out_sh...]
    all_to_all x6, blocking collectives: 102 us -> 98.5 us  [exchange(): return lax.all_to_all(x, axes, 0, 0, tiled=True)]
where the time goes in v4:
time: 147 us
  blocking collectives  98.5 us (67%)
  Pallas kernels  26.5 us (18%)
  starting transfers between devices  8.91 us (6%)
  waiting for transfers between devices  7.18 us (5%)
  other arithmetic  3.04 us (2%)
  local copies, waits for them, and re-layouts  1.85 us (1%)
    all_to_all x6, blocking collectives, exchange(): return lax.all_to_all(x, axes, 0, 0, tiled=True)  98.5 us
    pallas_call x1, Pallas kernels, solve(): pl.pallas_call(functools.partial(solve_kernel, float(total_rows)), out_sh...  21.3 us
    ppermute x3, starting transfers between devices, swap(): return lax.ppermute(x, 'core', [(0, 1), (1, 0)])  8.91 us
    ppermute x3, waiting for transfers between devices, swap(): return lax.ppermute(x, 'core', [(0, 1), (1, 0)])  7.18 us
    pallas_call x1, Pallas kernels, moments(): pl.pallas_call(moment_kernel, out_shape=(jax.ShapeDtypeStruct((width, row...  5.13 us
  transfers between devices with their start and end apart: 3, of which 3 were waited for; matrix products, arithmetic and copies ran while one was open for 0% of the time, Pallas kernels for 0%

profile of v4, /device:TPU:1, one launch (start us, length us, event | category | flops | bytes accessed | tf_op | source)
XLA Modules:
  0.0 146.7 jit_solution(6343554197288199524)
XLA Ops:
  0.6 0.7 reduce-precision_convert_fusion.1
  1.4 0.8 fusion.7
  2.2 16.1 %all_to_all.30 = bf16[8,4,896]{2,1,0:T(4,128)(2,1)S(1)} all-to-all(bf16[8,4,896]{2,1,0:T(4,128)(2,1)S(1)} %broadcast_in_dim.34), channel_id=1, replica_groups=mesh['x'=4,'y'=4,'z'=8,'core'=2] {'z'}, dimensions={0} | all-to-all | bytes 114688 | tf_op jit(solution)/shard_map/all_to_all | solution.py:363
  18.2 0.0 copy-start.5
  18.3 0.1 broadcast_in_dim.36
  18.4 19.7 %all_to_all.31 = bf16[16,32,896]{2,1,0:T(8,128)(2,1)S(1)} all-to-all(bf16[16,32,896]{2,1,0:T(8,128)(2,1)S(1)} %broadcast_in_dim.36), channel_id=1, replica_groups=mesh['x'=4,'y'=4,'z'=8,'core'=2] {'x','y'}, dimensions={0} | all-to-all | bytes 1835008 | tf_op jit(solution)/shard_map/all_to_all | solution.py:363
  38.0 3.4 %collective-permute-start = (bf16[512,896]{1,0:T(8,128)(2,1)S(1)}, bf16[512,896]{1,0:T(8,128)(2,1)S(1)}, u32[]{:S(2)}, u32[]{:S(2)}) collective-permute-start(bf16[512,896]{1,0:T(8,128)(2,1)S(1)} %bitcast.13), channel_id=1, source_target_pairs={{0,1},{1,0},{2,3},{3,2},{4,5},{5,4},{6,7},{7,6},{8,9},{9,8},{10,11... | collective-permute-start | bytes 2752520 | tf_op jit(solution)/shard_map/ppermute | solution.py:371
  41.4 0.2 reshape.30
  41.7 0.2 reshape.35.phase
  41.9 1.7 %collective-permute-done.other.other_old = bf16[512,896]{1,0:T(8,128)(2,1)S(1)} collective-permute-done((bf16[512,896]{1,0:T(8,128)(2,1)S(1)}, bf16[512,896]{1,0:T(8,128)(2,1)S(1)}, u32[]{:S(2)}, u32[]{:S(2)}) %collective-permute-start) | collective-permute-done | bytes 917536 | tf_op jit(solution)/shard_map/ppermute | solution.py:371
  43.5 1.2 copy-done.3
  44.7 5.1 %moments.1 = (bf16[1024,1024]{1,0:T(8,128)(2,1)S(1)}, f32[2688,128]{1,0:T(8,128)S(1)}, f32[2688,128]{1,0:T(8,128)S(1)}) custom-call(s32[1]{0:T(128)} %bitcast.place, bf16[512,896]{1,0:T(8,128)(2,1)S(1)} %bitcast.14, bf16[512,896]{1,0:T(8,128)(2,1)S(1)} %collective-permute-done.other.other_old, bf16[440,1024]{1,0:T(8,128)(2,1)S(1)} %bitcast.20, ...), custom_call_target="tpu_custom_call" | custom-call | tf_op jit(solution)/shard_map/moments/pallas_call | solution.py:132
  49.9 0.5 collective-permute-start.1
  50.3 2.8 %collective-permute-done.1 = f32[2688,128]{1,0:T(8,128)S(1)} collective-permute-done((f32[2688,128]{1,0:T(8,128)S(1)}, f32[2688,128]{1,0:T(8,128)S(1)}, u32[]{:S(2)}, u32[]{:S(2)}) %collective-permute-start.1) | collective-permute-done | bytes 1376288 | tf_op jit(solution)/shard_map/ppermute | solution.py:371
  53.1 0.1 add.7
  53.2 22.7 %all_to_all.32 = f32[16,168,128]{2,1,0:T(8,128)} all-to-all(f32[16,168,128]{2,1,0:T(8,128)S(1)} %bitcast.22), channel_id=1, replica_groups=mesh['x'=4,'y'=4,'z'=8,'core'=2] {'x','y'}, dimensions={0} | all-to-all | bytes 2752512 | tf_op jit(solution)/shard_map/all_to_all | solution.py:363
  75.9 1.4 reduce_sum.18
  77.4 10.1 %all_to_all.33 = f32[8,24,128]{2,1,0:T(8,128)S(1)} all-to-all(f32[8,24,128]{2,1,0:T(8,128)S(1)} %bitcast.24), channel_id=1, replica_groups=mesh['x'=4,'y'=4,'z'=8,'core'=2] {'z'}, dimensions={0} | all-to-all | bytes 196608 | tf_op jit(solution)/shard_map/all_to_all | solution.py:363
  87.5 10.1 %all_to_all.34 = f32[8,24,128]{2,1,0:T(8,128)S(1)} all-to-all(f32[8,24,128]{2,1,0:T(8,128)S(1)} %broadcast_in_dim.38), channel_id=1, replica_groups=mesh['x'=4,'y'=4,'z'=8,'core'=2] {'z'}, dimensions={0} | all-to-all | bytes 196608 | tf_op jit(solution)/shard_map/all_to_all | solution.py:363
  97.5 0.1 broadcast_in_dim.40
  97.6 19.9 %all_to_all.35 = f32[16,168,128]{2,1,0:T(8,128)S(1)} all-to-all(f32[16,168,128]{2,1,0:T(8,128)S(1)} %broadcast_in_dim.40), channel_id=1, replica_groups=mesh['x'=4,'y'=4,'z'=8,'core'=2] {'x','y'}, dimensions={0} | all-to-all | bytes 2752512 | tf_op jit(solution)/shard_map/all_to_all | solution.py:363
  117.6 5.0 %collective-permute-start.2 = (f32[2688,128]{1,0:T(8,128)S(1)}, f32[2688,128]{1,0:T(8,128)S(1)}, u32[]{:S(2)}, u32[]{:S(2)}) collective-permute-start(f32[2688,128]{1,0:T(8,128)S(1)} %bitcast.16), channel_id=1, source_target_pairs={{0,1},{1,0},{2,3},{3,2},{4,5},{5,4},{6,7},{7,6},{8,9},{9,8},{10,11... | collective-permute-start | bytes 4128776 | tf_op jit(solution)/shard_map/ppermute | solution.py:371
  122.6 2.8 %collective-permute-done.2.other = f32[2688,128]{1,0:T(8,128)S(1)} collective-permute-done((f32[2688,128]{1,0:T(8,128)S(1)}, f32[2688,128]{1,0:T(8,128)S(1)}, u32[]{:S(2)}, u32[]{:S(2)}) %collective-permute-start.2) | collective-permute-done | bytes 1376288 | tf_op jit(solution)/shard_map/ppermute | solution.py:371
  125.4 21.3 %solve.1 = (f32[147,1024]{1,0:T(8,128)}, f32[147,1024]{1,0:T(8,128)}) custom-call(s32[1]{0:T(128)} %bitcast.place, f32[2688,128]{1,0:T(8,128)S(1)} %bitcast.17, f32[2688,128]{1,0:T(8,128)S(1)} %collective-permute-done.2.other, bf16[512,896]{1,0:T(8,128)(2,1)S(1)} %bitcast.15, bf16[512,896]{1,0:T(8,128)(2,1)S(1)} %collective-permute-done.other.other_old, ...), custom_call_target="tpu_custom_call" | custom-call | tf_op jit(solution)/shard_map/solve/pallas_call | solution.py:337
  (24 shorter events, 0.1 us)
Async XLA Ops:
  18.2 23.2 %copy-start.5 = (f32[1024]{0:T(1024)S(1)}, f32[1024]{0:T(1024)}, u32[]{:S(2)}) copy-start(f32[1024]{0:T(1024)} %param.8) | copy-start | bytes 12292
  18.3 25.2 %copy-start = (f32[1024,147]{0,1:T(8,128)S(1)}, f32[1024,147]{0,1:T(8,128)}, u32[]{:S(2)}) copy-start(f32[1024,147]{0,1:T(8,128)} %param.10) | copy-start | bytes 1806340
  18.3 25.2 %copy-start.4 = (s32[1024]{0:T(1024)S(1)}, s32[1024]{0:T(1024)}, u32[]{:S(2)}) copy-start(s32[1024]{0:T(1024)} %param.9) | copy-start | bytes 12292
  38.0 5.5 %collective-permute-start = (bf16[512,896]{1,0:T(8,128)(2,1)S(1)}, bf16[512,896]{1,0:T(8,128)(2,1)S(1)}, u32[]{:S(2)}, u32[]{:S(2)}) collective-permute-start(bf16[512,896]{1,0:T(8,128)(2,1)S(1)} %bitcast.13), channel_id=1, source_target_pairs={{0,1},{1,0},{2,3},{3,2},{4,5},{5,4},{6,7},{7,6},{8,9},{9,8},{10,11... | collective-permute-start | bytes 2752520 | tf_op jit(solution)/shard_map/ppermute | solution.py:371
  43.5 1.2 copy-start.3
  49.9 3.4 %copy-start.1 = (bf16[1024,1024]{1,0:T(8,128)(2,1)}, bf16[1024,1024]{1,0:T(8,128)(2,1)S(1)}, u32[]{:S(2)}) copy-start(bf16[1024,1024]{1,0:T(8,128)(2,1)S(1)} %get-tuple-element.9.turned) | copy-start | bytes 6291460
  49.9 3.2 %collective-permute-start.1 = (f32[2688,128]{1,0:T(8,128)S(1)}, f32[2688,128]{1,0:T(8,128)S(1)}, u32[]{:S(2)}, u32[]{:S(2)}) collective-permute-start(f32[2688,128]{1,0:T(8,128)S(1)} %get-tuple-element.8), channel_id=1, source_target_pairs={{0,1},{1,0},{2,3},{3,2},{4,5},{5,4},{6,7},{7,6},{8,9},{9,8},{10,11... | collective-permute-start | bytes 4128776 | tf_op jit(solution)/shard_map/ppermute | solution.py:371
  97.6 27.7 %copy-start.2 = (bf16[1024,1024]{1,0:T(8,128)(2,1)S(1)}, bf16[1024,1024]{1,0:T(8,128)(2,1)}, u32[]{:S(2)}) copy-start(bf16[1024,1024]{1,0:T(8,128)(2,1)} %copy-done.1) | copy-start | bytes 6291460
  117.6 7.8 %collective-permute-start.2 = (f32[2688,128]{1,0:T(8,128)S(1)}, f32[2688,128]{1,0:T(8,128)S(1)}, u32[]{:S(2)}, u32[]{:S(2)}) collective-permute-start(f32[2688,128]{1,0:T(8,128)S(1)} %bitcast.16), channel_id=1, source_target_pairs={{0,1},{1,0},{2,3},{3,2},{4,5},{5,4},{6,7},{7,6},{8,9},{9,8},{10,11... | collective-permute-start | bytes 4128776 | tf_op jit(solution)/shard_map/ppermute | solution.py:371

commit v5 on v4

--- a/solution.py
+++ b/solution.py
@@ -50,23 +50,46 @@
 
 
 def product(a, b):
-    return dot(a[0], b[0]) + (dot(a[0], b[1]) + dot(a[1], b[0]))
+    rows = a[0].shape[0]
+    both = dot(jnp.concatenate(a, axis=0), b[0])
+    return both[:rows] + (both[rows:] + dot(a[0], b[1]))
 
 
 def exact_product(a, b):
     return lax.dot_general(a, b, NN, precision=lax.Precision.HIGHEST, preferred_element_type=f32)
 
 
-def pairs(blocks):
-    return [(a, b) for a in range(blocks) for b in range(a)]
+def three(x):
+    high, low = split(x)
+    return high, low, (x - high.astype(f32) - low.astype(f32)).astype(bf16)
+
+
+def wide_product(x, wide):
+    rows, depth = x.shape
+    parts = jnp.concatenate(three(x), axis=0)
+    result = []
+    for j in range(depth // step):
+        high, low, last = three(wide[:depth, j * step : (j + 1) * step])
+        one = dot(parts, high)
+        two = dot(parts[: 2 * rows], low)
+        small = one[2 * rows :] + two[rows:] + dot(parts[:rows], last)
+        result.append(one[:rows] + ((one[rows : 2 * rows] + two[:rows]) + small))
+    return jnp.concatenate(result, axis=1)
 
 
 def layout(width, classes):
-    blocks = width // tile
-    below = len(pairs(blocks)) * tile
-    lower = below + blocks // 2 * tile
     each = -(-(classes + 1) // 16) * 16
-    return blocks, below, lower, each, lower + blocks * each
+    places, ends, rows = {}, [], [0, 0]
+    for a in range(0, width // tile, 2):
+        blocks = [(c, b) for c in (a, a + 1) for b in range(c)] + [(a, a)]
+        for n, block in enumerate(blocks):
+            places[block] = (n % 2, rows[n % 2])
+            rows[n % 2] += tile
+        for part in range(2):
+            places["cross", a + part] = (part, rows[part])
+            rows[part] += each
+        ends.append(rows[0])
+    return each, places, ends
 
 
 def coordinates(side):
@@ -79,15 +102,19 @@
 ):
     width, (classes, rows) = phase.shape[0], predictions.shape
     depth = frames.shape[0]
-    blocks, below, lower, each, total = layout(width, classes)
-    half = total // 2
+    each, places, ends = layout(width, classes)
     core = place[0]
     at_row, at_lane = coordinates(tile)
+    copies = []
+
+    def put(name, value, behind=0):
+        part, row = places[name]
+        packed[part, row + behind : row + behind + value.shape[0], :] = value
+
     residual[...] = jnp.zeros_like(residual)
     onehot = labels[...] == lax.broadcasted_iota(jnp.int32, (classes, rows), 0)
     residual[:classes, :] = onehot.astype(f32) - predictions[...]
     wanted = residual[...].astype(bf16)
-    row = 0
     for i in range(width // step):
         here = slice(i * step, (i + 1) * step)
         first = (i * step) % (width // 2)
@@ -102,42 +129,38 @@
         for j in range(step // tile):
             a = i * (step // tile) + j
             for b in range(a):
-                packed[row // half, row % half : row % half + tile, :] = gram[
-                    j * tile : (j + 1) * tile, b * tile : (b + 1) * tile
-                ]
-                row += tile
-            start = lower + a * each - half
-            packed[1, start : start + each, :] = cross[:, j * tile : (j + 1) * tile]
+                put((a, b), gram[j * tile : (j + 1) * tile, b * tile : (b + 1) * tile])
+            put(("cross", a), cross[:, j * tile : (j + 1) * tile])
         even = gram[:tile, 2 * i * tile : (2 * i + 1) * tile]
         odd = gram[tile:, (2 * i + 1) * tile :]
-        start = below + i * tile
-        packed[start // half, start % half : start % half + tile, :] = jnp.where(at_row >= at_lane, even, odd)
-        start = lower + (2 * i + 1) * each + classes - half
-        packed[1, start : start + 1, :] = jnp.sum(jnp.where(at_row == at_lane, odd, 0.0), axis=0, keepdims=True)
-    copies = [
-        pltpu.make_async_copy(packed.at[core], keep, sems.at[0]),
-        pltpu.make_async_copy(packed.at[1 - core], send, sems.at[1]),
-    ]
-    for copy in copies:
-        copy.start()
+        put((2 * i, 2 * i), jnp.where(at_row >= at_lane, even, odd))
+        diagonal = jnp.sum(jnp.where(at_row == at_lane, odd, 0.0), axis=0, keepdims=True)
+        put(("cross", 2 * i + 1), diagonal, classes)
+        start = ends[i - 1] if i else 0
+        done = pl.ds(start, ends[i] - start)
+        for n, target in enumerate((keep, send)):
+            source = packed.at[core if n == 0 else 1 - core, done]
+            copy = pltpu.make_async_copy(source, target.at[done], sems.at[i, n])
+            copy.start()
+            copies.append(copy)
     for copy in copies:
         copy.wait()
 
 
 def moments(place, mine, other, frames, phase, labels, predictions):
     width, (classes, rows) = phase.shape[0], predictions.shape
-    _, _, _, each, total = layout(width, classes)
+    each, _, ends = layout(width, classes)
     here = pl.BlockSpec(memory_space=pltpu.VMEM)
-    half = jax.ShapeDtypeStruct((total // 2, tile), f32)
+    half = jax.ShapeDtypeStruct((ends[-1], tile), f32)
     return pl.pallas_call(
         moment_kernel,
         out_shape=(jax.ShapeDtypeStruct((width, rows), bf16), half, half),
         in_specs=[pl.BlockSpec(memory_space=pltpu.SMEM)] + [here] * 6,
         out_specs=(here, pl.BlockSpec(memory_space=pl.ANY), pl.BlockSpec(memory_space=pl.ANY)),
         scratch_shapes=[
-            pltpu.VMEM((2, total // 2, tile), f32),
+            pltpu.VMEM((2, ends[-1], tile), f32),
             pltpu.VMEM((each, rows), f32),
-            pltpu.SemaphoreType.DMA((2,)),
+            pltpu.SemaphoreType.DMA((len(ends), 2)),
         ],
         compiler_params=pltpu.CompilerParams(vmem_limit_bytes=18 * 1024 * 1024),
         name="moments",
@@ -179,15 +202,15 @@
 ):
     width = turned.shape[0]
     classes = predictions.shape[0]
-    blocks, below, lower, each, total = layout(width, classes)
-    count = width // step
+    _, places, _ = layout(width, classes)
+    blocks, count = width // tile, width // step
     scale = 1.0 / total_rows
     padded = found.shape[0]
     core = place[0]
 
-    def sums(start, rows):
-        part, start = divmod(start, total // 2)
-        there = slice(start, start + rows)
+    def sums(name, rows, behind=0):
+        part, start = places[name]
+        there = slice(start + behind, start + behind + rows)
         return jnp.where(core == part, mine[there, :], other[there, :])
 
     def at(k):
@@ -195,14 +218,15 @@
 
     eye = functools.reduce(jnp.equal, coordinates(step)).astype(f32)
     at_row, at_lane = coordinates(tile)
-    for t, (a, b) in enumerate(pairs(blocks)):
-        part = sums(t * tile, tile) * scale
-        system[a * tile : (a + 1) * tile, b * tile : (b + 1) * tile] = part
-        system[b * tile : (b + 1) * tile, a * tile : (a + 1) * tile] = part.T
+    for a in range(blocks):
+        for b in range(a):
+            part = sums((a, b), tile) * scale
+            system[a * tile : (a + 1) * tile, b * tile : (b + 1) * tile] = part
+            system[b * tile : (b + 1) * tile, a * tile : (a + 1) * tile] = part.T
     for i in range(blocks // 2):
-        part = sums(below + i * tile, tile)
+        part = sums((2 * i, 2 * i), tile)
         other_way = part.T
-        diagonal = sums(lower + (2 * i + 1) * each + classes, 1)
+        diagonal = sums(("cross", 2 * i + 1), 1, classes)
         even = jnp.where(at_row >= at_lane, part, other_way)
         odd = jnp.where(at_row == at_lane, diagonal, jnp.where(at_row < at_lane, part, other_way))
         for a, part in ((2 * i, even), (2 * i + 1, odd)):
@@ -224,7 +248,7 @@
         old[tile:, lanes] = jnp.zeros((padded - tile, tile), f32)
         old[tile:classes, lanes] = rest
         valid = lax.broadcasted_iota(jnp.int32, (padded, tile), 0) < classes
-        system[width:, lanes] = jnp.where(valid, sums(lower + m * each, padded) * scale - old[:, lanes], 0.0)
+        system[width:, lanes] = jnp.where(valid, sums(("cross", m), padded) * scale - old[:, lanes], 0.0)
     parts = []
     for k in range(count):
         source = system if k == 0 else work
@@ -273,7 +297,7 @@
         found[:, at(k)] = part
 
     def refine(state):
-        short = system[width:, :] - exact_product(found[...], system[:width, :])
+        short = system[width:, :] - wide_product(found[...], system)
         moved, size = 0.0, 0.0
         for k, part in enumerate(apply([short[:, at(k)] for k in range(count)])):
             found[:, at(k)] += part
@@ -324,9 +348,8 @@
     for u in range(width // (2 * tile)):
         one, two = slice(u * tile, (u + 1) * tile), slice(width // 2 + u * tile, width // 2 + (u + 1) * tile)
         part = jnp.concatenate([found[:, one] + old[:, one], found[:, two] + old[:, two]], axis=1)
-        high, low = split(part)
-        last = (part - high.astype(f32) - low.astype(f32)).astype(bf16)
-        moved = (dot(high, order) + dot(low, order)) + dot(last, order)
+        high, low, last = (dot(piece, order) for piece in three(part))
+        moved = (high + low) + last
         coeffs[:, 2 * u * tile : 2 * (u + 1) * tile] = moved[:classes]
 
 
@@ -359,6 +382,24 @@
     )(place, mine, other, mine_old, other_old, turned, predictions)
 
 
+def total_kernel(shares, result):
+    used = shares.shape[1]
+    result[:used, :] = functools.reduce(jnp.add, [shares[n] for n in range(shares.shape[0])])
+    if used < result.shape[0]:
+        result[used:, :] = jnp.zeros((result.shape[0] - used, result.shape[1]), f32)
+
+
+def total(shares, rows):
+    here = pl.BlockSpec(memory_space=pltpu.VMEM)
+    return pl.pallas_call(
+        total_kernel,
+        out_shape=jax.ShapeDtypeStruct((rows, shares.shape[2]), f32),
+        in_specs=[here],
+        out_specs=here,
+        name="total",
+    )(shares)
+
+
 def exchange(x, axes):
     return lax.all_to_all(x, axes, 0, 0, tiled=True)
 
@@ -381,9 +422,15 @@
     first = lax.reduce_precision(coeffs_old, 8, 7)
     second = lax.reduce_precision(coeffs_old - first, 8, 7)
     olds = [part.astype(bf16) for part in (first, second, coeffs_old - first - second)]
-    ends = jnp.concatenate([freqs.T] + [part[:, tile:] for part in olds], axis=1)
-    ends = jnp.pad(ends, ((0, 0), (0, -ends.shape[1] % tile)))
-    sent = jnp.concatenate([ends] + [part[:, :tile] for part in olds], axis=1)
+    filled = -(-(depth + 3 * (classes - tile)) // tile) * tile
+    lanes = filled + 3 * tile
+
+    def put(x, start):
+        return jnp.pad(x, ((0, 0), (start, lanes - start - x.shape[1])))
+
+    sent = put(freqs.T, 0)
+    for i, part in enumerate(olds):
+        sent += put(part[:, tile:], depth + i * (classes - tile)) + put(part[:, :tile], filled + i * tile)
     mine_sent = gather(sent, "z").reshape(-1, sent.shape[1])
     mine_sent = gather(mine_sent, ("x", "y")).reshape(width // cores, sent.shape[1])
     other_sent = swap(mine_sent)
@@ -393,9 +440,8 @@
     )
     shares = lax.axis_size("z")
     sums = (keep + swap(send)).reshape(lax.axis_size(("x", "y")), -1, tile)
-    sums = exchange(sums, ("x", "y")).sum(0)
-    share = sums.shape[0]
-    sums = jnp.pad(sums, ((0, -share % (8 * shares)), (0, 0)))
+    share = sums.shape[1]
+    sums = total(exchange(sums, ("x", "y")), -(-share // (8 * shares)) * 8 * shares)
     sums = exchange(sums.reshape(shares, -1, tile), "z").sum(0)
     sums = gather(sums, "z").reshape(-1, tile)[:share]
     mine = gather(sums, ("x", "y")).reshape(-1, tile)

time: 147 us -> 150 us (1.020)
  Pallas kernels: 26.5 us -> 29.4 us
    pallas_call x0 -> x1, Pallas kernels: none -> 2.05 us  [total(): pl.pallas_call(total_kernel, out_shape=jax.ShapeDtypeStruct((rows, shares...]
    pallas_call x1, Pallas kernels: 5.13 us -> 6.66 us  [moments(): pl.pallas_call(moment_kernel, out_shape=(jax.ShapeDtypeStruct((width, row...]
where the time goes in v5:
time: 150 us; the launch traced here: 149 us
  blocking collectives  99.4 us (66%)
  Pallas kernels  29.4 us (20%)
  starting transfers between devices  8.91 us (6%)
  waiting for transfers between devices  7.18 us (5%)
  local copies, waits for them, and re-layouts  1.84 us (1%)
  other arithmetic  1.62 us (1%)
    all_to_all x6, blocking collectives, exchange(): return lax.all_to_all(x, axes, 0, 0, tiled=True)  99.4 us
    pallas_call x1, Pallas kernels, solve(): pl.pallas_call(functools.partial(solve_kernel, float(total_rows)), out_sh...  20.7 us
    ppermute x3, starting transfers between devices, swap(): return lax.ppermute(x, 'core', [(0, 1), (1, 0)])  8.91 us
    ppermute x3, waiting for transfers between devices, swap(): return lax.ppermute(x, 'core', [(0, 1), (1, 0)])  7.18 us
    pallas_call x1, Pallas kernels, moments(): pl.pallas_call(moment_kernel, out_shape=(jax.ShapeDtypeStruct((width, row...  6.66 us
  transfers between devices with their start and end apart: 3, of which 3 were waited for; matrix products, arithmetic and copies ran while one was open for 0% of the time, Pallas kernels for 0%

profile of v5, /device:TPU:1, one launch (start us, length us, event | category | flops | bytes accessed | tf_op | source)
XLA Modules:
  0.0 149.1 jit_solution(13565512262585617418)
XLA Ops:
  0.6 0.7 reduce-precision_convert_fusion.1
  1.4 0.8 add_add_fusion
  2.2 16.1 %all_to_all.30 = bf16[8,4,896]{2,1,0:T(4,128)(2,1)S(1)} all-to-all(bf16[8,4,896]{2,1,0:T(4,128)(2,1)S(1)} %broadcast_in_dim.34), channel_id=1, replica_groups=mesh['x'=4,'y'=4,'z'=8,'core'=2] {'z'}, dimensions={0} | all-to-all | bytes 114688 | tf_op jit(solution)/shard_map/all_to_all | solution.py:404
  18.2 0.0 copy-start.5
  18.2 0.1 broadcast_in_dim.36
  18.3 19.7 %all_to_all.31 = bf16[16,32,896]{2,1,0:T(8,128)(2,1)S(1)} all-to-all(bf16[16,32,896]{2,1,0:T(8,128)(2,1)S(1)} %broadcast_in_dim.36), channel_id=1, replica_groups=mesh['x'=4,'y'=4,'z'=8,'core'=2] {'x','y'}, dimensions={0} | all-to-all | bytes 1835008 | tf_op jit(solution)/shard_map/all_to_all | solution.py:404
  38.0 3.4 %collective-permute-start = (bf16[512,896]{1,0:T(8,128)(2,1)S(1)}, bf16[512,896]{1,0:T(8,128)(2,1)S(1)}, u32[]{:S(2)}, u32[]{:S(2)}) collective-permute-start(bf16[512,896]{1,0:T(8,128)(2,1)S(1)} %bitcast.13), channel_id=1, source_target_pairs={{0,1},{1,0},{2,3},{3,2},{4,5},{5,4},{6,7},{7,6},{8,9},{9,8},{10,11... | collective-permute-start | bytes 2752520 | tf_op jit(solution)/shard_map/ppermute | solution.py:412
  41.4 0.2 reshape.30
  41.7 0.2 reshape.35.phase
  41.9 1.7 %collective-permute-done.other.other_old = bf16[512,896]{1,0:T(8,128)(2,1)S(1)} collective-permute-done((bf16[512,896]{1,0:T(8,128)(2,1)S(1)}, bf16[512,896]{1,0:T(8,128)(2,1)S(1)}, u32[]{:S(2)}, u32[]{:S(2)}) %collective-permute-start) | collective-permute-done | bytes 917536 | tf_op jit(solution)/shard_map/ppermute | solution.py:412
  43.5 1.2 copy-done.3
  44.7 6.7 %moments.1 = (bf16[1024,1024]{1,0:T(8,128)(2,1)S(1)}, f32[2688,128]{1,0:T(8,128)S(1)}, f32[2688,128]{1,0:T(8,128)S(1)}) custom-call(s32[1]{0:T(128)} %bitcast.place, bf16[512,896]{1,0:T(8,128)(2,1)S(1)} %bitcast.14, bf16[512,896]{1,0:T(8,128)(2,1)S(1)} %collective-permute-done.other.other_old, bf16[440,1024]{1,0:T(8,128)(2,1)S(1)} %bitcast.20, ...), custom_call_target="tpu_custom_call" | custom-call | tf_op jit(solution)/shard_map/moments/pallas_call | solution.py:155
  51.4 0.5 collective-permute-start.1
  51.8 2.8 %collective-permute-done.1 = f32[2688,128]{1,0:T(8,128)S(1)} collective-permute-done((f32[2688,128]{1,0:T(8,128)S(1)}, f32[2688,128]{1,0:T(8,128)S(1)}, u32[]{:S(2)}, u32[]{:S(2)}) %collective-permute-start.1) | collective-permute-done | bytes 1376288 | tf_op jit(solution)/shard_map/ppermute | solution.py:412
  54.6 0.1 add.41
  54.7 22.7 %all_to_all.32.shares = f32[16,168,128]{2,1,0:T(8,128)} all-to-all(f32[16,168,128]{2,1,0:T(8,128)S(1)} %bitcast.22), channel_id=1, replica_groups=mesh['x'=4,'y'=4,'z'=8,'core'=2] {'x','y'}, dimensions={0} | all-to-all | bytes 2752512 | tf_op jit(solution)/shard_map/all_to_all | solution.py:404
  77.4 2.0 %total.1 = f32[192,128]{1,0:T(8,128)} custom-call(f32[16,168,128]{2,1,0:T(8,128)} %all_to_all.32.shares), custom_call_target="tpu_custom_call" | custom-call | tf_op jit(solution)/shard_map/total/pallas_call | solution.py:394
  79.5 10.9 %all_to_all.33 = f32[8,24,128]{2,1,0:T(8,128)S(1)} all-to-all(f32[8,24,128]{2,1,0:T(8,128)} %bitcast.24), channel_id=1, replica_groups=mesh['x'=4,'y'=4,'z'=8,'core'=2] {'z'}, dimensions={0} | all-to-all | bytes 196608 | tf_op jit(solution)/shard_map/all_to_all | solution.py:404
  90.5 10.1 %all_to_all.34 = f32[8,24,128]{2,1,0:T(8,128)S(1)} all-to-all(f32[8,24,128]{2,1,0:T(8,128)S(1)} %broadcast_in_dim.38), channel_id=1, replica_groups=mesh['x'=4,'y'=4,'z'=8,'core'=2] {'z'}, dimensions={0} | all-to-all | bytes 196608 | tf_op jit(solution)/shard_map/all_to_all | solution.py:404
  100.5 0.1 broadcast_in_dim.40
  100.6 20.0 %all_to_all.35 = f32[16,168,128]{2,1,0:T(8,128)S(1)} all-to-all(f32[16,168,128]{2,1,0:T(8,128)S(1)} %broadcast_in_dim.40), channel_id=1, replica_groups=mesh['x'=4,'y'=4,'z'=8,'core'=2] {'x','y'}, dimensions={0} | all-to-all | bytes 2752512 | tf_op jit(solution)/shard_map/all_to_all | solution.py:404
  120.6 5.0 %collective-permute-start.2 = (f32[2688,128]{1,0:T(8,128)S(1)}, f32[2688,128]{1,0:T(8,128)S(1)}, u32[]{:S(2)}, u32[]{:S(2)}) collective-permute-start(f32[2688,128]{1,0:T(8,128)S(1)} %bitcast.16), channel_id=1, source_target_pairs={{0,1},{1,0},{2,3},{3,2},{4,5},{5,4},{6,7},{7,6},{8,9},{9,8},{10,11... | collective-permute-start | bytes 4128776 | tf_op jit(solution)/shard_map/ppermute | solution.py:412
  125.6 2.8 %collective-permute-done.2.other = f32[2688,128]{1,0:T(8,128)S(1)} collective-permute-done((f32[2688,128]{1,0:T(8,128)S(1)}, f32[2688,128]{1,0:T(8,128)S(1)}, u32[]{:S(2)}, u32[]{:S(2)}) %collective-permute-start.2) | collective-permute-done | bytes 1376288 | tf_op jit(solution)/shard_map/ppermute | solution.py:412
  128.4 20.7 %solve.1 = (f32[147,1024]{1,0:T(8,128)}, f32[147,1024]{1,0:T(8,128)}) custom-call(s32[1]{0:T(128)} %bitcast.place, f32[2688,128]{1,0:T(8,128)S(1)} %bitcast.17, f32[2688,128]{1,0:T(8,128)S(1)} %collective-permute-done.2.other, bf16[512,896]{1,0:T(8,128)(2,1)S(1)} %bitcast.15, bf16[512,896]{1,0:T(8,128)(2,1)S(1)} %collective-permute-done.other.other_old, ...), custom_call_target="tpu_custom_call" | custom-call | tf_op jit(solution)/shard_map/solve/pallas_call | solution.py:360
  (22 shorter events, 0.1 us)
Async XLA Ops:
  18.2 23.2 %copy-start.5 = (f32[1024]{0:T(1024)S(1)}, f32[1024]{0:T(1024)}, u32[]{:S(2)}) copy-start(f32[1024]{0:T(1024)} %param.8) | copy-start | bytes 12292
  18.3 25.2 %copy-start = (f32[1024,147]{0,1:T(8,128)S(1)}, f32[1024,147]{0,1:T(8,128)}, u32[]{:S(2)}) copy-start(f32[1024,147]{0,1:T(8,128)} %param.10) | copy-start | bytes 1806340
  18.3 25.2 %copy-start.4 = (s32[1024]{0:T(1024)S(1)}, s32[1024]{0:T(1024)}, u32[]{:S(2)}) copy-start(s32[1024]{0:T(1024)} %param.9) | copy-start | bytes 12292
  38.0 5.5 %collective-permute-start = (bf16[512,896]{1,0:T(8,128)(2,1)S(1)}, bf16[512,896]{1,0:T(8,128)(2,1)S(1)}, u32[]{:S(2)}, u32[]{:S(2)}) collective-permute-start(bf16[512,896]{1,0:T(8,128)(2,1)S(1)} %bitcast.13), channel_id=1, source_target_pairs={{0,1},{1,0},{2,3},{3,2},{4,5},{5,4},{6,7},{7,6},{8,9},{9,8},{10,11... | collective-permute-start | bytes 2752520 | tf_op jit(solution)/shard_map/ppermute | solution.py:412
  43.5 1.2 copy-start.3
  51.4 3.4 %copy-start.1 = (bf16[1024,1024]{1,0:T(8,128)(2,1)}, bf16[1024,1024]{1,0:T(8,128)(2,1)S(1)}, u32[]{:S(2)}) copy-start(bf16[1024,1024]{1,0:T(8,128)(2,1)S(1)} %get-tuple-element.9.turned) | copy-start | bytes 6291460
  51.4 3.2 %collective-permute-start.1 = (f32[2688,128]{1,0:T(8,128)S(1)}, f32[2688,128]{1,0:T(8,128)S(1)}, u32[]{:S(2)}, u32[]{:S(2)}) collective-permute-start(f32[2688,128]{1,0:T(8,128)S(1)} %get-tuple-element.8), channel_id=1, source_target_pairs={{0,1},{1,0},{2,3},{3,2},{4,5},{5,4},{6,7},{7,6},{8,9},{9,8},{10,11... | collective-permute-start | bytes 4128776 | tf_op jit(solution)/shard_map/ppermute | solution.py:412
  100.6 27.8 %copy-start.2 = (bf16[1024,1024]{1,0:T(8,128)(2,1)S(1)}, bf16[1024,1024]{1,0:T(8,128)(2,1)}, u32[]{:S(2)}) copy-start(bf16[1024,1024]{1,0:T(8,128)(2,1)} %copy-done.1) | copy-start | bytes 6291460
  120.6 7.8 %collective-permute-start.2 = (f32[2688,128]{1,0:T(8,128)S(1)}, f32[2688,128]{1,0:T(8,128)S(1)}, u32[]{:S(2)}, u32[]{:S(2)}) collective-permute-start(f32[2688,128]{1,0:T(8,128)S(1)} %bitcast.16), channel_id=1, source_target_pairs={{0,1},{1,0},{2,3},{3,2},{4,5},{5,4},{6,7},{7,6},{8,9},{9,8},{10,11... | collective-permute-start | bytes 4128776 | tf_op jit(solution)/shard_map/ppermute | solution.py:412

commit v6 on v4

--- a/solution.py
+++ b/solution.py
@@ -50,11 +50,31 @@
 
 
 def product(a, b):
-    return dot(a[0], b[0]) + (dot(a[0], b[1]) + dot(a[1], b[0]))
+    rows = a[0].shape[0]
+    both = dot(jnp.concatenate(a, axis=0), b[0])
+    return both[:rows] + (both[rows:] + dot(a[0], b[1]))
 
 
 def exact_product(a, b):
     return lax.dot_general(a, b, NN, precision=lax.Precision.HIGHEST, preferred_element_type=f32)
+
+
+def three(x):
+    high, low = split(x)
+    return high, low, (x - high.astype(f32) - low.astype(f32)).astype(bf16)
+
+
+def wide_product(x, wide):
+    rows, depth = x.shape
+    parts = jnp.concatenate(three(x), axis=0)
+    result = []
+    for j in range(depth // step):
+        high, low, last = three(wide[:depth, j * step : (j + 1) * step])
+        one = dot(parts, high)
+        two = dot(parts[: 2 * rows], low)
+        small = one[2 * rows :] + two[rows:] + dot(parts[:rows], last)
+        result.append(one[:rows] + ((one[rows : 2 * rows] + two[:rows]) + small))
+    return jnp.concatenate(result, axis=1)
 
 
 def pairs(blocks):
@@ -74,14 +94,14 @@
 
 
 def moment_kernel(
-    place, mine, other, frames, phase, labels, predictions, turned, keep, send,
-    packed, residual, sems,
+    place, mine, other, frames, phase, labels, predictions, turned, packed, residual,
 ):
     width, (classes, rows) = phase.shape[0], predictions.shape
     depth = frames.shape[0]
     blocks, below, lower, each, total = layout(width, classes)
     half = total // 2
     core = place[0]
+    part_of = (core, 1 - core)
     at_row, at_lane = coordinates(tile)
     residual[...] = jnp.zeros_like(residual)
     onehot = labels[...] == lax.broadcasted_iota(jnp.int32, (classes, rows), 0)
@@ -102,49 +122,39 @@
         for j in range(step // tile):
             a = i * (step // tile) + j
             for b in range(a):
-                packed[row // half, row % half : row % half + tile, :] = gram[
+                packed[part_of[row // half], row % half : row % half + tile, :] = gram[
                     j * tile : (j + 1) * tile, b * tile : (b + 1) * tile
                 ]
                 row += tile
             start = lower + a * each - half
-            packed[1, start : start + each, :] = cross[:, j * tile : (j + 1) * tile]
+            packed[part_of[1], start : start + each, :] = cross[:, j * tile : (j + 1) * tile]
         even = gram[:tile, 2 * i * tile : (2 * i + 1) * tile]
         odd = gram[tile:, (2 * i + 1) * tile :]
         start = below + i * tile
-        packed[start // half, start % half : start % half + tile, :] = jnp.where(at_row >= at_lane, even, odd)
+        packed[part_of[start // half], start % half : start % half + tile, :] = jnp.where(at_row >= at_lane, even, odd)
         start = lower + (2 * i + 1) * each + classes - half
-        packed[1, start : start + 1, :] = jnp.sum(jnp.where(at_row == at_lane, odd, 0.0), axis=0, keepdims=True)
-    copies = [
-        pltpu.make_async_copy(packed.at[core], keep, sems.at[0]),
-        pltpu.make_async_copy(packed.at[1 - core], send, sems.at[1]),
-    ]
-    for copy in copies:
-        copy.start()
-    for copy in copies:
-        copy.wait()
+        packed[part_of[1], start : start + 1, :] = jnp.sum(jnp.where(at_row == at_lane, odd, 0.0), axis=0, keepdims=True)
 
 
 def moments(place, mine, other, frames, phase, labels, predictions):
     width, (classes, rows) = phase.shape[0], predictions.shape
     _, _, _, each, total = layout(width, classes)
     here = pl.BlockSpec(memory_space=pltpu.VMEM)
-    half = jax.ShapeDtypeStruct((total // 2, tile), f32)
     return pl.pallas_call(
         moment_kernel,
-        out_shape=(jax.ShapeDtypeStruct((width, rows), bf16), half, half),
+        out_shape=(
+            jax.ShapeDtypeStruct((width, rows), bf16),
+            jax.ShapeDtypeStruct((2, total // 2, tile), f32),
+        ),
         in_specs=[pl.BlockSpec(memory_space=pltpu.SMEM)] + [here] * 6,
-        out_specs=(here, pl.BlockSpec(memory_space=pl.ANY), pl.BlockSpec(memory_space=pl.ANY)),
-        scratch_shapes=[
-            pltpu.VMEM((2, total // 2, tile), f32),
-            pltpu.VMEM((each, rows), f32),
-            pltpu.SemaphoreType.DMA((2,)),
-        ],
-        compiler_params=pltpu.CompilerParams(vmem_limit_bytes=18 * 1024 * 1024),
+        out_specs=(here, here),
+        scratch_shapes=[pltpu.VMEM((each, rows), f32)],
+        compiler_params=pltpu.CompilerParams(vmem_limit_bytes=20 * 1024 * 1024),
         name="moments",
     )(place, mine, other, frames, phase, labels, predictions)
 
 
-def inverse(a, eye, bound, steps, loop=False):
+def inverse(a, eye, bound, steps, loop=False, correct=True):
     scale = 2.0 / (2.0 * ridge + bound)
 
     def advance(k, state):
@@ -169,6 +179,8 @@
         for k in range(1, steps):
             state = advance(k, state)
     x = state[0]
+    if not correct:
+        return x
     missing = eye - product(split(a), split(x))
     return x + product(split(x), split(missing))
 
@@ -230,15 +242,15 @@
         source = system if k == 0 else work
         block = source[at(k), at(k)]
 
-        def invert(bound, steps, loop=False):
-            inv_h[at(k), :], inv_l[at(k), :] = split(inverse(block, eye, bound, steps, loop))
+        def invert(bound, steps, **options):
+            inv_h[at(k), :], inv_l[at(k), :] = split(inverse(block, eye, bound, steps, **options))
 
         if k == 0:
             invert(2.0 * step, 7)
         else:
             small = jnp.max(jnp.sum(jnp.abs(block - ridge * eye), axis=0)) <= 6.0
-            pl.when(small)(functools.partial(invert, 6.0, 3))
-            pl.when(jnp.logical_not(small))(functools.partial(invert, 2.0 * step, 7, True))
+            pl.when(small)(functools.partial(invert, 6.0, 4, correct=False))
+            pl.when(jnp.logical_not(small))(functools.partial(invert, 2.0 * step, 7, loop=True))
         x = inv_h[at(k), :], inv_l[at(k), :]
         column = product(split(source[(k + 1) * step :, at(k)]), x)
         parts.append(column[-padded:])
@@ -273,7 +285,7 @@
         found[:, at(k)] = part
 
     def refine(state):
-        short = system[width:, :] - exact_product(found[...], system[:width, :])
+        short = system[width:, :] - wide_product(found[...], system)
         moved, size = 0.0, 0.0
         for k, part in enumerate(apply([short[:, at(k)] for k in range(count)])):
             found[:, at(k)] += part
@@ -324,9 +336,8 @@
     for u in range(width // (2 * tile)):
         one, two = slice(u * tile, (u + 1) * tile), slice(width // 2 + u * tile, width // 2 + (u + 1) * tile)
         part = jnp.concatenate([found[:, one] + old[:, one], found[:, two] + old[:, two]], axis=1)
-        high, low = split(part)
-        last = (part - high.astype(f32) - low.astype(f32)).astype(bf16)
-        moved = (dot(high, order) + dot(low, order)) + dot(last, order)
+        high, low, last = (dot(piece, order) for piece in three(part))
+        moved = (high + low) + last
         coeffs[:, 2 * u * tile : 2 * (u + 1) * tile] = moved[:classes]
 
 
@@ -381,18 +392,24 @@
     first = lax.reduce_precision(coeffs_old, 8, 7)
     second = lax.reduce_precision(coeffs_old - first, 8, 7)
     olds = [part.astype(bf16) for part in (first, second, coeffs_old - first - second)]
-    ends = jnp.concatenate([freqs.T] + [part[:, tile:] for part in olds], axis=1)
-    ends = jnp.pad(ends, ((0, 0), (0, -ends.shape[1] % tile)))
-    sent = jnp.concatenate([ends] + [part[:, :tile] for part in olds], axis=1)
+    filled = -(-(depth + 3 * (classes - tile)) // tile) * tile
+    lanes = filled + 3 * tile
+
+    def put(x, start):
+        return jnp.pad(x, ((0, 0), (start, lanes - start - x.shape[1])))
+
+    sent = put(freqs.T, 0)
+    for i, part in enumerate(olds):
+        sent += put(part[:, tile:], depth + i * (classes - tile)) + put(part[:, :tile], filled + i * tile)
     mine_sent = gather(sent, "z").reshape(-1, sent.shape[1])
     mine_sent = gather(mine_sent, ("x", "y")).reshape(width // cores, sent.shape[1])
     other_sent = swap(mine_sent)
     phase = phase.reshape(devices // cores, cores, own).swapaxes(0, 1).reshape(width, 1)
-    turned, keep, send = moments(
+    turned, packed = moments(
         place, mine_sent, other_sent, frames.T, phase, labels[None, :], predictions.T
     )
     shares = lax.axis_size("z")
-    sums = (keep + swap(send)).reshape(lax.axis_size(("x", "y")), -1, tile)
+    sums = (packed[0] + swap(packed[1])).reshape(lax.axis_size(("x", "y")), -1, tile)
     sums = exchange(sums, ("x", "y")).sum(0)
     share = sums.shape[0]
     sums = jnp.pad(sums, ((0, -share % (8 * shares)), (0, 0)))

time: 147 us -> 146 us (level)
  Pallas kernels: 26.5 us -> 24.6 us
    pallas_call x1, Pallas kernels: 21.3 us -> 19.8 us  [solve(): pl.pallas_call(functools.partial(solve_kernel, float(total_rows)), out_sh...]
where the time goes in v6:
time: 146 us
  blocking collectives  98.5 us (67%)
  Pallas kernels  24.6 us (17%)
  starting transfers between devices  8.83 us (6%)
  waiting for transfers between devices  7.18 us (5%)
  local copies, waits for them, and re-layouts  3.19 us (2%)
  other arithmetic  3.03 us (2%)
    all_to_all x6, blocking collectives, exchange(): return lax.all_to_all(x, axes, 0, 0, tiled=True)  98.5 us
    pallas_call x1, Pallas kernels, solve(): pl.pallas_call(functools.partial(solve_kernel, float(total_rows)), out_sh...  19.8 us
    ppermute x3, starting transfers between devices, swap(): return lax.ppermute(x, 'core', [(0, 1), (1, 0)])  8.83 us
    ppermute x3, waiting for transfers between devices, swap(): return lax.ppermute(x, 'core', [(0, 1), (1, 0)])  7.18 us
    pallas_call x1, Pallas kernels, moments(): pl.pallas_call(moment_kernel, out_shape=(jax.ShapeDtypeStruct((width, row...  4.8 us
  transfers between devices with their start and end apart: 3, of which 3 were waited for; matrix products, arithmetic and copies ran while one was open for 0% of the time, Pallas kernels for 0%

profile of v6, /device:TPU:1, one launch (start us, length us, event | category | flops | bytes accessed | tf_op | source)
XLA Modules:
  0.0 146.0 jit_solution(12646394809020733461)
XLA Ops:
  0.6 0.7 reduce-precision_convert_fusion.1
  1.4 0.8 add_add_fusion
  2.2 16.1 %all_to_all.30 = bf16[8,4,896]{2,1,0:T(4,128)(2,1)S(1)} all-to-all(bf16[8,4,896]{2,1,0:T(4,128)(2,1)S(1)} %broadcast_in_dim.34), channel_id=1, replica_groups=mesh['x'=4,'y'=4,'z'=8,'core'=2] {'z'}, dimensions={0} | all-to-all | bytes 114688 | tf_op jit(solution)/shard_map/all_to_all | solution.py:374
  18.3 19.7 %all_to_all.31 = bf16[16,32,896]{2,1,0:T(8,128)(2,1)S(1)} all-to-all(bf16[16,32,896]{2,1,0:T(8,128)(2,1)S(1)} %broadcast_in_dim.36), channel_id=1, replica_groups=mesh['x'=4,'y'=4,'z'=8,'core'=2] {'x','y'}, dimensions={0} | all-to-all | bytes 1835008 | tf_op jit(solution)/shard_map/all_to_all | solution.py:374
  38.0 3.4 %collective-permute-start = (bf16[512,896]{1,0:T(8,128)(2,1)S(1)}, bf16[512,896]{1,0:T(8,128)(2,1)S(1)}, u32[]{:S(2)}, u32[]{:S(2)}) collective-permute-start(bf16[512,896]{1,0:T(8,128)(2,1)S(1)} %bitcast.17), channel_id=1, source_target_pairs={{0,1},{1,0},{2,3},{3,2},{4,5},{5,4},{6,7},{7,6},{8,9},{9,8},{10,11... | collective-permute-start | bytes 2752520 | tf_op jit(solution)/shard_map/ppermute | solution.py:382
  41.4 0.2 reshape.30
  41.7 0.2 reshape.35.phase
  41.9 1.7 %collective-permute-done.other.other_old = bf16[512,896]{1,0:T(8,128)(2,1)S(1)} collective-permute-done((bf16[512,896]{1,0:T(8,128)(2,1)S(1)}, bf16[512,896]{1,0:T(8,128)(2,1)S(1)}, u32[]{:S(2)}, u32[]{:S(2)}) %collective-permute-start) | collective-permute-done | bytes 917536 | tf_op jit(solution)/shard_map/ppermute | solution.py:382
  43.5 1.2 copy-done.3
  44.7 4.8 %moments.1 = (bf16[1024,1024]{1,0:T(8,128)(2,1)S(1)}, f32[2,2688,128]{2,1,0:T(8,128)S(1)}) custom-call(s32[1]{0:T(128)} %bitcast.place, bf16[512,896]{1,0:T(8,128)(2,1)S(1)} %bitcast.18, bf16[512,896]{1,0:T(8,128)(2,1)S(1)} %collective-permute-done.other.other_old, bf16[440,1024]{1,0:T(8,128)(2,1)S(1)} %bitcast.24, f32[1024,1]{1,0:T(8,128)S(1)} %reshape.35.phase, ...), custom_call_target="tpu_custom_call" | custom-call | tf_op jit(solution)/shard_map/moments/pallas_call | solution.py:143
  49.5 0.1 slice_bitcast_fusion
  49.6 1.2 copy-done.1
  50.9 0.4 collective-permute-start.1
  51.2 2.8 %collective-permute-done.1 = f32[2688,128]{1,0:T(8,128)S(1)} collective-permute-done((f32[2688,128]{1,0:T(8,128)S(1)}, f32[2688,128]{1,0:T(8,128)S(1)}, u32[]{:S(2)}, u32[]{:S(2)}) %collective-permute-start.1) | collective-permute-done | bytes 1376288 | tf_op jit(solution)/shard_map/ppermute | solution.py:382
  54.0 0.1 bitcast_add_fusion
  54.1 22.7 %all_to_all.32 = f32[16,168,128]{2,1,0:T(8,128)} all-to-all(f32[16,168,128]{2,1,0:T(8,128)S(1)} %bitcast.26), channel_id=1, replica_groups=mesh['x'=4,'y'=4,'z'=8,'core'=2] {'x','y'}, dimensions={0} | all-to-all | bytes 2752512 | tf_op jit(solution)/shard_map/all_to_all | solution.py:374
  76.9 1.4 reduce_sum.18
  78.3 10.1 %all_to_all.33 = f32[8,24,128]{2,1,0:T(8,128)S(1)} all-to-all(f32[8,24,128]{2,1,0:T(8,128)S(1)} %bitcast.28), channel_id=1, replica_groups=mesh['x'=4,'y'=4,'z'=8,'core'=2] {'z'}, dimensions={0} | all-to-all | bytes 196608 | tf_op jit(solution)/shard_map/all_to_all | solution.py:374
  88.4 10.1 %all_to_all.34 = f32[8,24,128]{2,1,0:T(8,128)S(1)} all-to-all(f32[8,24,128]{2,1,0:T(8,128)S(1)} %broadcast_in_dim.38), channel_id=1, replica_groups=mesh['x'=4,'y'=4,'z'=8,'core'=2] {'z'}, dimensions={0} | all-to-all | bytes 196608 | tf_op jit(solution)/shard_map/all_to_all | solution.py:374
  98.4 0.1 broadcast_in_dim.40
  98.5 19.9 %all_to_all.35 = f32[16,168,128]{2,1,0:T(8,128)S(1)} all-to-all(f32[16,168,128]{2,1,0:T(8,128)S(1)} %broadcast_in_dim.40), channel_id=1, replica_groups=mesh['x'=4,'y'=4,'z'=8,'core'=2] {'x','y'}, dimensions={0} | all-to-all | bytes 2752512 | tf_op jit(solution)/shard_map/all_to_all | solution.py:374
  118.5 5.0 %collective-permute-start.2 = (f32[2688,128]{1,0:T(8,128)S(1)}, f32[2688,128]{1,0:T(8,128)S(1)}, u32[]{:S(2)}, u32[]{:S(2)}) collective-permute-start(f32[2688,128]{1,0:T(8,128)S(1)} %bitcast.20), channel_id=1, source_target_pairs={{0,1},{1,0},{2,3},{3,2},{4,5},{5,4},{6,7},{7,6},{8,9},{9,8},{10,11... | collective-permute-start | bytes 4128776 | tf_op jit(solution)/shard_map/ppermute | solution.py:382
  123.5 2.8 %collective-permute-done.2.other = f32[2688,128]{1,0:T(8,128)S(1)} collective-permute-done((f32[2688,128]{1,0:T(8,128)S(1)}, f32[2688,128]{1,0:T(8,128)S(1)}, u32[]{:S(2)}, u32[]{:S(2)}) %collective-permute-start.2) | collective-permute-done | bytes 1376288 | tf_op jit(solution)/shard_map/ppermute | solution.py:382
  126.3 19.8 %solve.1 = (f32[147,1024]{1,0:T(8,128)}, f32[147,1024]{1,0:T(8,128)}) custom-call(s32[1]{0:T(128)} %bitcast.place, f32[2688,128]{1,0:T(8,128)S(1)} %bitcast.21, f32[2688,128]{1,0:T(8,128)S(1)} %collective-permute-done.2.other, bf16[512,896]{1,0:T(8,128)(2,1)S(1)} %bitcast.19, bf16[512,896]{1,0:T(8,128)(2,1)S(1)} %collective-permute-done.other.other_old, ...), custom_call_target="tpu_custom_call" | custom-call | tf_op jit(solution)/shard_map/solve/pallas_call | solution.py:348
  (24 shorter events, 0.2 us)
Async XLA Ops:
  18.2 23.2 %copy-start.5 = (f32[1024]{0:T(1024)S(1)}, f32[1024]{0:T(1024)}, u32[]{:S(2)}) copy-start(f32[1024]{0:T(1024)} %param.8) | copy-start | bytes 12292
  18.3 25.2 %copy-start = (f32[1024,147]{0,1:T(8,128)S(1)}, f32[1024,147]{0,1:T(8,128)}, u32[]{:S(2)}) copy-start(f32[1024,147]{0,1:T(8,128)} %param.10) | copy-start | bytes 1806340
  18.3 25.2 %copy-start.4 = (s32[1024]{0:T(1024)S(1)}, s32[1024]{0:T(1024)}, u32[]{:S(2)}) copy-start(s32[1024]{0:T(1024)} %param.9) | copy-start | bytes 12292
  38.0 5.5 %collective-permute-start = (bf16[512,896]{1,0:T(8,128)(2,1)S(1)}, bf16[512,896]{1,0:T(8,128)(2,1)S(1)}, u32[]{:S(2)}, u32[]{:S(2)}) collective-permute-start(bf16[512,896]{1,0:T(8,128)(2,1)S(1)} %bitcast.17), channel_id=1, source_target_pairs={{0,1},{1,0},{2,3},{3,2},{4,5},{5,4},{6,7},{7,6},{8,9},{9,8},{10,11... | collective-permute-start | bytes 2752520 | tf_op jit(solution)/shard_map/ppermute | solution.py:382
  43.5 1.2 copy-start.3
  49.5 1.4 copy-start.1
  50.9 3.1 %collective-permute-start.1 = (f32[2688,128]{1,0:T(8,128)S(1)}, f32[2688,128]{1,0:T(8,128)S(1)}, u32[]{:S(2)}, u32[]{:S(2)}) collective-permute-start(f32[2688,128]{1,0:T(8,128)S(1)} %slice_bitcast_fusion), channel_id=1, source_target_pairs={{0,1},{1,0},{2,3},{3,2},{4,5},{5,4},{6,7},{7,6},{8,9},{9,8},{10,11... | collective-permute-start | bytes 4128776 | tf_op jit(solution)/shard_map/ppermute | solution.py:382
  98.5 27.7 %copy-start.2 = (bf16[1024,1024]{1,0:T(8,128)(2,1)S(1)}, bf16[1024,1024]{1,0:T(8,128)(2,1)}, u32[]{:S(2)}) copy-start(bf16[1024,1024]{1,0:T(8,128)(2,1)} %copy-done.1) | copy-start | bytes 6291460
  118.5 7.8 %collective-permute-start.2 = (f32[2688,128]{1,0:T(8,128)S(1)}, f32[2688,128]{1,0:T(8,128)S(1)}, u32[]{:S(2)}, u32[]{:S(2)}) collective-permute-start(f32[2688,128]{1,0:T(8,128)S(1)} %bitcast.20), channel_id=1, source_target_pairs={{0,1},{1,0},{2,3},{3,2},{4,5},{5,4},{6,7},{7,6},{8,9},{9,8},{10,11... | collective-permute-start | bytes 4128776 | tf_op jit(solution)/shard_map/ppermute | solution.py:382

commit v7 on v6

--- a/solution.py
+++ b/solution.py
@@ -94,14 +94,14 @@
 
 
 def moment_kernel(
-    place, mine, other, frames, phase, labels, predictions, turned, packed, residual,
+    place, mine, other, frames, phase, labels, predictions, turned, keep, send,
+    packed, residual, sems,
 ):
     width, (classes, rows) = phase.shape[0], predictions.shape
     depth = frames.shape[0]
     blocks, below, lower, each, total = layout(width, classes)
     half = total // 2
     core = place[0]
-    part_of = (core, 1 - core)
     at_row, at_lane = coordinates(tile)
     residual[...] = jnp.zeros_like(residual)
     onehot = labels[...] == lax.broadcasted_iota(jnp.int32, (classes, rows), 0)
@@ -122,34 +122,44 @@
         for j in range(step // tile):
             a = i * (step // tile) + j
             for b in range(a):
-                packed[part_of[row // half], row % half : row % half + tile, :] = gram[
+                packed[row // half, row % half : row % half + tile, :] = gram[
                     j * tile : (j + 1) * tile, b * tile : (b + 1) * tile
                 ]
                 row += tile
             start = lower + a * each - half
-            packed[part_of[1], start : start + each, :] = cross[:, j * tile : (j + 1) * tile]
+            packed[1, start : start + each, :] = cross[:, j * tile : (j + 1) * tile]
         even = gram[:tile, 2 * i * tile : (2 * i + 1) * tile]
         odd = gram[tile:, (2 * i + 1) * tile :]
         start = below + i * tile
-        packed[part_of[start // half], start % half : start % half + tile, :] = jnp.where(at_row >= at_lane, even, odd)
+        packed[start // half, start % half : start % half + tile, :] = jnp.where(at_row >= at_lane, even, odd)
         start = lower + (2 * i + 1) * each + classes - half
-        packed[part_of[1], start : start + 1, :] = jnp.sum(jnp.where(at_row == at_lane, odd, 0.0), axis=0, keepdims=True)
+        packed[1, start : start + 1, :] = jnp.sum(jnp.where(at_row == at_lane, odd, 0.0), axis=0, keepdims=True)
+    copies = [
+        pltpu.make_async_copy(packed.at[core], keep, sems.at[0]),
+        pltpu.make_async_copy(packed.at[1 - core], send, sems.at[1]),
+    ]
+    for copy in copies:
+        copy.start()
+    for copy in copies:
+        copy.wait()
 
 
 def moments(place, mine, other, frames, phase, labels, predictions):
     width, (classes, rows) = phase.shape[0], predictions.shape
     _, _, _, each, total = layout(width, classes)
     here = pl.BlockSpec(memory_space=pltpu.VMEM)
+    half = jax.ShapeDtypeStruct((total // 2, tile), f32)
     return pl.pallas_call(
         moment_kernel,
-        out_shape=(
-            jax.ShapeDtypeStruct((width, rows), bf16),
-            jax.ShapeDtypeStruct((2, total // 2, tile), f32),
-        ),
+        out_shape=(jax.ShapeDtypeStruct((width, rows), bf16), half, half),
         in_specs=[pl.BlockSpec(memory_space=pltpu.SMEM)] + [here] * 6,
-        out_specs=(here, here),
-        scratch_shapes=[pltpu.VMEM((each, rows), f32)],
-        compiler_params=pltpu.CompilerParams(vmem_limit_bytes=20 * 1024 * 1024),
+        out_specs=(here, pl.BlockSpec(memory_space=pl.ANY), pl.BlockSpec(memory_space=pl.ANY)),
+        scratch_shapes=[
+            pltpu.VMEM((2, total // 2, tile), f32),
+            pltpu.VMEM((each, rows), f32),
+            pltpu.SemaphoreType.DMA((2,)),
+        ],
+        compiler_params=pltpu.CompilerParams(vmem_limit_bytes=18 * 1024 * 1024),
         name="moments",
     )(place, mine, other, frames, phase, labels, predictions)
 
@@ -405,11 +415,11 @@
     mine_sent = gather(mine_sent, ("x", "y")).reshape(width // cores, sent.shape[1])
     other_sent = swap(mine_sent)
     phase = phase.reshape(devices // cores, cores, own).swapaxes(0, 1).reshape(width, 1)
-    turned, packed = moments(
+    turned, keep, send = moments(
         place, mine_sent, other_sent, frames.T, phase, labels[None, :], predictions.T
     )
     shares = lax.axis_size("z")
-    sums = (packed[0] + swap(packed[1])).reshape(lax.axis_size(("x", "y")), -1, tile)
+    sums = (keep + swap(send)).reshape(lax.axis_size(("x", "y")), -1, tile)
     sums = exchange(sums, ("x", "y")).sum(0)
     share = sums.shape[0]
     sums = jnp.pad(sums, ((0, -share % (8 * shares)), (0, 0)))

time: 146 us -> 146 us (level)
  no operation moved by 1% of the time
where the time goes in v7:
time: 146 us; the launch traced here: 145 us
  blocking collectives  98.5 us (67%)
  Pallas kernels  24.9 us (17%)
  starting transfers between devices  8.91 us (6%)
  waiting for transfers between devices  7.17 us (5%)
  other arithmetic  3.03 us (2%)
  local copies, waits for them, and re-layouts  1.85 us (1%)
    all_to_all x6, blocking collectives, exchange(): return lax.all_to_all(x, axes, 0, 0, tiled=True)  98.5 us
    pallas_call x1, Pallas kernels, solve(): pl.pallas_call(functools.partial(solve_kernel, float(total_rows)), out_sh...  19.8 us
    ppermute x3, starting transfers between devices, swap(): return lax.ppermute(x, 'core', [(0, 1), (1, 0)])  8.91 us
    ppermute x3, waiting for transfers between devices, swap(): return lax.ppermute(x, 'core', [(0, 1), (1, 0)])  7.17 us
    pallas_call x1, Pallas kernels, moments(): pl.pallas_call(moment_kernel, out_shape=(jax.ShapeDtypeStruct((width, row...  5.13 us
  transfers between devices with their start and end apart: 3, of which 3 were waited for; matrix products, arithmetic and copies ran while one was open for 0% of the time, Pallas kernels for 0%

profile of v7, /device:TPU:1, one launch (start us, length us, event | category | flops | bytes accessed | tf_op | source)
XLA Modules:
  0.0 145.1 jit_solution(17339984131790124052)
XLA Ops:
  0.6 0.7 reduce-precision_convert_fusion.1
  1.4 0.8 add_add_fusion
  2.2 16.1 %all_to_all.30 = bf16[8,4,896]{2,1,0:T(4,128)(2,1)S(1)} all-to-all(bf16[8,4,896]{2,1,0:T(4,128)(2,1)S(1)} %broadcast_in_dim.34), channel_id=1, replica_groups=mesh['x'=4,'y'=4,'z'=8,'core'=2] {'z'}, dimensions={0} | all-to-all | bytes 114688 | tf_op jit(solution)/shard_map/all_to_all | solution.py:384
  18.2 0.0 copy-start.5
  18.2 0.1 broadcast_in_dim.36
  18.3 19.7 %all_to_all.31 = bf16[16,32,896]{2,1,0:T(8,128)(2,1)S(1)} all-to-all(bf16[16,32,896]{2,1,0:T(8,128)(2,1)S(1)} %broadcast_in_dim.36), channel_id=1, replica_groups=mesh['x'=4,'y'=4,'z'=8,'core'=2] {'x','y'}, dimensions={0} | all-to-all | bytes 1835008 | tf_op jit(solution)/shard_map/all_to_all | solution.py:384
  38.0 3.4 %collective-permute-start = (bf16[512,896]{1,0:T(8,128)(2,1)S(1)}, bf16[512,896]{1,0:T(8,128)(2,1)S(1)}, u32[]{:S(2)}, u32[]{:S(2)}) collective-permute-start(bf16[512,896]{1,0:T(8,128)(2,1)S(1)} %bitcast.13), channel_id=1, source_target_pairs={{0,1},{1,0},{2,3},{3,2},{4,5},{5,4},{6,7},{7,6},{8,9},{9,8},{10,11... | collective-permute-start | bytes 2752520 | tf_op jit(solution)/shard_map/ppermute | solution.py:392
  41.4 0.2 reshape.30
  41.7 0.2 reshape.35.phase
  41.9 1.7 %collective-permute-done.other.other_old = bf16[512,896]{1,0:T(8,128)(2,1)S(1)} collective-permute-done((bf16[512,896]{1,0:T(8,128)(2,1)S(1)}, bf16[512,896]{1,0:T(8,128)(2,1)S(1)}, u32[]{:S(2)}, u32[]{:S(2)}) %collective-permute-start) | collective-permute-done | bytes 917536 | tf_op jit(solution)/shard_map/ppermute | solution.py:392
  43.5 1.2 copy-done.3
  44.7 5.1 %moments.1 = (bf16[1024,1024]{1,0:T(8,128)(2,1)S(1)}, f32[2688,128]{1,0:T(8,128)S(1)}, f32[2688,128]{1,0:T(8,128)S(1)}) custom-call(s32[1]{0:T(128)} %bitcast.place, bf16[512,896]{1,0:T(8,128)(2,1)S(1)} %bitcast.14, bf16[512,896]{1,0:T(8,128)(2,1)S(1)} %collective-permute-done.other.other_old, bf16[440,1024]{1,0:T(8,128)(2,1)S(1)} %bitcast.20, ...), custom_call_target="tpu_custom_call" | custom-call | tf_op jit(solution)/shard_map/moments/pallas_call | solution.py:152
  49.8 0.5 collective-permute-start.1
  50.3 2.8 %collective-permute-done.1 = f32[2688,128]{1,0:T(8,128)S(1)} collective-permute-done((f32[2688,128]{1,0:T(8,128)S(1)}, f32[2688,128]{1,0:T(8,128)S(1)}, u32[]{:S(2)}, u32[]{:S(2)}) %collective-permute-start.1) | collective-permute-done | bytes 1376288 | tf_op jit(solution)/shard_map/ppermute | solution.py:392
  53.1 0.1 add.43
  53.2 22.7 %all_to_all.32 = f32[16,168,128]{2,1,0:T(8,128)} all-to-all(f32[16,168,128]{2,1,0:T(8,128)S(1)} %bitcast.22), channel_id=1, replica_groups=mesh['x'=4,'y'=4,'z'=8,'core'=2] {'x','y'}, dimensions={0} | all-to-all | bytes 2752512 | tf_op jit(solution)/shard_map/all_to_all | solution.py:384
  75.9 1.4 reduce_sum.18
  77.4 10.1 %all_to_all.33 = f32[8,24,128]{2,1,0:T(8,128)S(1)} all-to-all(f32[8,24,128]{2,1,0:T(8,128)S(1)} %bitcast.24), channel_id=1, replica_groups=mesh['x'=4,'y'=4,'z'=8,'core'=2] {'z'}, dimensions={0} | all-to-all | bytes 196608 | tf_op jit(solution)/shard_map/all_to_all | solution.py:384
  87.4 10.1 %all_to_all.34 = f32[8,24,128]{2,1,0:T(8,128)S(1)} all-to-all(f32[8,24,128]{2,1,0:T(8,128)S(1)} %broadcast_in_dim.38), channel_id=1, replica_groups=mesh['x'=4,'y'=4,'z'=8,'core'=2] {'z'}, dimensions={0} | all-to-all | bytes 196608 | tf_op jit(solution)/shard_map/all_to_all | solution.py:384
  97.5 0.1 broadcast_in_dim.40
  97.6 20.0 %all_to_all.35 = f32[16,168,128]{2,1,0:T(8,128)S(1)} all-to-all(f32[16,168,128]{2,1,0:T(8,128)S(1)} %broadcast_in_dim.40), channel_id=1, replica_groups=mesh['x'=4,'y'=4,'z'=8,'core'=2] {'x','y'}, dimensions={0} | all-to-all | bytes 2752512 | tf_op jit(solution)/shard_map/all_to_all | solution.py:384
  117.6 5.0 %collective-permute-start.2 = (f32[2688,128]{1,0:T(8,128)S(1)}, f32[2688,128]{1,0:T(8,128)S(1)}, u32[]{:S(2)}, u32[]{:S(2)}) collective-permute-start(f32[2688,128]{1,0:T(8,128)S(1)} %bitcast.16), channel_id=1, source_target_pairs={{0,1},{1,0},{2,3},{3,2},{4,5},{5,4},{6,7},{7,6},{8,9},{9,8},{10,11... | collective-permute-start | bytes 4128776 | tf_op jit(solution)/shard_map/ppermute | solution.py:392
  122.6 2.8 %collective-permute-done.2.other = f32[2688,128]{1,0:T(8,128)S(1)} collective-permute-done((f32[2688,128]{1,0:T(8,128)S(1)}, f32[2688,128]{1,0:T(8,128)S(1)}, u32[]{:S(2)}, u32[]{:S(2)}) %collective-permute-start.2) | collective-permute-done | bytes 1376288 | tf_op jit(solution)/shard_map/ppermute | solution.py:392
  125.4 19.8 %solve.1 = (f32[147,1024]{1,0:T(8,128)}, f32[147,1024]{1,0:T(8,128)}) custom-call(s32[1]{0:T(128)} %bitcast.place, f32[2688,128]{1,0:T(8,128)S(1)} %bitcast.17, f32[2688,128]{1,0:T(8,128)S(1)} %collective-permute-done.2.other, bf16[512,896]{1,0:T(8,128)(2,1)S(1)} %bitcast.15, bf16[512,896]{1,0:T(8,128)(2,1)S(1)} %collective-permute-done.other.other_old, ...), custom_call_target="tpu_custom_call" | custom-call | tf_op jit(solution)/shard_map/solve/pallas_call | solution.py:358
  (23 shorter events, 0.1 us)
Async XLA Ops:
  18.2 23.2 %copy-start.5 = (f32[1024]{0:T(1024)S(1)}, f32[1024]{0:T(1024)}, u32[]{:S(2)}) copy-start(f32[1024]{0:T(1024)} %param.8) | copy-start | bytes 12292
  18.3 25.2 %copy-start = (f32[1024,147]{0,1:T(8,128)S(1)}, f32[1024,147]{0,1:T(8,128)}, u32[]{:S(2)}) copy-start(f32[1024,147]{0,1:T(8,128)} %param.10) | copy-start | bytes 1806340
  18.3 25.2 %copy-start.4 = (s32[1024]{0:T(1024)S(1)}, s32[1024]{0:T(1024)}, u32[]{:S(2)}) copy-start(s32[1024]{0:T(1024)} %param.9) | copy-start | bytes 12292
  38.0 5.5 %collective-permute-start = (bf16[512,896]{1,0:T(8,128)(2,1)S(1)}, bf16[512,896]{1,0:T(8,128)(2,1)S(1)}, u32[]{:S(2)}, u32[]{:S(2)}) collective-permute-start(bf16[512,896]{1,0:T(8,128)(2,1)S(1)} %bitcast.13), channel_id=1, source_target_pairs={{0,1},{1,0},{2,3},{3,2},{4,5},{5,4},{6,7},{7,6},{8,9},{9,8},{10,11... | collective-permute-start | bytes 2752520 | tf_op jit(solution)/shard_map/ppermute | solution.py:392
  43.5 1.2 copy-start.3
  49.8 3.4 %copy-start.1 = (bf16[1024,1024]{1,0:T(8,128)(2,1)}, bf16[1024,1024]{1,0:T(8,128)(2,1)S(1)}, u32[]{:S(2)}) copy-start(bf16[1024,1024]{1,0:T(8,128)(2,1)S(1)} %get-tuple-element.9.turned) | copy-start | bytes 6291460
  49.8 3.2 %collective-permute-start.1 = (f32[2688,128]{1,0:T(8,128)S(1)}, f32[2688,128]{1,0:T(8,128)S(1)}, u32[]{:S(2)}, u32[]{:S(2)}) collective-permute-start(f32[2688,128]{1,0:T(8,128)S(1)} %get-tuple-element.8), channel_id=1, source_target_pairs={{0,1},{1,0},{2,3},{3,2},{4,5},{5,4},{6,7},{7,6},{8,9},{9,8},{10,11... | collective-permute-start | bytes 4128776 | tf_op jit(solution)/shard_map/ppermute | solution.py:392
  97.6 27.8 %copy-start.2 = (bf16[1024,1024]{1,0:T(8,128)(2,1)S(1)}, bf16[1024,1024]{1,0:T(8,128)(2,1)}, u32[]{:S(2)}) copy-start(bf16[1024,1024]{1,0:T(8,128)(2,1)} %copy-done.1) | copy-start | bytes 6291460
  117.6 7.8 %collective-permute-start.2 = (f32[2688,128]{1,0:T(8,128)S(1)}, f32[2688,128]{1,0:T(8,128)S(1)}, u32[]{:S(2)}, u32[]{:S(2)}) collective-permute-start(f32[2688,128]{1,0:T(8,128)S(1)} %bitcast.16), channel_id=1, source_target_pairs={{0,1},{1,0},{2,3},{3,2},{4,5},{5,4},{6,7},{7,6},{8,9},{9,8},{10,11... | collective-permute-start | bytes 4128776 | tf_op jit(solution)/shard_map/ppermute | solution.py:392

commit v8 on v7

--- a/solution.py
+++ b/solution.py
@@ -94,11 +94,12 @@
 
 
 def moment_kernel(
-    place, mine, other, frames, phase, labels, predictions, turned, keep, send,
+    place, mine, other, frames, labels, predictions, turned, keep, send,
     packed, residual, sems,
 ):
-    width, (classes, rows) = phase.shape[0], predictions.shape
+    width, (classes, rows) = turned.shape[0], predictions.shape
     depth = frames.shape[0]
+    spare = classes + 1 - tile
     blocks, below, lower, each, total = layout(width, classes)
     half = total // 2
     core = place[0]
@@ -113,8 +114,11 @@
         first = (i * step) % (width // 2)
         side = core == (i * step) // (width // 2)
         there = slice(first, first + step)
-        freqs = jnp.where(side, mine[there, :depth], other[there, :depth])
-        angles = dot(freqs, frames[...]) + phase[here, :]
+        freqs = jnp.where(side, mine[there, : 4 * tile], other[there, : 4 * tile])
+        phase = 0.0
+        for n in range(1, 4):
+            phase = phase + freqs[:, depth + n * spare - 1 : depth + n * spare].astype(f32)
+        angles = dot(freqs[:, :depth], frames[...]) + phase
         block = features_of(angles)
         turned[here, :] = block
         gram = dot(block, turned[: (i + 1) * step, :], NT)
@@ -144,15 +148,15 @@
         copy.wait()
 
 
-def moments(place, mine, other, frames, phase, labels, predictions):
-    width, (classes, rows) = phase.shape[0], predictions.shape
+def moments(place, mine, other, frames, labels, predictions):
+    width, (classes, rows) = 2 * mine.shape[0], predictions.shape
     _, _, _, each, total = layout(width, classes)
     here = pl.BlockSpec(memory_space=pltpu.VMEM)
     half = jax.ShapeDtypeStruct((total // 2, tile), f32)
     return pl.pallas_call(
         moment_kernel,
         out_shape=(jax.ShapeDtypeStruct((width, rows), bf16), half, half),
-        in_specs=[pl.BlockSpec(memory_space=pltpu.SMEM)] + [here] * 6,
+        in_specs=[pl.BlockSpec(memory_space=pltpu.SMEM)] + [here] * 5,
         out_specs=(here, pl.BlockSpec(memory_space=pl.ANY), pl.BlockSpec(memory_space=pl.ANY)),
         scratch_shapes=[
             pltpu.VMEM((2, total // 2, tile), f32),
@@ -161,7 +165,7 @@
         ],
         compiler_params=pltpu.CompilerParams(vmem_limit_bytes=18 * 1024 * 1024),
         name="moments",
-    )(place, mine, other, frames, phase, labels, predictions)
+    )(place, mine, other, frames, labels, predictions)
 
 
 def inverse(a, eye, bound, steps, loop=False, correct=True):
@@ -237,11 +241,11 @@
         main, rest = 0.0, 0.0
         ends = jnp.where(side, mine_old[there, 3 * tile : 4 * tile], other_old[there, 3 * tile : 4 * tile])
         ends = ends.astype(f32).T
-        first = depth_of % tile
+        first, spare = depth_of % tile, classes + 1 - tile
         for i in range(3):
             lane = slice((4 + i) * tile, (5 + i) * tile)
             main = main + jnp.where(side, mine_old[there, lane], other_old[there, lane]).astype(f32)
-            rest = rest + ends[first + i * (classes - tile) : first + (i + 1) * (classes - tile)]
+            rest = rest + ends[first + i * spare : first + i * spare + classes - tile]
         old[:tile, lanes] = main.T
         old[tile:, lanes] = jnp.zeros((padded - tile, tile), f32)
         old[tile:classes, lanes] = rest
@@ -399,10 +403,14 @@
     cores = lax.axis_size("core")
     devices = width // own
     place = lax.axis_index("core").astype(jnp.int32)[None]
-    first = lax.reduce_precision(coeffs_old, 8, 7)
-    second = lax.reduce_precision(coeffs_old - first, 8, 7)
-    olds = [part.astype(bf16) for part in (first, second, coeffs_old - first - second)]
-    filled = -(-(depth + 3 * (classes - tile)) // tile) * tile
+    device = lax.axis_index(("x", "y", "z", "core"))
+    phase = lax.dynamic_slice_in_dim(phase, device * own, own)
+    held = jnp.concatenate([coeffs_old, phase[:, None]], axis=1)
+    spare = classes + 1 - tile
+    first = lax.reduce_precision(held, 8, 7)
+    second = lax.reduce_precision(held - first, 8, 7)
+    olds = [part.astype(bf16) for part in (first, second, held - first - second)]
+    filled = -(-(depth + 3 * spare) // tile) * tile
     lanes = filled + 3 * tile
 
     def put(x, start):
@@ -410,13 +418,12 @@
 
     sent = put(freqs.T, 0)
     for i, part in enumerate(olds):
-        sent += put(part[:, tile:], depth + i * (classes - tile)) + put(part[:, :tile], filled + i * tile)
+        sent += put(part[:, tile:], depth + i * spare) + put(part[:, :tile], filled + i * tile)
     mine_sent = gather(sent, "z").reshape(-1, sent.shape[1])
     mine_sent = gather(mine_sent, ("x", "y")).reshape(width // cores, sent.shape[1])
     other_sent = swap(mine_sent)
-    phase = phase.reshape(devices // cores, cores, own).swapaxes(0, 1).reshape(width, 1)
     turned, keep, send = moments(
-        place, mine_sent, other_sent, frames.T, phase, labels[None, :], predictions.T
+        place, mine_sent, other_sent, frames.T, labels[None, :], predictions.T
     )
     shares = lax.axis_size("z")
     sums = (keep + swap(send)).reshape(lax.axis_size(("x", "y")), -1, tile)

time: 146 us -> 146 us (level)
  no operation moved by 1% of the time
where the time goes in v8:
time: 146 us; the launch traced here: 145 us
  blocking collectives  98.5 us (67%)
  Pallas kernels  25.1 us (17%)
  starting transfers between devices  8.92 us (6%)
  waiting for transfers between devices  7.61 us (5%)
  other arithmetic  3.11 us (2%)
    all_to_all x6, blocking collectives, exchange(): return lax.all_to_all(x, axes, 0, 0, tiled=True)  98.5 us
    pallas_call x1, Pallas kernels, solve(): pl.pallas_call(functools.partial(solve_kernel, float(total_rows)), out_sh...  19.9 us
    ppermute x3, starting transfers between devices, swap(): return lax.ppermute(x, 'core', [(0, 1), (1, 0)])  8.92 us
    ppermute x3, waiting for transfers between devices, swap(): return lax.ppermute(x, 'core', [(0, 1), (1, 0)])  7.61 us
    pallas_call x1, Pallas kernels, moments(): pl.pallas_call(moment_kernel, out_shape=(jax.ShapeDtypeStruct((width, row...  5.2 us
  transfers between devices with their start and end apart: 3, of which 3 were waited for; matrix products, arithmetic and copies ran while one was open for 0% of the time, Pallas kernels for 0%

profile of v8, /device:TPU:1, one launch (start us, length us, event | category | flops | bytes accessed | tf_op | source)
XLA Modules:
  0.0 145.1 jit_solution(18067310378811993067)
XLA Ops:
  0.6 0.0 copy-start
  0.7 0.7 copy-done
  1.3 0.1 dynamic-slice_bitcast_fusion
  1.4 0.1 copy.9
  1.5 0.8 reduce-precision_convert_fusion.1
  2.3 0.8 add_add_fusion
  3.1 16.1 %all_to_all.30 = bf16[8,4,896]{2,1,0:T(4,128)(2,1)S(1)} all-to-all(bf16[8,4,896]{2,1,0:T(4,128)(2,1)S(1)} %broadcast_in_dim.38), channel_id=1, replica_groups=mesh['x'=4,'y'=4,'z'=8,'core'=2] {'z'}, dimensions={0} | all-to-all | bytes 114688 | tf_op jit(solution)/shard_map/all_to_all | solution.py:388
  19.2 0.1 broadcast_in_dim.40
  19.3 19.7 %all_to_all.31 = bf16[16,32,896]{2,1,0:T(8,128)(2,1)S(1)} all-to-all(bf16[16,32,896]{2,1,0:T(8,128)(2,1)S(1)} %broadcast_in_dim.40), channel_id=1, replica_groups=mesh['x'=4,'y'=4,'z'=8,'core'=2] {'x','y'}, dimensions={0} | all-to-all | bytes 1835008 | tf_op jit(solution)/shard_map/all_to_all | solution.py:388
  38.9 3.4 %collective-permute-start = (bf16[512,896]{1,0:T(8,128)(2,1)S(1)}, bf16[512,896]{1,0:T(8,128)(2,1)S(1)}, u32[]{:S(2)}, u32[]{:S(2)}) collective-permute-start(bf16[512,896]{1,0:T(8,128)(2,1)S(1)} %bitcast.14), channel_id=1, source_target_pairs={{0,1},{1,0},{2,3},{3,2},{4,5},{5,4},{6,7},{7,6},{8,9},{9,8},{10,11... | collective-permute-start | bytes 2752520 | tf_op jit(solution)/shard_map/ppermute | solution.py:396
  42.4 2.1 %collective-permute-done.other.other_old = bf16[512,896]{1,0:T(8,128)(2,1)S(1)} collective-permute-done((bf16[512,896]{1,0:T(8,128)(2,1)S(1)}, bf16[512,896]{1,0:T(8,128)(2,1)S(1)}, u32[]{:S(2)}, u32[]{:S(2)}) %collective-permute-start) | collective-permute-done | bytes 917536 | tf_op jit(solution)/shard_map/ppermute | solution.py:396
  44.5 5.2 %moments.1 = (bf16[1024,1024]{1,0:T(8,128)(2,1)S(1)}, f32[2688,128]{1,0:T(8,128)S(1)}, f32[2688,128]{1,0:T(8,128)S(1)}) custom-call(s32[1]{0:T(128)} %bitcast.place, bf16[512,896]{1,0:T(8,128)(2,1)S(1)} %bitcast.15, bf16[512,896]{1,0:T(8,128)(2,1)S(1)} %collective-permute-done.other.other_old, bf16[440,1024]{1,0:T(8,128)(2,1)S(1)} %bitcast.21, ...), custom_call_target="tpu_custom_call" | custom-call | tf_op jit(solution)/shard_map/moments/pallas_call | solution.py:156
  49.7 0.5 collective-permute-start.1
  50.1 2.8 %collective-permute-done.1 = f32[2688,128]{1,0:T(8,128)S(1)} collective-permute-done((f32[2688,128]{1,0:T(8,128)S(1)}, f32[2688,128]{1,0:T(8,128)S(1)}, u32[]{:S(2)}, u32[]{:S(2)}) %collective-permute-start.1) | collective-permute-done | bytes 1376288 | tf_op jit(solution)/shard_map/ppermute | solution.py:396
  52.9 0.1 add.59
  53.1 22.7 %all_to_all.32 = f32[16,168,128]{2,1,0:T(8,128)} all-to-all(f32[16,168,128]{2,1,0:T(8,128)S(1)} %bitcast.23), channel_id=1, replica_groups=mesh['x'=4,'y'=4,'z'=8,'core'=2] {'x','y'}, dimensions={0} | all-to-all | bytes 2752512 | tf_op jit(solution)/shard_map/all_to_all | solution.py:388
  75.8 1.4 reduce_sum.18
  77.2 10.1 %all_to_all.33 = f32[8,24,128]{2,1,0:T(8,128)S(1)} all-to-all(f32[8,24,128]{2,1,0:T(8,128)S(1)} %bitcast.24), channel_id=1, replica_groups=mesh['x'=4,'y'=4,'z'=8,'core'=2] {'z'}, dimensions={0} | all-to-all | bytes 196608 | tf_op jit(solution)/shard_map/all_to_all | solution.py:388
  87.3 10.1 %all_to_all.34 = f32[8,24,128]{2,1,0:T(8,128)S(1)} all-to-all(f32[8,24,128]{2,1,0:T(8,128)S(1)} %broadcast_in_dim.42), channel_id=1, replica_groups=mesh['x'=4,'y'=4,'z'=8,'core'=2] {'z'}, dimensions={0} | all-to-all | bytes 196608 | tf_op jit(solution)/shard_map/all_to_all | solution.py:388
  97.4 0.1 broadcast_in_dim.44
  97.5 19.9 %all_to_all.35 = f32[16,168,128]{2,1,0:T(8,128)S(1)} all-to-all(f32[16,168,128]{2,1,0:T(8,128)S(1)} %broadcast_in_dim.44), channel_id=1, replica_groups=mesh['x'=4,'y'=4,'z'=8,'core'=2] {'x','y'}, dimensions={0} | all-to-all | bytes 2752512 | tf_op jit(solution)/shard_map/all_to_all | solution.py:388
  117.4 5.0 %collective-permute-start.2 = (f32[2688,128]{1,0:T(8,128)S(1)}, f32[2688,128]{1,0:T(8,128)S(1)}, u32[]{:S(2)}, u32[]{:S(2)}) collective-permute-start(f32[2688,128]{1,0:T(8,128)S(1)} %bitcast.17), channel_id=1, source_target_pairs={{0,1},{1,0},{2,3},{3,2},{4,5},{5,4},{6,7},{7,6},{8,9},{9,8},{10,11... | collective-permute-start | bytes 4128776 | tf_op jit(solution)/shard_map/ppermute | solution.py:396
  122.4 2.8 %collective-permute-done.2.other = f32[2688,128]{1,0:T(8,128)S(1)} collective-permute-done((f32[2688,128]{1,0:T(8,128)S(1)}, f32[2688,128]{1,0:T(8,128)S(1)}, u32[]{:S(2)}, u32[]{:S(2)}) %collective-permute-start.2) | collective-permute-done | bytes 1376288 | tf_op jit(solution)/shard_map/ppermute | solution.py:396
  125.2 19.9 %solve.1 = (f32[147,1024]{1,0:T(8,128)}, f32[147,1024]{1,0:T(8,128)}) custom-call(s32[1]{0:T(128)} %bitcast.place, f32[2688,128]{1,0:T(8,128)S(1)} %bitcast.18, f32[2688,128]{1,0:T(8,128)S(1)} %collective-permute-done.2.other, bf16[512,896]{1,0:T(8,128)(2,1)S(1)} %bitcast.16, bf16[512,896]{1,0:T(8,128)(2,1)S(1)} %collective-permute-done.other.other_old, ...), custom_call_target="tpu_custom_call" | custom-call | tf_op jit(solution)/shard_map/solve/pallas_call | solution.py:362
  (22 shorter events, 0.1 us)
Async XLA Ops:
  0.6 0.7 copy-start
  19.2 25.3 %copy-start.1 = (f32[1024,147]{0,1:T(8,128)S(1)}, f32[1024,147]{0,1:T(8,128)}, u32[]{:S(2)}) copy-start(f32[1024,147]{0,1:T(8,128)} %param.10) | copy-start | bytes 1806340
  19.2 25.3 %copy-start.4 = (bf16[1024,440]{0,1:T(8,128)(2,1)S(1)}, bf16[1024,440]{0,1:T(8,128)(2,1)}, u32[]{:S(2)}) copy-start(bf16[1024,440]{0,1:T(8,128)(2,1)} %param.6) | copy-start | bytes 2703364
  19.2 25.3 %copy-start.5 = (s32[1024]{0:T(1024)S(1)}, s32[1024]{0:T(1024)}, u32[]{:S(2)}) copy-start(s32[1024]{0:T(1024)} %param.9) | copy-start | bytes 12292
  38.9 5.5 %collective-permute-start = (bf16[512,896]{1,0:T(8,128)(2,1)S(1)}, bf16[512,896]{1,0:T(8,128)(2,1)S(1)}, u32[]{:S(2)}, u32[]{:S(2)}) collective-permute-start(bf16[512,896]{1,0:T(8,128)(2,1)S(1)} %bitcast.14), channel_id=1, source_target_pairs={{0,1},{1,0},{2,3},{3,2},{4,5},{5,4},{6,7},{7,6},{8,9},{9,8},{10,11... | collective-permute-start | bytes 2752520 | tf_op jit(solution)/shard_map/ppermute | solution.py:396
  49.7 3.4 %copy-start.2 = (bf16[1024,1024]{1,0:T(8,128)(2,1)}, bf16[1024,1024]{1,0:T(8,128)(2,1)S(1)}, u32[]{:S(2)}) copy-start(bf16[1024,1024]{1,0:T(8,128)(2,1)S(1)} %get-tuple-element.9.turned) | copy-start | bytes 6291460
  49.7 3.2 %collective-permute-start.1 = (f32[2688,128]{1,0:T(8,128)S(1)}, f32[2688,128]{1,0:T(8,128)S(1)}, u32[]{:S(2)}, u32[]{:S(2)}) collective-permute-start(f32[2688,128]{1,0:T(8,128)S(1)} %get-tuple-element.8), channel_id=1, source_target_pairs={{0,1},{1,0},{2,3},{3,2},{4,5},{5,4},{6,7},{7,6},{8,9},{9,8},{10,11... | collective-permute-start | bytes 4128776 | tf_op jit(solution)/shard_map/ppermute | solution.py:396
  97.4 27.7 %copy-start.3 = (bf16[1024,1024]{1,0:T(8,128)(2,1)S(1)}, bf16[1024,1024]{1,0:T(8,128)(2,1)}, u32[]{:S(2)}) copy-start(bf16[1024,1024]{1,0:T(8,128)(2,1)} %copy-done.2) | copy-start | bytes 6291460
  117.4 7.8 %collective-permute-start.2 = (f32[2688,128]{1,0:T(8,128)S(1)}, f32[2688,128]{1,0:T(8,128)S(1)}, u32[]{:S(2)}, u32[]{:S(2)}) collective-permute-start(f32[2688,128]{1,0:T(8,128)S(1)} %bitcast.17), channel_id=1, source_target_pairs={{0,1},{1,0},{2,3},{3,2},{4,5},{5,4},{6,7},{7,6},{8,9},{9,8},{10,11... | collective-permute-start | bytes 4128776 | tf_op jit(solution)/shard_map/ppermute | solution.py:396

commit v9 on v7

--- a/solution.py
+++ b/solution.py
@@ -97,7 +97,7 @@
     place, mine, other, frames, phase, labels, predictions, turned, keep, send,
     packed, residual, sems,
 ):
-    width, (classes, rows) = phase.shape[0], predictions.shape
+    width, (classes, rows) = turned.shape[0], predictions.shape
     depth = frames.shape[0]
     blocks, below, lower, each, total = layout(width, classes)
     half = total // 2
@@ -114,7 +114,11 @@
         side = core == (i * step) // (width // 2)
         there = slice(first, first + step)
         freqs = jnp.where(side, mine[there, :depth], other[there, :depth])
-        angles = dot(freqs, frames[...]) + phase[here, :]
+        item = lax.broadcasted_iota(jnp.int32, (step, 2 * step), 0)
+        goal = item // own_width * (2 * own_width) + i * step // (width // 2) * own_width + item % own_width
+        chosen = goal == lax.broadcasted_iota(jnp.int32, (step, 2 * step), 1)
+        shift = jnp.sum(jnp.where(chosen, phase[:, 2 * first : 2 * (first + step)], 0.0), axis=1, keepdims=True)
+        angles = dot(freqs, frames[...]) + shift
         block = features_of(angles)
         turned[here, :] = block
         gram = dot(block, turned[: (i + 1) * step, :], NT)
@@ -145,7 +149,7 @@
 
 
 def moments(place, mine, other, frames, phase, labels, predictions):
-    width, (classes, rows) = phase.shape[0], predictions.shape
+    width, (classes, rows) = phase.shape[1], predictions.shape
     _, _, _, each, total = layout(width, classes)
     here = pl.BlockSpec(memory_space=pltpu.VMEM)
     half = jax.ShapeDtypeStruct((total // 2, tile), f32)
@@ -414,9 +418,8 @@
     mine_sent = gather(sent, "z").reshape(-1, sent.shape[1])
     mine_sent = gather(mine_sent, ("x", "y")).reshape(width // cores, sent.shape[1])
     other_sent = swap(mine_sent)
-    phase = phase.reshape(devices // cores, cores, own).swapaxes(0, 1).reshape(width, 1)
     turned, keep, send = moments(
-        place, mine_sent, other_sent, frames.T, phase, labels[None, :], predictions.T
+        place, mine_sent, other_sent, frames.T, phase[None, :], labels[None, :], predictions.T
     )
     shares = lax.axis_size("z")
     sums = (keep + swap(send)).reshape(lax.axis_size(("x", "y")), -1, tile)

time: 146 us -> 144 us (0.986)
  local copies, waits for them, and re-layouts: 1.85 us -> 0.27 us
where the time goes in v9:
time: 144 us
  blocking collectives  98.5 us (68%)
  Pallas kernels  24.9 us (17%)
  starting transfers between devices  8.92 us (6%)
  waiting for transfers between devices  7.61 us (5%)
  other arithmetic  3.03 us (2%)
    all_to_all x6, blocking collectives, exchange(): return lax.all_to_all(x, axes, 0, 0, tiled=True)  98.5 us
    pallas_call x1, Pallas kernels, solve(): pl.pallas_call(functools.partial(solve_kernel, float(total_rows)), out_sh...  19.7 us
    ppermute x3, starting transfers between devices, swap(): return lax.ppermute(x, 'core', [(0, 1), (1, 0)])  8.92 us
    ppermute x3, waiting for transfers between devices, swap(): return lax.ppermute(x, 'core', [(0, 1), (1, 0)])  7.61 us
    pallas_call x1, Pallas kernels, moments(): pl.pallas_call(moment_kernel, out_shape=(jax.ShapeDtypeStruct((width, row...  5.2 us
  transfers between devices with their start and end apart: 3, of which 3 were waited for; matrix products, arithmetic and copies ran while one was open for 0% of the time, Pallas kernels for 0%

profile of v9, /device:TPU:1, one launch (start us, length us, event | category | flops | bytes accessed | tf_op | source)
XLA Modules:
  0.0 144.0 jit_solution(232349159403719723)
XLA Ops:
  0.6 0.7 reduce-precision_convert_fusion.1
  1.4 0.8 add_add_fusion
  2.2 16.1 %all_to_all.30 = bf16[8,4,896]{2,1,0:T(4,128)(2,1)S(1)} all-to-all(bf16[8,4,896]{2,1,0:T(4,128)(2,1)S(1)} %broadcast_in_dim.37), channel_id=1, replica_groups=mesh['x'=4,'y'=4,'z'=8,'core'=2] {'z'}, dimensions={0} | all-to-all | bytes 114688 | tf_op jit(solution)/shard_map/all_to_all | solution.py:388
  18.2 0.0 copy-start
  18.2 0.0 copy-start.3
  18.3 0.0 copy-start.4
  18.3 0.0 copy-start.5
  18.3 0.1 broadcast_in_dim.39
  18.4 19.7 %all_to_all.31 = bf16[16,32,896]{2,1,0:T(8,128)(2,1)S(1)} all-to-all(bf16[16,32,896]{2,1,0:T(8,128)(2,1)S(1)} %broadcast_in_dim.39), channel_id=1, replica_groups=mesh['x'=4,'y'=4,'z'=8,'core'=2] {'x','y'}, dimensions={0} | all-to-all | bytes 1835008 | tf_op jit(solution)/shard_map/all_to_all | solution.py:388
  38.0 3.4 %collective-permute-start = (bf16[512,896]{1,0:T(8,128)(2,1)S(1)}, bf16[512,896]{1,0:T(8,128)(2,1)S(1)}, u32[]{:S(2)}, u32[]{:S(2)}) collective-permute-start(bf16[512,896]{1,0:T(8,128)(2,1)S(1)} %bitcast.13), channel_id=1, source_target_pairs={{0,1},{1,0},{2,3},{3,2},{4,5},{5,4},{6,7},{7,6},{8,9},{9,8},{10,11... | collective-permute-start | bytes 2752520 | tf_op jit(solution)/shard_map/ppermute | solution.py:396
  41.4 2.1 %collective-permute-done.other.other_old = bf16[512,896]{1,0:T(8,128)(2,1)S(1)} collective-permute-done((bf16[512,896]{1,0:T(8,128)(2,1)S(1)}, bf16[512,896]{1,0:T(8,128)(2,1)S(1)}, u32[]{:S(2)}, u32[]{:S(2)}) %collective-permute-start) | collective-permute-done | bytes 917536 | tf_op jit(solution)/shard_map/ppermute | solution.py:396
  43.5 5.2 %moments.1 = (bf16[1024,1024]{1,0:T(8,128)(2,1)S(1)}, f32[2688,128]{1,0:T(8,128)S(1)}, f32[2688,128]{1,0:T(8,128)S(1)}) custom-call(s32[1]{0:T(128)} %bitcast.place, bf16[512,896]{1,0:T(8,128)(2,1)S(1)} %bitcast.14, bf16[512,896]{1,0:T(8,128)(2,1)S(1)} %collective-permute-done.other.other_old, bf16[440,1024]{1,0:T(8,128)(2,1)S(1)} %bitcast.20, ...), custom_call_target="tpu_custom_call" | custom-call | tf_op jit(solution)/shard_map/moments/pallas_call | solution.py:156
  48.8 0.5 collective-permute-start.1
  49.2 2.8 %collective-permute-done.1 = f32[2688,128]{1,0:T(8,128)S(1)} collective-permute-done((f32[2688,128]{1,0:T(8,128)S(1)}, f32[2688,128]{1,0:T(8,128)S(1)}, u32[]{:S(2)}, u32[]{:S(2)}) %collective-permute-start.1) | collective-permute-done | bytes 1376288 | tf_op jit(solution)/shard_map/ppermute | solution.py:396
  52.0 0.1 add.43
  52.1 22.7 %all_to_all.32 = f32[16,168,128]{2,1,0:T(8,128)} all-to-all(f32[16,168,128]{2,1,0:T(8,128)S(1)} %bitcast.23), channel_id=1, replica_groups=mesh['x'=4,'y'=4,'z'=8,'core'=2] {'x','y'}, dimensions={0} | all-to-all | bytes 2752512 | tf_op jit(solution)/shard_map/all_to_all | solution.py:388
  74.9 1.4 reduce_sum.18
  76.3 10.1 %all_to_all.33 = f32[8,24,128]{2,1,0:T(8,128)S(1)} all-to-all(f32[8,24,128]{2,1,0:T(8,128)S(1)} %bitcast.24), channel_id=1, replica_groups=mesh['x'=4,'y'=4,'z'=8,'core'=2] {'z'}, dimensions={0} | all-to-all | bytes 196608 | tf_op jit(solution)/shard_map/all_to_all | solution.py:388
  86.4 10.1 %all_to_all.34 = f32[8,24,128]{2,1,0:T(8,128)S(1)} all-to-all(f32[8,24,128]{2,1,0:T(8,128)S(1)} %broadcast_in_dim.42), channel_id=1, replica_groups=mesh['x'=4,'y'=4,'z'=8,'core'=2] {'z'}, dimensions={0} | all-to-all | bytes 196608 | tf_op jit(solution)/shard_map/all_to_all | solution.py:388
  96.4 0.1 broadcast_in_dim.44
  96.6 19.9 %all_to_all.35 = f32[16,168,128]{2,1,0:T(8,128)S(1)} all-to-all(f32[16,168,128]{2,1,0:T(8,128)S(1)} %broadcast_in_dim.44), channel_id=1, replica_groups=mesh['x'=4,'y'=4,'z'=8,'core'=2] {'x','y'}, dimensions={0} | all-to-all | bytes 2752512 | tf_op jit(solution)/shard_map/all_to_all | solution.py:388
  116.5 5.0 %collective-permute-start.2 = (f32[2688,128]{1,0:T(8,128)S(1)}, f32[2688,128]{1,0:T(8,128)S(1)}, u32[]{:S(2)}, u32[]{:S(2)}) collective-permute-start(f32[2688,128]{1,0:T(8,128)S(1)} %bitcast.16), channel_id=1, source_target_pairs={{0,1},{1,0},{2,3},{3,2},{4,5},{5,4},{6,7},{7,6},{8,9},{9,8},{10,11... | collective-permute-start | bytes 4128776 | tf_op jit(solution)/shard_map/ppermute | solution.py:396
  121.5 2.8 %collective-permute-done.2.other = f32[2688,128]{1,0:T(8,128)S(1)} collective-permute-done((f32[2688,128]{1,0:T(8,128)S(1)}, f32[2688,128]{1,0:T(8,128)S(1)}, u32[]{:S(2)}, u32[]{:S(2)}) %collective-permute-start.2) | collective-permute-done | bytes 1376288 | tf_op jit(solution)/shard_map/ppermute | solution.py:396
  124.3 19.7 %solve.1 = (f32[147,1024]{1,0:T(8,128)}, f32[147,1024]{1,0:T(8,128)}) custom-call(s32[1]{0:T(128)} %bitcast.place, f32[2688,128]{1,0:T(8,128)S(1)} %bitcast.17, f32[2688,128]{1,0:T(8,128)S(1)} %collective-permute-done.2.other, bf16[512,896]{1,0:T(8,128)(2,1)S(1)} %bitcast.15, bf16[512,896]{1,0:T(8,128)(2,1)S(1)} %collective-permute-done.other.other_old, ...), custom_call_target="tpu_custom_call" | custom-call | tf_op jit(solution)/shard_map/solve/pallas_call | solution.py:362
  (20 shorter events, 0.1 us)
Async XLA Ops:
  18.2 25.3 %copy-start = (f32[1024,147]{0,1:T(8,128)S(1)}, f32[1024,147]{0,1:T(8,128)}, u32[]{:S(2)}) copy-start(f32[1024,147]{0,1:T(8,128)} %param.10) | copy-start | bytes 1806340
  18.2 25.3 %copy-start.3 = (bf16[1024,440]{0,1:T(8,128)(2,1)S(1)}, bf16[1024,440]{0,1:T(8,128)(2,1)}, u32[]{:S(2)}) copy-start(bf16[1024,440]{0,1:T(8,128)(2,1)} %param.6) | copy-start | bytes 2703364
  18.3 25.3 %copy-start.4 = (f32[1024]{0:T(1024)S(1)}, f32[1024]{0:T(1024)}, u32[]{:S(2)}) copy-start(f32[1024]{0:T(1024)} %param.8) | copy-start | bytes 12292
  18.3 25.3 %copy-start.5 = (s32[1024]{0:T(1024)S(1)}, s32[1024]{0:T(1024)}, u32[]{:S(2)}) copy-start(s32[1024]{0:T(1024)} %param.9) | copy-start | bytes 12292
  38.0 5.5 %collective-permute-start = (bf16[512,896]{1,0:T(8,128)(2,1)S(1)}, bf16[512,896]{1,0:T(8,128)(2,1)S(1)}, u32[]{:S(2)}, u32[]{:S(2)}) collective-permute-start(bf16[512,896]{1,0:T(8,128)(2,1)S(1)} %bitcast.13), channel_id=1, source_target_pairs={{0,1},{1,0},{2,3},{3,2},{4,5},{5,4},{6,7},{7,6},{8,9},{9,8},{10,11... | collective-permute-start | bytes 2752520 | tf_op jit(solution)/shard_map/ppermute | solution.py:396
  48.8 3.4 %copy-start.1 = (bf16[1024,1024]{1,0:T(8,128)(2,1)}, bf16[1024,1024]{1,0:T(8,128)(2,1)S(1)}, u32[]{:S(2)}) copy-start(bf16[1024,1024]{1,0:T(8,128)(2,1)S(1)} %get-tuple-element.9.turned) | copy-start | bytes 6291460
  48.8 3.2 %collective-permute-start.1 = (f32[2688,128]{1,0:T(8,128)S(1)}, f32[2688,128]{1,0:T(8,128)S(1)}, u32[]{:S(2)}, u32[]{:S(2)}) collective-permute-start(f32[2688,128]{1,0:T(8,128)S(1)} %get-tuple-element.8), channel_id=1, source_target_pairs={{0,1},{1,0},{2,3},{3,2},{4,5},{5,4},{6,7},{7,6},{8,9},{9,8},{10,11... | collective-permute-start | bytes 4128776 | tf_op jit(solution)/shard_map/ppermute | solution.py:396
  96.5 27.7 %copy-start.2 = (bf16[1024,1024]{1,0:T(8,128)(2,1)S(1)}, bf16[1024,1024]{1,0:T(8,128)(2,1)}, u32[]{:S(2)}) copy-start(bf16[1024,1024]{1,0:T(8,128)(2,1)} %copy-done.1) | copy-start | bytes 6291460
  116.5 7.8 %collective-permute-start.2 = (f32[2688,128]{1,0:T(8,128)S(1)}, f32[2688,128]{1,0:T(8,128)S(1)}, u32[]{:S(2)}, u32[]{:S(2)}) collective-permute-start(f32[2688,128]{1,0:T(8,128)S(1)} %bitcast.16), channel_id=1, source_target_pairs={{0,1},{1,0},{2,3},{3,2},{4,5},{5,4},{6,7},{7,6},{8,9},{9,8},{10,11... | collective-permute-start | bytes 4128776 | tf_op jit(solution)/shard_map/ppermute | solution.py:396
